TPU v7x, 128 devices: a whole 4x4x4 slice. The times are simulated.
128 devices in a mesh: attn: 4 (over x_lo, core), expert: 32 (over z, y, x_hi).
Axes of the slice: x: 4 (x_hi: 2, x_lo: 2; x = x_hi * 2 + x_lo), y: 4, z: 4, core: 2. Of those that a mesh axis runs over, the one named last changes fastest.
Arguments:
- tokens: bfloat16 [1024, 7168], P(('attn', 'expert')), may hold values from -6 to 6
- gates: float32 [1024, 8], P(('attn', 'expert')), may hold values from 0.1 to 1
- top_ids: int32 [1024, 8], P(('attn', 'expert')), may hold values from 0 to 31, all different within a row; in each aligned block of 8 rows (0 to 7, 8 to 15, ...) at most 3 rows name the same one
- home_expert: int32 [32], replicated, may hold values from 0 to 31, each once
- copy_source: int32 [32], replicated, may hold values from 0 to 31
- home_gate: bfloat16 [32, 7168, 1024], P('expert', None, 'attn'), may hold values from -0.0625 to 0.0625
- home_up: bfloat16 [32, 7168, 1024], P('expert', None, 'attn'), may hold values from -0.0625 to 0.0625
- home_down: bfloat16 [32, 7168, 1024], P('expert', None, 'attn'), may hold values from -0.1875 to 0.1875
Outputs:
- mixed: bfloat16 [1024, 7168], P(('attn', 'expert'))
- replica_gate: bfloat16 [32, 7168, 1024], P('expert', None, 'attn')
- replica_up: bfloat16 [32, 7168, 1024], P('expert', None, 'attn')
- replica_down: bfloat16 [32, 7168, 1024], P('expert', None, 'attn')
Inputs may be any that keep to these rules, and one draw needn't show every extreme that they name: `top_ids`: among the 8 rows of one device no expert is named by more than 3 rows, a bound that some block reaches.
All inputs are finite; a program needn't handle non-finite values.
Results may differ from a plain program's by a relative error of at most 0.015.
Values may be sent and summed in bfloat16 or wider, within the bound.
No kernel may reach another device: no remote copies, remote signals or barrier semaphores. Data moves between devices by JAX's collectives and lax.ppermute only.
A program may use at most 128 MiB of HBM per device.

v0:
```python
import jax
import jax.numpy as jnp
from jax import lax
from jax.sharding import PartitionSpec as P


def on_device(tokens, gates, top_ids, home_expert, copy_source, home_gate, home_up, home_down):
    expert_count = lax.axis_size("expert")
    tok_rows, model_width = tokens.shape
    fanout = top_ids.shape[1]
    capacity = min(tok_rows, (tok_rows * fanout + expert_count - 1) // expert_count + 1)
    spread = (
        lax.all_to_all(home_gate, "expert", split_axis=1, concat_axis=0, tiled=True),
        lax.all_to_all(home_up, "expert", split_axis=1, concat_axis=0, tiled=True),
        lax.all_to_all(home_down, "expert", split_axis=1, concat_axis=0, tiled=True),
    )
    picked = (spread[0][copy_source], spread[1][copy_source], spread[2][copy_source])
    replica_gate, replica_up, replica_down = (
        lax.all_to_all(picked[0], "expert", split_axis=0, concat_axis=1, tiled=True),
        lax.all_to_all(picked[1], "expert", split_axis=0, concat_axis=1, tiled=True),
        lax.all_to_all(picked[2], "expert", split_axis=0, concat_axis=1, tiled=True),
    )
    slot_expert = jnp.stack([home_expert, home_expert[copy_source]], axis=1).reshape(-1)
    slot_total = slot_expert.shape[0]
    slot_index = jnp.arange(slot_total, dtype=jnp.int32)
    named_slot = top_ids[:, :, None] == slot_expert[None, None, :]
    chosen = named_slot & (slot_index % 2 == 0)[None, None, :]
    chosen = chosen.reshape(tok_rows, fanout, expert_count, 2)[:, :, :, :1]
    per_device = chosen.shape[3]
    pair_count = tok_rows * fanout
    onehot = chosen.reshape(pair_count, expert_count * per_device).astype(jnp.int32)
    before = jnp.cumsum(onehot, axis=0) - onehot
    position = jnp.sum(onehot * before, axis=1)
    slot_number = jnp.sum(
        onehot * jnp.arange(expert_count * per_device, dtype=jnp.int32)[None, :], axis=1
    )
    target = slot_number * capacity + position
    place_count = expert_count * per_device * capacity
    landing = target[None, :] == jnp.arange(place_count, dtype=jnp.int32)[:, None]
    take_rows = jnp.any(landing.reshape(place_count, tok_rows, fanout), axis=2).astype(jnp.bfloat16)
    outbound = jnp.dot(take_rows, tokens, preferred_element_type=jnp.float32).astype(jnp.bfloat16)
    outbound = outbound.reshape(expert_count, per_device * capacity, model_width)
    arrived = lax.all_to_all(outbound, "expert", split_axis=0, concat_axis=0, tiled=True)
    weight_banks = [(home_gate, home_up, home_down), (replica_gate, replica_up, replica_down)][
        :per_device
    ]
    piece = lax.all_gather(arrived, "attn", axis=0, tiled=True)
    piece_rows = piece.shape[0]
    results = []
    for bank_index, (bank_gate, bank_up, bank_down) in enumerate(weight_banks):
        slot_rows = piece.reshape(-1, model_width)
        gate_act = jnp.dot(slot_rows, bank_gate[0], preferred_element_type=jnp.float32)
        up_act = jnp.dot(slot_rows, bank_up[0], preferred_element_type=jnp.float32)
        hidden = (jax.nn.silu(gate_act) * up_act).astype(jnp.bfloat16)
        partial_value = lax.dot_general(
            hidden, bank_down[0], (((1,), (1,)), ((), ())), preferred_element_type=jnp.float32
        )
        results.append(partial_value.reshape(piece_rows, capacity, model_width))
    partials = results[0]
    summed = lax.psum_scatter(
        partials.astype(jnp.bfloat16), "attn", scatter_dimension=0, tiled=True
    )
    answered = lax.all_to_all(summed, "expert", split_axis=0, concat_axis=0, tiled=True)
    select = jnp.transpose(landing).astype(jnp.bfloat16)
    pair_out = jnp.dot(
        select, answered.reshape(place_count, model_width), preferred_element_type=jnp.float32
    )
    pair_out = pair_out.reshape(tok_rows, fanout, model_width)
    mixed = jnp.sum(gates[:, :, None] * pair_out, axis=1).astype(jnp.bfloat16)
    return (mixed, replica_gate, replica_up, replica_down)


def solution(mesh):
    return jax.shard_map(
        on_device,
        mesh=mesh,
        in_specs=(
            P(("attn", "expert"), None),
            P(("attn", "expert"), None),
            P(("attn", "expert"), None),
            P(),
            P(),
            P("expert", None, "attn"),
            P("expert", None, "attn"),
            P("expert", None, "attn"),
        ),
        out_specs=(
            P(("attn", "expert"), None),
            P("expert", None, "attn"),
            P("expert", None, "attn"),
            P("expert", None, "attn"),
        ),
        check_vma=False,
    )
```

profile of v0, /device:TPU:2, one launch (start us, length us, event | category | flops | bytes accessed | tf_op | source)
XLA Modules:
  0.0 529.0 jit_solution(891379484010508446)
XLA Ops:
  7.2 0.0 copy-start
  7.2 0.7 compare_select_fusion
  7.9 1.4 gather_fusion
  9.3 0.7 pad_add_fusion
  9.9 0.8 convert_bitcast_fusion
  10.7 0.1 reduce_window_sum.13
  10.8 1.1 select_reduce_fusion
  11.9 0.1 fusion.17
  12.0 0.6 convolution_convert_fusion.1
  12.6 2.2 reshape.103
  14.7 9.9 %all-to-all-start = ((bf16[32,3,7168]{2,1,0:T(4,128)(2,1)}), bf16[32,3,7168]{2,1,0:T(4,128)(2,1)S(1)}, u32[]{:S(2)}, u32[]{:S(2)}) async-start(bf16[32,3,7168]{2,1,0:T(4,128)(2,1)} %reshape.103), calls=%async_computation | async-start | bytes 3670016 | tf_op jit(solution)/shard_map/all_to_all | solution.py:43
  24.6 7.8 %copy.46 = bf16[1,7168,256]{2,0,1:T(2,128)(2,1)} copy(bf16[1,7168,256]{2,1,0:T(8,128)(2,1)} %param.13) | data formatting | bytes 7340032 | tf_op args[5]
  32.4 0.5 broadcast.90
  32.9 38.4 %reduce.2 = bf16[7168,256]{1,0:T(8,128)(2,1)} reduce(bf16[7168,1,256]{2,1,0:T(2,128)(2,1)} %bitcast.48, bf16[]{:T(256)} %broadcast.90), dimensions={1}, to_apply=%bitcast.45.reduce_sub_computation | reduce | bytes 7340034
  71.3 8.4 %reshape.146 = bf16[32,2,28672]{2,1,0:T(2,128)(2,1)} reshape(bf16[7168,256]{1,0:T(8,128)(2,1)} %reduce.2) | data formatting | bytes 7340032
  79.7 9.9 %all-to-all-start.2 = ((bf16[32,2,28672]{2,1,0:T(2,128)(2,1)}), bf16[32,2,28672]{2,1,0:T(2,128)(2,1)}, u32[]{:S(2)}, u32[]{:S(2)}) async-start(bf16[32,2,28672]{2,1,0:T(2,128)(2,1)} %reshape.146), calls=%async_computation.3 | async-start | bytes 7340032 | tf_op jit(solution)/shard_map/all_to_all | solution.py:13
  89.6 0.5 all-gather.2.cloned.1.call-start
  90.1 1.6 copy.29
  91.7 0.0 all-gather.2.cloned.1.call-update
  91.7 7.8 %copy.45 = bf16[1,7168,256]{2,0,1:T(2,128)(2,1)} copy(bf16[1,7168,256]{2,1,0:T(8,128)(2,1)} %param.14) | data formatting | bytes 7340032 | tf_op args[6]
  99.5 38.4 %reduce.3 = bf16[7168,256]{1,0:T(8,128)(2,1)} reduce(bf16[7168,1,256]{2,1,0:T(2,128)(2,1)} %bitcast.53, bf16[]{:T(256)} %broadcast.90), dimensions={1}, to_apply=%bitcast.44.reduce_sub_computation | reduce | bytes 7340034
  137.9 8.4 %reshape.148 = bf16[32,2,28672]{2,1,0:T(2,128)(2,1)} reshape(bf16[7168,256]{1,0:T(8,128)(2,1)} %reduce.3) | data formatting | bytes 7340032
  146.3 15.1 %all-to-all-done.2 = bf16[32,2,28672]{2,1,0:T(2,128)(2,1)} async-done(((bf16[32,2,28672]{2,1,0:T(2,128)(2,1)}), bf16[32,2,28672]{2,1,0:T(2,128)(2,1)}, u32[]{:S(2)}, u32[]{:S(2)}) %all-to-all-start.2) | async-done | bytes 3670048 | tf_op jit(solution)/shard_map/all_to_all | solution.py:13
  161.4 4.8 all-to-all-start.4
  166.2 7.8 %copy.44 = bf16[1,7168,256]{2,0,1:T(2,128)(2,1)} copy(bf16[1,7168,256]{2,1,0:T(8,128)(2,1)} %param.15) | data formatting | bytes 7340032 | tf_op args[7]
  174.0 38.4 %reduce.4 = bf16[7168,256]{1,0:T(8,128)(2,1)} reduce(bf16[7168,1,256]{2,1,0:T(2,128)(2,1)} %bitcast.49, bf16[]{:T(256)} %broadcast.90), dimensions={1}, to_apply=%bitcast.43.reduce_sub_computation | reduce | bytes 7340034
  212.4 8.4 %reshape.150 = bf16[32,2,28672]{2,1,0:T(2,128)(2,1)} reshape(bf16[7168,256]{1,0:T(8,128)(2,1)} %reduce.4) | data formatting | bytes 7340032
  220.8 0.0 all-to-all-done.4
  220.8 9.8 %all-to-all-start.6 = ((bf16[32,2,28672]{2,1,0:T(2,128)(2,1)}), bf16[32,2,28672]{2,1,0:T(2,128)(2,1)}, u32[]{:S(2)}, u32[]{:S(2)}) async-start(bf16[32,2,28672]{2,1,0:T(2,128)(2,1)} %reshape.150), calls=%async_computation.7 | async-start | bytes 7340032 | tf_op jit(solution)/shard_map/all_to_all | solution.py:15
  230.6 0.2 reduce-scatter.2.cloned.1.call-start
  230.8 0.0 all-gather.2.cloned.1.call-done
  230.9 10.2 %copy.30 = bf16[128,3,7168]{2,1,0:T(4,128)(2,1)} copy(bf16[128,3,7168]{2,0,1:T(8,128)(2,1)} %all-gather.2.cloned.1.call-done) | data formatting | bytes 11010048 | tf_op jit(solution)/shard_map/all_gather | solution.py:47
  241.1 13.0 %reshape.104 = bf16[384,7168]{1,0:T(8,128)(2,1)} reshape(bf16[128,3,7168]{2,1,0:T(4,128)(2,1)} %copy.30) | data formatting | bytes 11010048 | tf_op jit(solution)/shard_map/reshape | solution.py:51
  254.1 5.4 %fusion.3 = f32[384,256]{1,0:T(8,128)S(1)} fusion(bf16[384,7168]{1,0:T(8,128)(2,1)} %reshape.104, bf16[1,7168,256]{2,1,0:T(8,128)(2,1)} %param.13), kind=kOutput, calls=%fused_computation.10 | convolution fusion | flops 1409286144 | bytes 9568256 | tf_op jit(solution)/shard_map/dot_general | solution.py:52
  259.5 0.9 copy-done.3
  260.5 1.6 fusion.9
  262.0 0.1 dot_general.20
  262.1 6.0 %convolution_convert_fusion = bf16[128,3,7168]{2,0,1:T(8,128)(2,1)} fusion(bf16[1,7168,256]{2,1,0:T(8,128)(2,1)} %param.15, bf16[128,3,256]{2,1,0:T(4,128)(2,1)S(1)} %dot_general.20), kind=kOutput, calls=%fused_computation.4 | convolution fusion | flops 1412038656 | bytes 9371648 | tf_op jit(solution)/shard_map/dot_general | solution.py:55
  268.2 0.0 reduce-scatter.2.cloned.1.call-update
  268.2 19.4 %reshape.147 = bf16[7168,1,256]{2,1,0:T(2,128)(2,1)} reshape(bf16[32,2,28672]{2,1,0:T(2,128)(2,1)} %all-to-all-done.2) | data formatting | bytes 7340032
  287.6 5.6 %copy.36 = bf16[1,7168,256]{2,1,0:T(8,128)(2,1)} copy(bf16[1,7168,256]{2,0,1:T(2,128)(2,1)} %bitcast.50) | data formatting | bytes 7340032
  293.2 4.7 gather_fusion.1
  297.9 0.0 all-to-all-done.6
  297.9 10.0 %all-to-all-start.3 = ((bf16[32,224,256]{2,1,0:T(8,128)(2,1)}), bf16[32,224,256]{2,1,0:T(8,128)(2,1)}, u32[]{:S(2)}, u32[]{:S(2)}) async-start(bf16[32,224,256]{2,1,0:T(8,128)(2,1)} %gather_fusion.1), calls=%async_computation.4 | async-start | bytes 7340032 | tf_op jit(solution)/shard_map/all_to_all | solution.py:19
  307.9 19.3 %reshape.149 = bf16[7168,1,256]{2,1,0:T(2,128)(2,1)} reshape(bf16[32,2,28672]{2,1,0:T(2,128)(2,1)} %all-to-all-done.4) | data formatting | bytes 7340032
  327.2 5.5 %copy.37 = bf16[1,7168,256]{2,1,0:T(8,128)(2,1)} copy(bf16[1,7168,256]{2,0,1:T(2,128)(2,1)} %bitcast.51) | data formatting | bytes 7340032
  332.8 4.7 gather_fusion.2
  337.4 32.9 %all-to-all-done.3 = bf16[32,224,256]{2,1,0:T(8,128)(2,1)} async-done(((bf16[32,224,256]{2,1,0:T(8,128)(2,1)}), bf16[32,224,256]{2,1,0:T(8,128)(2,1)}, u32[]{:S(2)}, u32[]{:S(2)}) %all-to-all-start.3) | async-done | bytes 3670048 | tf_op jit(solution)/shard_map/all_to_all | solution.py:19
  370.4 4.8 all-to-all-start.5
  375.2 19.3 %reshape.151 = bf16[7168,1,256]{2,1,0:T(2,128)(2,1)} reshape(bf16[32,2,28672]{2,1,0:T(2,128)(2,1)} %all-to-all-done.6) | data formatting | bytes 7340032
  394.5 5.5 %copy.38 = bf16[1,7168,256]{2,1,0:T(8,128)(2,1)} copy(bf16[1,7168,256]{2,0,1:T(2,128)(2,1)} %bitcast.52) | data formatting | bytes 7340032
  400.0 4.7 gather_fusion.3
  404.7 17.3 %all-to-all-done.5 = bf16[32,224,256]{2,1,0:T(8,128)(2,1)} async-done(((bf16[32,224,256]{2,1,0:T(8,128)(2,1)}), bf16[32,224,256]{2,1,0:T(8,128)(2,1)}, u32[]{:S(2)}, u32[]{:S(2)}) %all-to-all-start.5) | async-done | bytes 3670048 | tf_op jit(solution)/shard_map/all_to_all | solution.py:20
  422.0 6.2 %all-to-all-start.7 = ((bf16[32,224,256]{2,1,0:T(8,128)(2,1)}), bf16[32,224,256]{2,1,0:T(8,128)(2,1)}, u32[]{:S(2)}, u32[]{:S(2)}) async-start(bf16[32,224,256]{2,1,0:T(8,128)(2,1)} %gather_fusion.3), calls=%async_computation.8 | async-start | bytes 7340032 | tf_op jit(solution)/shard_map/all_to_all | solution.py:21
  428.2 0.0 reduce-scatter.2.cloned.1.call-done
  428.3 3.7 copy.32
  432.0 41.7 %all-to-all-done.7 = bf16[32,224,256]{2,1,0:T(8,128)(2,1)} async-done(((bf16[32,224,256]{2,1,0:T(8,128)(2,1)}), bf16[32,224,256]{2,1,0:T(8,128)(2,1)}, u32[]{:S(2)}, u32[]{:S(2)}) %all-to-all-start.7) | async-done | bytes 3670048 | tf_op jit(solution)/shard_map/all_to_all | solution.py:21
  473.8 6.7 %all-to-all-start.1 = ((bf16[32,3,7168]{2,1,0:T(4,128)(2,1)}), bf16[32,3,7168]{2,1,0:T(4,128)(2,1)S(1)}, u32[]{:S(2)}, u32[]{:S(2)}) async-start(bf16[32,3,7168]{2,1,0:T(4,128)(2,1)} %copy.32), calls=%async_computation.2 | async-start | bytes 3670016 | tf_op jit(solution)/shard_map/all_to_all | solution.py:63
  480.5 26.4 %all-to-all-done.1 = bf16[32,3,7168]{2,1,0:T(4,128)(2,1)S(1)} async-done(((bf16[32,3,7168]{2,1,0:T(4,128)(2,1)}), bf16[32,3,7168]{2,1,0:T(4,128)(2,1)S(1)}, u32[]{:S(2)}, u32[]{:S(2)}) %all-to-all-start.1) | async-done | bytes 1376288 | tf_op jit(solution)/shard_map/all_to_all | solution.py:63
  506.9 1.2 reshape.144
  508.1 1.5 fusion.5
  509.6 4.1 copy.50
  513.7 4.1 copy.51
  517.9 4.1 copy.52
  (13 shorter events, 0.0 us)
Async XLA Ops:
  7.2 4.8 copy-start
  14.7 64.9 %all-to-all-start = ((bf16[32,3,7168]{2,1,0:T(4,128)(2,1)}), bf16[32,3,7168]{2,1,0:T(4,128)(2,1)S(1)}, u32[]{:S(2)}, u32[]{:S(2)}) async-start(bf16[32,3,7168]{2,1,0:T(4,128)(2,1)} %reshape.103), calls=%async_computation | async-start | bytes 3670016 | tf_op jit(solution)/shard_map/all_to_all | solution.py:43
  79.7 81.7 %all-to-all-start.2 = ((bf16[32,2,28672]{2,1,0:T(2,128)(2,1)}), bf16[32,2,28672]{2,1,0:T(2,128)(2,1)}, u32[]{:S(2)}, u32[]{:S(2)}) async-start(bf16[32,2,28672]{2,1,0:T(2,128)(2,1)} %reshape.146), calls=%async_computation.3 | async-start | bytes 7340032 | tf_op jit(solution)/shard_map/all_to_all | solution.py:13
  89.6 141.3 %all-gather.2.cloned.1.call-start = ((), (), s32[]{:S(2)}) async-start(), calls=%async_computation.9 | async-start | bytes 6881280 | tf_op jit(solution)/shard_map/all_gather | solution.py:47
  161.4 59.4 %all-to-all-start.4 = ((bf16[32,2,28672]{2,1,0:T(2,128)(2,1)}), bf16[32,2,28672]{2,1,0:T(2,128)(2,1)}, u32[]{:S(2)}, u32[]{:S(2)}) async-start(bf16[32,2,28672]{2,1,0:T(2,128)(2,1)} %reshape.148), calls=%async_computation.5 | async-start | bytes 7340032 | tf_op jit(solution)/shard_map/all_to_all | solution.py:14
  220.8 77.1 %all-to-all-start.6 = ((bf16[32,2,28672]{2,1,0:T(2,128)(2,1)}), bf16[32,2,28672]{2,1,0:T(2,128)(2,1)}, u32[]{:S(2)}, u32[]{:S(2)}) async-start(bf16[32,2,28672]{2,1,0:T(2,128)(2,1)} %reshape.150), calls=%async_computation.7 | async-start | bytes 7340032 | tf_op jit(solution)/shard_map/all_to_all | solution.py:15
  230.6 197.6 %reduce-scatter.2.cloned.1.call-start = ((), (), s32[]{:S(2)}) async-start(), calls=%async_computation.10 | async-start | bytes 6881280 | tf_op jit(solution)/shard_map/reduce_scatter | solution.py:60
  254.1 5.4 %copy-start.2 = (bf16[384,7168]{1,0:T(8,128)(2,1)S(1)}, bf16[384,7168]{1,0:T(8,128)(2,1)}, u32[]{:S(2)}) copy-start(bf16[384,7168]{1,0:T(8,128)(2,1)} %reshape.104) | copy-start | bytes 16515076
  254.1 6.3 %copy-start.3 = (bf16[1,7168,256]{2,1,0:T(8,128)(2,1)S(1)}, bf16[1,7168,256]{2,1,0:T(8,128)(2,1)}, u32[]{:S(2)}) copy-start(bf16[1,7168,256]{2,1,0:T(8,128)(2,1)} %param.14) | copy-start | bytes 11010052
  297.9 72.5 %all-to-all-start.3 = ((bf16[32,224,256]{2,1,0:T(8,128)(2,1)}), bf16[32,224,256]{2,1,0:T(8,128)(2,1)}, u32[]{:S(2)}, u32[]{:S(2)}) async-start(bf16[32,224,256]{2,1,0:T(8,128)(2,1)} %gather_fusion.1), calls=%async_computation.4 | async-start | bytes 7340032 | tf_op jit(solution)/shard_map/all_to_all | solution.py:19
  370.4 51.6 %all-to-all-start.5 = ((bf16[32,224,256]{2,1,0:T(8,128)(2,1)}), bf16[32,224,256]{2,1,0:T(8,128)(2,1)}, u32[]{:S(2)}, u32[]{:S(2)}) async-start(bf16[32,224,256]{2,1,0:T(8,128)(2,1)} %gather_fusion.2), calls=%async_computation.6 | async-start | bytes 7340032 | tf_op jit(solution)/shard_map/all_to_all | solution.py:20
  422.0 51.7 %all-to-all-start.7 = ((bf16[32,224,256]{2,1,0:T(8,128)(2,1)}), bf16[32,224,256]{2,1,0:T(8,128)(2,1)}, u32[]{:S(2)}, u32[]{:S(2)}) async-start(bf16[32,224,256]{2,1,0:T(8,128)(2,1)} %gather_fusion.3), calls=%async_computation.8 | async-start | bytes 7340032 | tf_op jit(solution)/shard_map/all_to_all | solution.py:21
  432.0 76.1 %copy-start.4 = (f32[8,8]{1,0:T(8,128)S(1)}, f32[8,8]{1,0:T(8,128)}, u32[]{:S(2)}) copy-start(f32[8,8]{1,0:T(8,128)} %param.9) | copy-start | bytes 772
  473.8 33.2 %all-to-all-start.1 = ((bf16[32,3,7168]{2,1,0:T(4,128)(2,1)}), bf16[32,3,7168]{2,1,0:T(4,128)(2,1)S(1)}, u32[]{:S(2)}, u32[]{:S(2)}) async-start(bf16[32,3,7168]{2,1,0:T(4,128)(2,1)} %copy.32), calls=%async_computation.2 | async-start | bytes 3670016 | tf_op jit(solution)/shard_map/all_to_all | solution.py:63
  513.7 8.3 %copy-start.1 = (bf16[8,7168]{1,0:T(8,128)(2,1)S(1)}, bf16[8,7168]{1,0:T(8,128)(2,1)}, u32[]{:S(2)}) copy-start(bf16[8,7168]{1,0:T(8,128)(2,1)} %param.8) | copy-start | bytes 344068
Sparse Core Ops, SparseCore 0:
  92.1 93.6 all-gather.1
  268.3 76.5 reduce-scatter.1
where the time goes:
time: 538 us; the launch traced here: 529 us
  local copies, waits for them, and re-layouts  184 us (34%)
  waiting for transfers between devices  134 us (25%)
  other arithmetic  119 us (22%)
  starting transfers between devices  63 us (12%)
  matrix products  15 us (3%)
  between operations  14.4 us (3%)
    unnamed x26, local copies, waits for them, and re-layouts  137 us
    unnamed x3, other arithmetic  115 us
    all_to_all x1, waiting for transfers between devices, on_device(): lax.all_to_all(picked[2], 'expert', split_axis=0, concat_axis=1, tiled=True)  41.7 us
    all_to_all x1, waiting for transfers between devices, on_device(): lax.all_to_all(picked[0], 'expert', split_axis=0, concat_axis=1, tiled=True)  32.9 us
    all_to_all x1, waiting for transfers between devices, on_device(): lax.all_to_all(summed, 'expert', split_axis=0, concat_axis=0, tiled=True)  26.4 us
    all_to_all x1, waiting for transfers between devices, on_device(): lax.all_to_all(picked[1], 'expert', split_axis=0, concat_axis=1, tiled=True)  17.3 us
    all_to_all x1, waiting for transfers between devices, on_device(): lax.all_to_all(home_gate, 'expert', split_axis=1, concat_axis=0, tiled=True)  15.1 us
    reshape x1, local copies, waits for them, and re-layouts, on_device(): slot_rows = piece.reshape(-1, model_width)  13 us
  transfers between devices with their start and end apart: 10, of which 5 were waited for; matrix products, arithmetic and copies ran while one was open for 56% of the time, Pallas kernels for 0%

commit v1 on v0

v1 whole, which is shorter than its diff:
```python
import jax
import jax.numpy as jnp
from jax import lax
from jax.sharding import PartitionSpec as P

LANES = 128
CORE_SWAP = [(0, 1), (1, 0), (2, 3), (3, 2)]
CHIP_SWAP = [(0, 2), (1, 3), (2, 0), (3, 1)]


def swap_blocks(blocks):
    return lax.all_to_all(blocks, "expert", split_axis=0, concat_axis=0, tiled=True)


def on_device(tokens, gates, top_ids, home_expert, copy_source, home_gate, home_up, home_down):
    experts = lax.axis_size("expert")
    rows, width = tokens.shape
    fanout = top_ids.shape[1]
    pairs = rows * fanout
    capacity = min(rows, (pairs + experts - 1) // experts + 1)
    places = experts * capacity
    slabs = width // LANES
    depth, units = home_gate.shape[1:]
    share = depth // experts

    named = top_ids.reshape(pairs)[:, None] == home_expert[None, :]
    onehot = named.astype(jnp.int32)
    rank = jnp.sum(onehot * (jnp.cumsum(onehot, axis=0) - onehot), axis=1)
    slot = jnp.sum(onehot * jnp.arange(experts, dtype=jnp.int32)[None, :], axis=1)
    target = slot * capacity + rank
    landing = target[None, :] == jnp.arange(places, dtype=jnp.int32)[:, None]
    row_of = jnp.arange(pairs, dtype=jnp.int32) // fanout
    taken = jnp.sum(jnp.where(landing, row_of[None, :], 0), axis=1)

    weights = (home_gate, home_up, home_down)
    spread = [swap_blocks(w.reshape(experts, share, units)) for w in weights]
    replicas = [swap_blocks(s[copy_source]).reshape(1, depth, units) for s in spread]

    outbound = tokens.reshape(rows, slabs, LANES)[taken]
    arrived = swap_blocks(outbound.reshape(experts, capacity * slabs, LANES))
    arrived = arrived.reshape(places, slabs, LANES)
    both = jnp.concatenate([arrived, lax.ppermute(arrived, "attn", CHIP_SWAP)], axis=0)
    slot_rows = jnp.concatenate([both, lax.ppermute(both, "attn", CORE_SWAP)], axis=0)
    slot_rows = slot_rows.reshape(4 * places, width)

    gate_act = jnp.dot(slot_rows, home_gate[0], preferred_element_type=jnp.float32)
    up_act = jnp.dot(slot_rows, home_up[0], preferred_element_type=jnp.float32)
    hidden = (jax.nn.silu(gate_act) * up_act).astype(jnp.bfloat16)
    partial = lax.dot_general(
        hidden, home_down[0], (((1,), (1,)), ((), ())), preferred_element_type=jnp.float32
    ).astype(jnp.bfloat16)

    kept, sent = partial[: 2 * places], partial[2 * places :]
    pair_sum = kept.astype(jnp.float32) + lax.ppermute(sent, "attn", CORE_SWAP).astype(jnp.float32)
    far = lax.ppermute(pair_sum[places:].astype(jnp.bfloat16), "attn", CHIP_SWAP)
    expert_out = (pair_sum[:places] + far.astype(jnp.float32)).astype(jnp.bfloat16)

    answered = swap_blocks(expert_out.reshape(experts, capacity * slabs, LANES))
    answered = answered.reshape(places, width)
    mixing = jnp.sum(
        jnp.where(landing, gates.reshape(pairs)[None, :], 0.0).reshape(places, rows, fanout), axis=2
    )
    mixed = lax.dot_general(
        mixing,
        answered.astype(jnp.float32),
        (((0,), (0,)), ((), ())),
        precision=lax.Precision.HIGHEST,
        preferred_element_type=jnp.float32,
    ).astype(jnp.bfloat16)
    return (mixed, *replicas)


def solution(mesh):
    row_spec = P(("attn", "expert"), None)
    weight_spec = P("expert", None, "attn")
    return jax.shard_map(
        on_device,
        mesh=mesh,
        in_specs=(row_spec, row_spec, row_spec, P(), P(), weight_spec, weight_spec, weight_spec),
        out_specs=(row_spec, weight_spec, weight_spec, weight_spec),
        check_vma=False,
    )
```

time: 538 us -> 475 us (0.88); the launches traced: 529 us -> 472 us
  local copies, waits for them, and re-layouts: 184 us -> 44.5 us
  blocking collectives: 0 us -> 134 us
  other arithmetic: 119 us -> 6.49 us
  waiting for transfers between devices: 134 us -> 226 us
  starting transfers between devices: 63 us -> 46.5 us
  between operations: 14.4 us -> 0.85 us
    ppermute x0 -> x4, waiting for transfers between devices: none -> 136 us  [the longest x1 69.1 us: on_device(): lax.ppermute(arrived, 'attn', CHIP_SWAP)]
    all_to_all x0 -> x3, blocking collectives: none -> 134 us  [swap_blocks(): lax.all_to_all(blocks, 'expert', split_axis=0, concat_axis=0, tiled=True)]
    unnamed x26 -> x18, local copies, waits for them, and re-layouts: 137 us -> 19.5 us
    unnamed x3 -> x0, other arithmetic: 115 us -> none
    all_to_all x8 -> x5, waiting for transfers between devices: 134 us -> 90.9 us  [swap_blocks(): lax.all_to_all(blocks, 'expert', split_axis=0, concat_axis=0, tiled=True)]
    all_to_all x8 -> x5, starting transfers between devices: 62.3 us -> 44.9 us  [swap_blocks(): lax.all_to_all(blocks, 'expert', split_axis=0, concat_axis=0, tiled=True)]
    reshape x3 -> x2, local copies, waits for them, and re-layouts: 16.4 us -> 2.12 us  [the longest x1 1.51 us: on_device(): answered = swap_blocks(expert_out.reshape(experts, capacity * slabs, LANES))]
    all_gather x1 -> x0, local copies, waits for them, and re-layouts: 10.2 us -> none  [on_device(): piece = lax.all_gather(arrived, 'attn', axis=0, tiled=True)]
  transfers between devices with their start and end apart: 10 -> 9, of which waited for: 5 -> 5; matrix products, arithmetic and copies ran while one was open for 56% -> 9% of each run, Pallas kernels for 0% -> 0%
where the time goes in v1:
time: 475 us; the launch traced here: 472 us
  waiting for transfers between devices  226 us (48%)
  blocking collectives  134 us (28%)
  starting transfers between devices  46.5 us (10%)
  local copies, waits for them, and re-layouts  44.5 us (9%)
  matrix products  12.5 us (3%)
  other arithmetic  6.49 us (1%)
    all_to_all x3, blocking collectives, swap_blocks(): lax.all_to_all(blocks, 'expert', split_axis=0, concat_axis=0, tiled=True)  134 us
    all_to_all x5, waiting for transfers between devices, swap_blocks(): lax.all_to_all(blocks, 'expert', split_axis=0, concat_axis=0, tiled=True)  90.9 us
    ppermute x1, waiting for transfers between devices, on_device(): lax.ppermute(arrived, 'attn', CHIP_SWAP)  69.1 us
    ppermute x1, waiting for transfers between devices, on_device(): lax.ppermute(pair_sum[places:].astype(jnp.bfloat16), 'attn', CHIP_SWAP)  66.5 us
    all_to_all x5, starting transfers between devices, swap_blocks(): lax.all_to_all(blocks, 'expert', split_axis=0, concat_axis=0, tiled=True)  44.9 us
    unnamed x18, local copies, waits for them, and re-layouts  19.5 us
    gather x3, local copies, waits for them, and re-layouts, on_device(): s[copy_source]  14 us
  transfers between devices with their start and end apart: 9, of which 5 were waited for; matrix products, arithmetic and copies ran while one was open for 9% of the time, Pallas kernels for 0%

profile of v1, /device:TPU:2, one launch (start us, length us, event | category | flops | bytes accessed | tf_op | source)
XLA Modules:
  0.0 471.7 jit_solution(151968624764685950)
XLA Ops:
  0.6 0.8 eq.35
  1.4 0.7 compare_convert_fusion
  2.1 0.1 reduce_window_sum.11
  2.2 0.8 fusion.7
  3.1 0.9 copy.18
  4.0 0.1 select_reduce_fusion
  4.1 0.9 gather_fusion
  5.0 32.6 %all_to_all.40 = bf16[32,168,128]{2,1,0:T(8,128)(2,1)S(1)} all-to-all(bf16[32,168,128]{2,1,0:T(8,128)(2,1)S(1)} %bitcast.40), channel_id=1, replica_groups=mesh['attn'=4,'expert'=32] {'expert'}, dimensions={0} | all-to-all | bytes 2752512 | tf_op jit(solution)/shard_map/all_to_all | solution.py:12
  37.6 0.0 copy-start.2
  37.6 51.6 %all_to_all.41 = bf16[32,224,256]{2,1,0:T(8,128)(2,1)} all-to-all(bf16[32,224,256]{2,1,0:T(8,128)(2,1)} %bitcast.42), channel_id=1, replica_groups=mesh['attn'=4,'expert'=32] {'expert'}, dimensions={0} | all-to-all | bytes 7340032 | tf_op jit(solution)/shard_map/all_to_all | solution.py:12
  89.2 0.0 copy-done.2
  89.2 50.2 %all_to_all.42 = bf16[32,224,256]{2,1,0:T(8,128)(2,1)} all-to-all(bf16[32,224,256]{2,1,0:T(8,128)(2,1)S(1)} %bitcast.41), channel_id=1, replica_groups=mesh['attn'=4,'expert'=32] {'expert'}, dimensions={0} | all-to-all | bytes 7340032 | tf_op jit(solution)/shard_map/all_to_all | solution.py:12
  139.4 4.8 %all-to-all-start.6 = ((bf16[32,224,256]{2,1,0:T(8,128)(2,1)}), bf16[32,224,256]{2,1,0:T(8,128)(2,1)}, u32[]{:S(2)}, u32[]{:S(2)}) async-start(bf16[32,224,256]{2,1,0:T(8,128)(2,1)} %bitcast.36), calls=%async_computation.6 | async-start | bytes 7340032 | tf_op jit(solution)/shard_map/all_to_all | solution.py:12
  144.2 0.0 copy-start.5
  144.3 1.5 collective-permute-start
  145.7 69.1 %collective-permute-done = bf16[96,56,128]{2,1,0:T(8,128)(2,1)S(1)} collective-permute-done((bf16[96,56,128]{2,1,0:T(8,128)(2,1)S(1)}, bf16[96,56,128]{2,1,0:T(8,128)(2,1)S(1)}, u32[]{:S(2)}, u32[]{:S(2)}) %collective-permute-start) | collective-permute-done | bytes 1376288 | tf_op jit(solution)/shard_map/ppermute | solution.py:42
  214.9 1.8 pad_maximum_fusion
  216.7 0.0 collective-permute-start.1
  216.7 0.0 copy-done.5
  216.7 1.5 concatenate.14
  218.1 2.5 constant_dynamic-update-slice_fusion
  220.7 4.7 gather_fusion.1
  225.3 0.0 all-to-all-done.6
  225.3 8.1 %all-to-all-start.3 = ((bf16[32,224,256]{2,1,0:T(8,128)(2,1)}), bf16[32,224,256]{2,1,0:T(8,128)(2,1)}, u32[]{:S(2)}, u32[]{:S(2)}) async-start(bf16[32,224,256]{2,1,0:T(8,128)(2,1)} %gather_fusion.1), calls=%async_computation.3 | async-start | bytes 7340032 | tf_op jit(solution)/shard_map/all_to_all | solution.py:12
  233.4 1.3 bitcast_dynamic-update-slice_fusion.1
  234.7 4.7 gather_fusion.2
  239.3 0.0 copy-start.3
  239.3 0.0 collective-permute-done.1
  239.4 3.9 bitcast_dynamic-update-slice_fusion
  243.3 0.0 copy-done.3
  243.3 4.1 fusion.1
  247.4 37.2 %all-to-all-done.3 = bf16[32,224,256]{2,1,0:T(8,128)(2,1)} async-done(((bf16[32,224,256]{2,1,0:T(8,128)(2,1)}), bf16[32,224,256]{2,1,0:T(8,128)(2,1)}, u32[]{:S(2)}, u32[]{:S(2)}) %all-to-all-start.3) | async-done | bytes 3670048 | tf_op jit(solution)/shard_map/all_to_all | solution.py:12
  284.6 11.0 %all-to-all-start.5 = ((bf16[32,224,256]{2,1,0:T(8,128)(2,1)}), bf16[32,224,256]{2,1,0:T(8,128)(2,1)}, u32[]{:S(2)}, u32[]{:S(2)}) async-start(bf16[32,224,256]{2,1,0:T(8,128)(2,1)} %gather_fusion.2), calls=%async_computation.5 | async-start | bytes 7340032 | tf_op jit(solution)/shard_map/all_to_all | solution.py:12
  295.7 0.0 copy-start.1
  295.7 5.4 %fusion.3 = f32[384,256]{1,0:T(8,128)S(1)} fusion(bf16[384,7168]{1,0:T(8,128)(2,1)} %bitcast_dynamic-update-slice_fusion, bf16[1,7168,256]{2,1,0:T(8,128)(2,1)} %param.13), kind=kOutput, calls=%fused_computation.10 | convolution fusion | flops 1409286144 | bytes 9568256 | tf_op jit(solution)/shard_map/dot_general | solution.py:46
  301.1 0.0 copy-done.1
  301.1 1.7 convolution_convert_fusion
  302.7 0.0 copy-start
  302.8 2.4 copy-done
  305.2 1.7 slice.26
  306.9 0.0 collective-permute-start.2
  306.9 4.7 gather_fusion.3
  311.5 32.6 %all-to-all-done.5 = bf16[32,224,256]{2,1,0:T(8,128)(2,1)} async-done(((bf16[32,224,256]{2,1,0:T(8,128)(2,1)}), bf16[32,224,256]{2,1,0:T(8,128)(2,1)}, u32[]{:S(2)}, u32[]{:S(2)}) %all-to-all-start.5) | async-done | bytes 3670048 | tf_op jit(solution)/shard_map/all_to_all | solution.py:12
  344.1 10.2 %all-to-all-start.7 = ((bf16[32,224,256]{2,1,0:T(8,128)(2,1)}), bf16[32,224,256]{2,1,0:T(8,128)(2,1)}, u32[]{:S(2)}, u32[]{:S(2)}) async-start(bf16[32,224,256]{2,1,0:T(8,128)(2,1)} %gather_fusion.3), calls=%async_computation.7 | async-start | bytes 7340032 | tf_op jit(solution)/shard_map/all_to_all | solution.py:12
  354.3 0.0 collective-permute-done.2
  354.3 2.5 convert_add_fusion
  356.8 0.2 slice.34
  357.0 0.1 collective-permute-start.3
  357.1 66.5 %collective-permute-done.3 = bf16[96,7168]{1,0:T(8,128)(2,1)S(1)} collective-permute-done((bf16[96,7168]{1,0:T(8,128)(2,1)S(1)}, bf16[96,7168]{1,0:T(8,128)(2,1)S(1)}, u32[]{:S(2)}, u32[]{:S(2)}) %collective-permute-start.3) | collective-permute-done | bytes 1376288 | tf_op jit(solution)/shard_map/ppermute | solution.py:55
  423.6 0.3 fusion.5
  423.9 0.0 copy-start.4
  423.9 1.5 reshape.103
  425.4 0.0 all-to-all-done.7
  425.4 10.8 %all-to-all-start.1 = ((bf16[32,168,128]{2,1,0:T(8,128)(2,1)}), bf16[32,168,128]{2,1,0:T(8,128)(2,1)S(1)}, u32[]{:S(2)}, u32[]{:S(2)}) async-start(bf16[32,168,128]{2,1,0:T(8,128)(2,1)} %reshape.103), calls=%async_computation.1 | async-start | bytes 2752512 | tf_op jit(solution)/shard_map/all_to_all | solution.py:12
  436.2 0.1 add.45
  436.3 0.0 copy-done.4
  436.3 0.1 select_reduce_fusion.1
  436.4 21.0 %all-to-all-done.1 = bf16[32,168,128]{2,1,0:T(8,128)(2,1)S(1)} async-done(((bf16[32,168,128]{2,1,0:T(8,128)(2,1)}), bf16[32,168,128]{2,1,0:T(8,128)(2,1)S(1)}, u32[]{:S(2)}, u32[]{:S(2)}) %all-to-all-start.1) | async-done | bytes 1376288 | tf_op jit(solution)/shard_map/all_to_all | solution.py:12
  457.4 0.6 reshape.104
  458.0 1.3 convolution_convert_fusion.1
  459.3 4.1 copy.24
  463.5 4.1 copy.25
  467.6 4.1 copy.26
  (5 shorter events, 0.0 us)
Async XLA Ops:
  37.6 51.6 %copy-start.2 = (bf16[1,7168,256]{2,1,0:T(8,128)(2,1)S(1)}, bf16[1,7168,256]{2,1,0:T(8,128)(2,1)}, u32[]{:S(2)}) copy-start(bf16[1,7168,256]{2,1,0:T(8,128)(2,1)} %param.14) | copy-start | bytes 11010052
  139.4 85.9 %all-to-all-start.6 = ((bf16[32,224,256]{2,1,0:T(8,128)(2,1)}), bf16[32,224,256]{2,1,0:T(8,128)(2,1)}, u32[]{:S(2)}, u32[]{:S(2)}) async-start(bf16[32,224,256]{2,1,0:T(8,128)(2,1)} %bitcast.36), calls=%async_computation.6 | async-start | bytes 7340032 | tf_op jit(solution)/shard_map/all_to_all | solution.py:12
  144.2 72.4 %copy-start.5 = (s32[32]{0:T(128)S(1)}, s32[32]{0:T(128)}, u32[]{:S(2)}) copy-start(s32[32]{0:T(128)} %param.12) | copy-start | bytes 388
  144.3 70.6 %collective-permute-start = (bf16[96,56,128]{2,1,0:T(8,128)(2,1)S(1)}, bf16[96,56,128]{2,1,0:T(8,128)(2,1)S(1)}, u32[]{:S(2)}, u32[]{:S(2)}) collective-permute-start(bf16[96,56,128]{2,1,0:T(8,128)(2,1)S(1)} %bitcast.37), channel_id=1, source_target_pairs={{0,64},{32,96},{64,0},{96,32},{1,65},{33,97},{65,1},{97,33},{2,66}... | collective-permute-start | bytes 4128776 | tf_op jit(solution)/shard_map/ppermute | solution.py:42
  216.7 22.7 %collective-permute-start.1 = (bf16[192,56,128]{2,1,0:T(8,128)(2,1)}, bf16[192,56,128]{2,1,0:T(8,128)(2,1)}, u32[]{:S(2)}, u32[]{:S(2)}) collective-permute-start(bf16[192,56,128]{2,1,0:T(8,128)(2,1)} %pad_maximum_fusion), channel_id=1, source_target_pairs={{0,32},{32,0},{64,96},{96,64},{1,33},{33,1},{65,97},{97,65},{2,34}... | collective-permute-start | bytes 8257544 | tf_op jit(solution)/shard_map/ppermute | solution.py:43
  225.3 59.3 %all-to-all-start.3 = ((bf16[32,224,256]{2,1,0:T(8,128)(2,1)}), bf16[32,224,256]{2,1,0:T(8,128)(2,1)}, u32[]{:S(2)}, u32[]{:S(2)}) async-start(bf16[32,224,256]{2,1,0:T(8,128)(2,1)} %gather_fusion.1), calls=%async_computation.3 | async-start | bytes 7340032 | tf_op jit(solution)/shard_map/all_to_all | solution.py:12
  239.3 3.9 copy-start.3
  284.6 59.5 %all-to-all-start.5 = ((bf16[32,224,256]{2,1,0:T(8,128)(2,1)}), bf16[32,224,256]{2,1,0:T(8,128)(2,1)}, u32[]{:S(2)}, u32[]{:S(2)}) async-start(bf16[32,224,256]{2,1,0:T(8,128)(2,1)} %gather_fusion.2), calls=%async_computation.5 | async-start | bytes 7340032 | tf_op jit(solution)/shard_map/all_to_all | solution.py:12
  295.7 5.4 %copy-start.1 = (bf16[1,7168,256]{2,1,0:T(8,128)(2,1)S(1)}, bf16[1,7168,256]{2,1,0:T(8,128)(2,1)}, u32[]{:S(2)}) copy-start(bf16[1,7168,256]{2,1,0:T(8,128)(2,1)} %param.15) | copy-start | bytes 11010052
  302.7 2.4 copy-start
  306.9 47.4 %collective-permute-start.2 = (bf16[192,7168]{1,0:T(8,128)(2,1)}, bf16[192,7168]{1,0:T(8,128)(2,1)S(1)}, u32[]{:S(2)}, u32[]{:S(2)}) collective-permute-start(bf16[192,7168]{1,0:T(8,128)(2,1)} %slice.26), channel_id=1, source_target_pairs={{0,32},{32,0},{64,96},{96,64},{1,33},{33,1},{65,97},{97,65},{2,34}... | collective-permute-start | bytes 8257544 | tf_op jit(solution)/shard_map/ppermute | solution.py:54
  344.1 81.3 %all-to-all-start.7 = ((bf16[32,224,256]{2,1,0:T(8,128)(2,1)}), bf16[32,224,256]{2,1,0:T(8,128)(2,1)}, u32[]{:S(2)}, u32[]{:S(2)}) async-start(bf16[32,224,256]{2,1,0:T(8,128)(2,1)} %gather_fusion.3), calls=%async_computation.7 | async-start | bytes 7340032 | tf_op jit(solution)/shard_map/all_to_all | solution.py:12
  357.0 66.6 %collective-permute-start.3 = (bf16[96,7168]{1,0:T(8,128)(2,1)S(1)}, bf16[96,7168]{1,0:T(8,128)(2,1)S(1)}, u32[]{:S(2)}, u32[]{:S(2)}) collective-permute-start(bf16[96,7168]{1,0:T(8,128)(2,1)S(1)} %slice.34), channel_id=1, source_target_pairs={{0,64},{32,96},{64,0},{96,32},{1,65},{33,97},{65,1},{97,33},{2,66}... | collective-permute-start | bytes 4128776 | tf_op jit(solution)/shard_map/ppermute | solution.py:55
  423.9 12.4 %copy-start.4 = (f32[8,8]{1,0:T(8,128)S(1)}, f32[8,8]{1,0:T(8,128)}, u32[]{:S(2)}) copy-start(f32[8,8]{1,0:T(8,128)} %param.9) | copy-start | bytes 772
  425.4 32.0 %all-to-all-start.1 = ((bf16[32,168,128]{2,1,0:T(8,128)(2,1)}), bf16[32,168,128]{2,1,0:T(8,128)(2,1)S(1)}, u32[]{:S(2)}, u32[]{:S(2)}) async-start(bf16[32,168,128]{2,1,0:T(8,128)(2,1)} %reshape.103), calls=%async_computation.1 | async-start | bytes 2752512 | tf_op jit(solution)/shard_map/all_to_all | solution.py:12

commit v2 on v1

v2 whole, which is shorter than its diff:
```python
import functools

import jax
import jax.numpy as jnp
from jax import lax
from jax.experimental import pallas as pl
from jax.experimental.pallas import tpu as pltpu
from jax.sharding import PartitionSpec as P

RING = 4
NOTE = 128
EXPERT_AXIS = RING * RING * 2
WORK = 1 << 36
BOTH = ("attn", "expert")


def table(step):
    pairs = []
    for x_lo in range(2):
        for core in range(2):
            for z in range(RING):
                for y in range(RING):
                    for x_hi in range(2):
                        to = step(x_lo, core, z, y, x_hi)
                        ends = []
                        for a, c, k, j, i in ((x_lo, core, z, y, x_hi), to):
                            slot = ((k % RING) * RING + j % RING) * 2 + i % 2
                            ends.append(((a % 2) * 2 + c % 2) * EXPERT_AXIS + slot)
                        pairs.append(tuple(ends))
    return pairs


def row_step(n):
    return table(lambda a, c, z, y, x: (a + n % 2, c, z, y, x + n // 2))


def wide_step(n):
    return table(lambda a, c, z, y, x: (a, c, z + n * c, y + n * (1 - c), x))


def deep_step(n):
    return table(lambda a, c, z, y, x: (a, c, z + n * (1 - c), y + n * c, x))


CORE_SWAP = table(lambda a, c, z, y, x: (a, c + 1, z, y, x))


def send(value, pairs):
    return lax.ppermute(value, BOTH, pairs)


def swap_blocks(blocks):
    return lax.all_to_all(blocks, "expert", split_axis=0, concat_axis=0, tiled=True)


def bf16_pieces(values):
    pieces, rest = [], values
    for _ in range(3):
        piece = lax.reduce_precision(rest, exponent_bits=8, mantissa_bits=7)
        pieces.append(piece.astype(jnp.bfloat16))
        rest = rest - piece
    return pieces


def select_kernel(fanout, capacity, chunk, column_ref, *refs):
    blocks, (chosen_ref, mixing_ref) = refs[:RING], refs[RING:]
    width = chosen_ref.shape[1]
    f32 = jnp.float32
    note = jnp.concatenate([b[:, width:].astype(f32) for b in blocks], axis=0)
    plane = note.shape[0]
    ids = note[:, :fanout]
    gate = (
        note[:, fanout : 2 * fanout]
        + note[:, 2 * fanout : 3 * fanout]
        + note[:, 3 * fanout : 4 * fanout]
    )
    places = RING * capacity
    lane = lax.broadcasted_iota(jnp.int32, (plane, places), 1)
    row = lax.broadcasted_iota(jnp.int32, (plane, plane), 0)
    earlier = (lax.broadcasted_iota(jnp.int32, (plane, plane), 1) < row).astype(f32)
    taken = jnp.zeros((plane, places), f32)
    mixing = jnp.zeros((plane, places), f32)
    for j in range(RING):
        named = ids == column_ref[j].astype(f32)
        hit = jnp.max(jnp.where(named, 1.0, 0.0), axis=1, keepdims=True)
        weight = jnp.sum(jnp.where(named, gate, 0.0), axis=1, keepdims=True)
        rank = jnp.dot(
            earlier, jnp.broadcast_to(hit, (plane, NOTE)), preferred_element_type=f32
        )[:, :1]
        mark = (lane == rank.astype(jnp.int32) + j * capacity) & (lane >= j * capacity)
        mark = mark & (lane < (j + 1) * capacity) & (hit > 0.5)
        taken = jnp.where(mark, 1.0, taken)
        mixing = jnp.where(mark, weight, mixing)
    mixing_ref[...] = mixing
    taken = taken.astype(jnp.bfloat16)
    for low in range(0, width, chunk):
        held = jnp.concatenate([b[:, low : low + chunk] for b in blocks], axis=0)
        chosen_ref[:, low : low + chunk] = lax.dot_general(
            taken, held, (((0,), (0,)), ((), ())), preferred_element_type=f32
        ).astype(jnp.bfloat16)


def whole(kernel, out_shape, work, *operands, scalars=()):
    return pl.pallas_call(
        kernel,
        out_shape=out_shape,
        in_specs=[pl.BlockSpec(memory_space=pltpu.SMEM)] * len(scalars)
        + [pl.BlockSpec(memory_space=pltpu.VMEM)] * len(operands),
        out_specs=jax.tree.map(lambda _: pl.BlockSpec(memory_space=pltpu.VMEM), out_shape),
        compiler_params=pltpu.CompilerParams(vmem_limit_bytes=40 << 20),
        cost_estimate=pl.CostEstimate(flops=work, bytes_accessed=1 << 20, transcendentals=0),
    )(*scalars, *operands)


def stack_kernel(*refs):
    low = 0
    for ref in refs[:-1]:
        refs[-1][low : low + ref.shape[0]] = ref[...]
        low += ref.shape[0]


def gated_kernel(chunk, mixing_ref, *refs):
    blocks, (own_ref, *part_refs) = refs[:RING], refs[RING:]
    pieces, rest = [], mixing_ref[...]
    for _ in range(3):
        piece = rest.astype(jnp.bfloat16)
        pieces.append(piece)
        rest = rest - piece.astype(jnp.float32)
    line = own_ref.shape[0]
    for low in range(0, own_ref.shape[1], chunk):
        span = slice(low, low + chunk)
        back = jnp.concatenate([b[:, span] for b in blocks], axis=0)
        total = jnp.dot(pieces[0], back, preferred_element_type=jnp.float32)
        for piece in pieces[1:]:
            total = total + jnp.dot(piece, back, preferred_element_type=jnp.float32)
        own_ref[:, span] = total[:line]
        for n, part_ref in enumerate(part_refs):
            low_row = (n + 1) * line
            part_ref[:, span] = total[low_row : low_row + line].astype(jnp.bfloat16)


def sum_kernel(own_ref, *refs):
    total = own_ref[...]
    for ref in refs[: RING - 1]:
        total = total + ref[...].astype(jnp.float32)
    low = 0
    for ref in refs[RING - 1 :]:
        ref[...] = total[low : low + ref.shape[0]].astype(ref.dtype)
        low += ref.shape[0]


def expert_kernel(chunk, rows_ref, gate_ref, up_ref, down_ref, out_ref):
    f32 = jnp.float32
    gate_act = jnp.dot(rows_ref[...], gate_ref[0], preferred_element_type=f32)
    up_act = jnp.dot(rows_ref[...], up_ref[0], preferred_element_type=f32)
    hidden = (gate_act / (1.0 + jnp.exp(-gate_act)) * up_act).astype(jnp.bfloat16)
    for low in range(0, out_ref.shape[1], chunk):
        out_ref[:, low : low + chunk] = lax.dot_general(
            hidden,
            down_ref[0, low : low + chunk],
            (((1,), (1,)), ((), ())),
            preferred_element_type=f32,
        ).astype(out_ref.dtype)


def add_kernel(one_ref, two_ref, out_ref):
    out_ref[...] = (one_ref[...] + two_ref[...].astype(jnp.float32)).astype(out_ref.dtype)


def copy_kernel(from_ref, to_ref, held, came, went):
    share = held.shape[1]
    spans = [pl.ds(n * share, share) for n in range(held.shape[0])]
    inward = [
        pltpu.make_async_copy(from_ref.at[0, span], held.at[n], came.at[n])
        for n, span in enumerate(spans)
    ]
    outward = [
        pltpu.make_async_copy(held.at[n], to_ref.at[0, span], went.at[n])
        for n, span in enumerate(spans)
    ]
    for copy in inward:
        copy.start()
    for first, second in zip(inward, outward):
        first.wait()
        second.start()
    for copy in outward:
        copy.wait()


def copied(value):
    parts, (_, depth, units) = 8, value.shape
    return pl.pallas_call(
        copy_kernel,
        out_shape=jax.ShapeDtypeStruct(value.shape, value.dtype),
        in_specs=[pl.BlockSpec(memory_space=pl.ANY)],
        out_specs=pl.BlockSpec(memory_space=pl.ANY),
        scratch_shapes=[
            pltpu.VMEM((parts, depth // parts, units), value.dtype),
            pltpu.SemaphoreType.DMA((parts,)),
            pltpu.SemaphoreType.DMA((parts,)),
        ],
        compiler_params=pltpu.CompilerParams(vmem_limit_bytes=16 << 20),
        cost_estimate=pl.CostEstimate(flops=0, bytes_accessed=8 << 20, transcendentals=0),
    )(value)


def on_device(tokens, gates, top_ids, home_expert, copy_source, home_gate, home_up, home_down):
    experts = lax.axis_size("expert")
    rows, width = tokens.shape
    fanout = top_ids.shape[1]
    most = (rows * fanout + experts - 1) // experts + 1
    capacity = 4 * RING * most
    depth, units = home_gate.shape[1:]
    blocked = (experts, depth // experts, units)
    here = lax.axis_index("expert")
    core = lax.axis_index("attn") % 2
    z, y, x_hi = here // (2 * RING), here // 2 % RING, here % 2
    bf16, f32 = jnp.bfloat16, jnp.float32
    ahead = jnp.arange(RING, dtype=jnp.int32)
    column = ((z + ahead * (1 - core)) % RING * RING + (y + ahead * core) % RING) * 2 + x_hi
    column_expert = home_expert[column]
    tie = lax.optimization_barrier

    note = jnp.concatenate([top_ids.astype(bf16)] + bf16_pieces(gates), axis=1)
    note = jnp.pad(note, ((0, 0), (0, NOTE - note.shape[1])))
    held, gate_blocks = tie((jnp.concatenate([tokens, note], axis=1), home_gate.reshape(blocked)))
    near = [send(held, row_step(n)) for n in range(1, 4)]
    gate_spread = swap_blocks(gate_blocks)
    line = 4 * rows
    held = whole(
        stack_kernel, jax.ShapeDtypeStruct((line, width + NOTE), bf16), WORK, held, *near
    )

    held, up_blocks, gate_spread = tie((held, home_up.reshape(blocked), gate_spread))
    blocks = [held] + [send(held, wide_step(n)) for n in range(1, RING)]
    up_spread = swap_blocks(up_blocks)
    blocks, gate_spread = tie((blocks, gate_spread))
    blocks, gate_picks = tie((blocks, gate_spread[copy_source]))
    places = RING * capacity
    chosen, mixing = whole(
        functools.partial(select_kernel, fanout, capacity, width // 8),
        (
            jax.ShapeDtypeStruct((places, width), bf16),
            jax.ShapeDtypeStruct((RING * line, places), f32),
        ),
        WORK,
        *blocks,
        scalars=(column_expert,),
    )

    chosen, down_blocks, up_spread = tie((chosen, home_down.reshape(blocked), up_spread))
    chosen = chosen.reshape(RING, capacity, width)
    mine = [chosen[0]] + [send(chosen[n], deep_step(n)) for n in range(1, RING)]
    down_spread = swap_blocks(down_blocks)
    mine = whole(stack_kernel, jax.ShapeDtypeStruct((places, width), bf16), WORK, *mine)

    mine, gate_picks, down_spread = tie((mine, gate_picks, down_spread))
    other = send(mine, CORE_SWAP)
    replica_gate = swap_blocks(gate_picks)
    other, up_spread, down_spread = tie((other, up_spread, down_spread))
    other, up_picks, down_picks = tie((other, up_spread[copy_source], down_spread[copy_source]))

    def expert_part(slot_rows, dtype):
        return whole(
            functools.partial(expert_kernel, width // 8),
            jax.ShapeDtypeStruct((places, width), dtype),
            WORK,
            slot_rows,
            home_gate,
            home_up,
            home_down,
        )

    given = send(expert_part(other, bf16), CORE_SWAP)
    summed = whole(
        add_kernel,
        jax.ShapeDtypeStruct((places, width), bf16),
        1 << 20,
        expert_part(mine, f32),
        given,
    )

    summed, up_picks, replica_gate = tie((summed, up_picks, replica_gate))
    summed = summed.reshape(RING, capacity, width)
    back = [summed[0]] + [send(summed[n], deep_step(-n)) for n in range(1, RING)]
    replica_up = swap_blocks(up_picks)
    own, *parts = whole(
        functools.partial(gated_kernel, width // 8),
        (jax.ShapeDtypeStruct((line, width), f32),)
        + (jax.ShapeDtypeStruct((line, width), bf16),) * (RING - 1),
        WORK,
        mixing,
        *back,
    )

    parts, down_picks, replica_up = tie((parts, down_picks, replica_up))
    parts = [send(parts[n - 1], wide_step(-n)) for n in range(1, RING)]
    replica_down = swap_blocks(down_picks)
    replica_gate = copied(replica_gate.reshape(1, depth, units))
    replica_up = copied(replica_up.reshape(1, depth, units))
    parts, replica_gate, replica_up = tie((parts, replica_gate, replica_up))
    own, *parts = whole(
        sum_kernel,
        (jax.ShapeDtypeStruct((rows, width), f32),)
        + (jax.ShapeDtypeStruct((rows, width), bf16),) * 3,
        WORK,
        own,
        *parts,
    )

    parts, replica_down = tie((parts, replica_down))
    parts = [send(parts[n - 1], row_step(n)) for n in range(1, 4)]
    replica_down = copied(replica_down.reshape(1, depth, units))
    mixed = whole(sum_kernel, (jax.ShapeDtypeStruct((rows, width), bf16),), 1 << 20, own, *parts)[0]
    return (mixed, replica_gate, replica_up, replica_down)


def solution(mesh):
    row_spec = P(("attn", "expert"), None)
    weight_spec = P("expert", None, "attn")
    return jax.shard_map(
        on_device,
        mesh=mesh,
        in_specs=(row_spec, row_spec, row_spec, P(), P(), weight_spec, weight_spec, weight_spec),
        out_specs=(row_spec, weight_spec, weight_spec, weight_spec),
        check_vma=False,
    )
```

time: 475 us -> 401 us (0.84)
  blocking collectives: 134 us -> 0 us
  starting transfers between devices: 46.5 us -> 76.5 us
  waiting for transfers between devices: 226 us -> 254 us
  Pallas kernels: 0 us -> 25.4 us
  matrix products: 12.5 us -> 0 us
  local copies, waits for them, and re-layouts: 44.5 us -> 38.4 us
    all_to_all x3 -> x0, blocking collectives: 134 us -> none  [swap_blocks(): lax.all_to_all(blocks, 'expert', split_axis=0, concat_axis=0, tiled=True)]
    all_to_all x5 -> x6, waiting for transfers between devices: 90.9 us -> 131 us  [swap_blocks(): lax.all_to_all(blocks, 'expert', split_axis=0, concat_axis=0, tiled=True)]
    pallas_call x0 -> x12, Pallas kernels: none -> 25.4 us  [the longest x9 16.2 us: whole(): pl.pallas_call(kernel, out_shape=out_shape, in_specs=[pl.BlockSpec(memory...]
    ppermute x4 -> x20, starting transfers between devices: 1.57 us -> 23.6 us  [send(): return lax.ppermute(value, BOTH, pairs)]
    ppermute x4 -> x20, waiting for transfers between devices: 136 us -> 123 us  [send(): return lax.ppermute(value, BOTH, pairs)]
    dot_general x4 -> x0, matrix products: 12.5 us -> none  [the longest x1 5.39 us: on_device(): jnp.dot(slot_rows, home_gate[0], preferred_element_type=jnp.float32)]
    all_to_all x5 -> x6, starting transfers between devices: 44.9 us -> 52.9 us  [swap_blocks(): lax.all_to_all(blocks, 'expert', split_axis=0, concat_axis=0, tiled=True)]
    concatenate x2 -> x0, local copies, waits for them, and re-layouts: 5.39 us -> none  [on_device(): jnp.concatenate([both, lax.ppermute(both, 'attn', CORE_SWAP)], axis=0)]
  transfers between devices with their start and end apart: 9 -> 26, of which waited for: 5 -> 11; matrix products, arithmetic and copies ran while one was open for 9% -> 4% of each run, Pallas kernels for 0% -> 6%
where the time goes in v2:
time: 401 us; the launch traced here: 398 us
  waiting for transfers between devices  254 us (63%)
  starting transfers between devices  76.5 us (19%)
  local copies, waits for them, and re-layouts  38.4 us (10%)
  Pallas kernels  25.4 us (6%)
    all_to_all x6, waiting for transfers between devices, swap_blocks(): lax.all_to_all(blocks, 'expert', split_axis=0, concat_axis=0, tiled=True)  131 us
    ppermute x20, waiting for transfers between devices, send(): return lax.ppermute(value, BOTH, pairs)  123 us
    all_to_all x6, starting transfers between devices, swap_blocks(): lax.all_to_all(blocks, 'expert', split_axis=0, concat_axis=0, tiled=True)  52.9 us
    ppermute x20, starting transfers between devices, send(): return lax.ppermute(value, BOTH, pairs)  23.6 us
    unnamed x52, local copies, waits for them, and re-layouts  21.1 us
    pallas_call x9, Pallas kernels, whole(): pl.pallas_call(kernel, out_shape=out_shape, in_specs=[pl.BlockSpec(memory...  16.2 us
    pallas_call x3, Pallas kernels, copied(): pl.pallas_call(copy_kernel, out_shape=jax.ShapeDtypeStruct(value.shape, v...  9.19 us
  transfers between devices with their start and end apart: 26, of which 11 were waited for; matrix products, arithmetic and copies ran while one was open for 4% of the time, Pallas kernels for 6%

profile of v2, /device:TPU:2, one launch (start us, length us, event | category | flops | bytes accessed | tf_op | source)
XLA Modules:
  0.0 397.5 jit_solution(11518470026398493126)
XLA Ops:
  0.6 0.7 reduce-precision_convert_fusion.1
  1.3 0.7 convert_element_type.14
  2.1 0.9 pad_maximum_fusion.refs_0_
  3.6 2.5 collective-permute-start.1
  6.1 0.5 collective-permute-start.2
  6.6 11.2 %all-to-all-start = ((bf16[32,224,256]{2,1,0:T(8,128)(2,1)}), bf16[32,224,256]{2,1,0:T(8,128)(2,1)}, u32[]{:S(2)}, u32[]{:S(2)}) async-start(bf16[32,224,256]{2,1,0:T(8,128)(2,1)} %bitcast.8), calls=%async_computation | async-start | bytes 7340032 | tf_op jit(solution)/shard_map/all_to_all | solution.py:53
  18.0 47.1 %all-to-all-done = bf16[32,224,256]{2,1,0:T(8,128)(2,1)} async-done(((bf16[32,224,256]{2,1,0:T(8,128)(2,1)}), bf16[32,224,256]{2,1,0:T(8,128)(2,1)}, u32[]{:S(2)}, u32[]{:S(2)}) %all-to-all-start) | async-done | bytes 3670048 | tf_op jit(solution)/shard_map/all_to_all | solution.py:53
  65.0 2.4 collective-permute-start.3
  67.4 2.7 collective-permute-start.5
  70.1 0.6 gather_fusion
  70.8 5.5 %all-to-all-start.1 = ((bf16[32,224,256]{2,1,0:T(8,128)(2,1)}), bf16[32,224,256]{2,1,0:T(8,128)(2,1)}, u32[]{:S(2)}, u32[]{:S(2)}) async-start(bf16[32,224,256]{2,1,0:T(8,128)(2,1)} %bitcast.9), calls=%async_computation.1 | async-start | bytes 7340032 | tf_op jit(solution)/shard_map/all_to_all | solution.py:53
  76.3 31.3 %collective-permute-done.3.refs_1_ = bf16[32,7296]{1,0:T(8,128)(2,1)S(1)} collective-permute-done((bf16[32,7296]{1,0:T(8,128)(2,1)S(1)}, bf16[32,7296]{1,0:T(8,128)(2,1)S(1)}, u32[]{:S(2)}, u32[]{:S(2)}) %collective-permute-start.3) | collective-permute-done | bytes 466976 | tf_op jit(solution)/shard_map/ppermute | solution.py:49
  107.6 0.8 copy-done.13
  108.4 0.8 copy-done.15
  109.1 0.8 copy-done.17
  109.9 4.7 %gather_fusion.1 = bf16[32,224,256]{2,1,0:T(8,128)(2,1)} fusion(bf16[32,224,256]{2,1,0:T(8,128)(2,1)} %all-to-all-done, s32[1024]{0:T(1024)S(1)} %pad_clamp_fusion), kind=kCustom, calls=%fused_computation.1 | custom fusion | bytes 7340160 | tf_op jit(solution)/shard_map/gather | solution.py:238
  114.6 1.0 copy-done.14
  115.6 1.0 copy-done.16
  116.6 1.0 copy-done.18
  117.7 1.9 shard_map.112
  119.6 0.6 copy-done.23
  120.2 4.8 %all-to-all-done.1 = bf16[32,224,256]{2,1,0:T(8,128)(2,1)} async-done(((bf16[32,224,256]{2,1,0:T(8,128)(2,1)}), bf16[32,224,256]{2,1,0:T(8,128)(2,1)}, u32[]{:S(2)}, u32[]{:S(2)}) %all-to-all-start.1) | async-done | bytes 3670048 | tf_op jit(solution)/shard_map/all_to_all | solution.py:53
  125.0 1.4 fusion.15
  126.3 3.0 collective-permute-start.7
  129.7 5.5 %all-to-all-start.2 = ((bf16[32,224,256]{2,1,0:T(8,128)(2,1)}), bf16[32,224,256]{2,1,0:T(8,128)(2,1)}, u32[]{:S(2)}, u32[]{:S(2)}) async-start(bf16[32,224,256]{2,1,0:T(8,128)(2,1)} %bitcast.10), calls=%async_computation.2 | async-start | bytes 7340032 | tf_op jit(solution)/shard_map/all_to_all | solution.py:53
  135.2 5.9 %collective-permute-done.6.refs_1_ = bf16[48,7168]{1,0:T(8,128)(2,1)S(1)} collective-permute-done((bf16[48,7168]{1,0:T(8,128)(2,1)}, bf16[48,7168]{1,0:T(8,128)(2,1)S(1)}, u32[]{:S(2)}, u32[]{:S(2)}) %collective-permute-start.6) | collective-permute-done | bytes 688160 | tf_op jit(solution)/shard_map/ppermute | solution.py:49
  141.1 0.9 copy-done.7
  142.0 42.8 %collective-permute-done.7.refs_2_ = bf16[48,7168]{1,0:T(8,128)(2,1)S(1)} collective-permute-done((bf16[48,7168]{1,0:T(8,128)(2,1)}, bf16[48,7168]{1,0:T(8,128)(2,1)S(1)}, u32[]{:S(2)}, u32[]{:S(2)}) %collective-permute-start.7) | collective-permute-done | bytes 688160 | tf_op jit(solution)/shard_map/ppermute | solution.py:49
  184.8 0.8 copy-done.9
  185.7 0.8 copy-done.11
  186.5 1.1 copy-done.8
  187.6 1.1 copy-done.10
  188.7 1.1 copy-done.12
  190.1 6.0 %all-to-all-start.3 = ((bf16[32,224,256]{2,1,0:T(8,128)(2,1)}), bf16[32,224,256]{2,1,0:T(8,128)(2,1)}, u32[]{:S(2)}, u32[]{:S(2)}) async-start(bf16[32,224,256]{2,1,0:T(8,128)(2,1)} %gather_fusion.1), calls=%async_computation.3 | async-start | bytes 7340032 | tf_op jit(solution)/shard_map/all_to_all | solution.py:53
  196.1 4.6 %gather_fusion.3 = bf16[32,224,256]{2,1,0:T(8,128)(2,1)} fusion(bf16[32,224,256]{2,1,0:T(8,128)(2,1)} %all-to-all-done.2, s32[1024]{0:T(1024)S(1)} %pad_clamp_fusion), kind=kCustom, calls=%fused_computation.3 | custom fusion | bytes 7340160 | tf_op jit(solution)/shard_map/gather | solution.py:261
  200.8 4.7 %gather_fusion.2 = bf16[32,224,256]{2,1,0:T(8,128)(2,1)} fusion(bf16[32,224,256]{2,1,0:T(8,128)(2,1)} %all-to-all-done.1, s32[1024]{0:T(1024)S(1)} %pad_clamp_fusion), kind=kCustom, calls=%fused_computation.2 | custom fusion | bytes 7340160 | tf_op jit(solution)/shard_map/gather | solution.py:261
  205.4 2.0 copy-done.3
  207.4 2.0 copy-done.5
  209.5 5.8 %shard_map.115 = bf16[192,7168]{1,0:T(8,128)(2,1)S(1)} custom-call(bf16[192,7168]{1,0:T(8,128)(2,1)} %collective-permute-done.9.rows_ref, bf16[1,7168,256]{2,1,0:T(8,128)(2,1)S(1)} %copy-done.3, bf16[1,7168,256]{2,1,0:T(8,128)(2,1)S(1)} %copy-done.5, bf16[1,7168,256]{2,1,0:T(8,128)(2,1)} %down_ref.3), custom_call_target="tpu_custom_call" | custom-call | flops 68719476736 | bytes 1048576 | tf_op jit(solution)/shard_map/pallas_call | solution.py:104
  215.8 5.2 %shard_map.114.one_ref = f32[192,7168]{1,0:T(8,128)} custom-call(bf16[192,7168]{1,0:T(8,128)(2,1)S(1)} %shard_map.113.rows_ref, bf16[1,7168,256]{2,1,0:T(8,128)(2,1)S(1)} %copy-done.4, bf16[1,7168,256]{2,1,0:T(8,128)(2,1)S(1)} %copy-done.5, bf16[1,7168,256]{2,1,0:T(8,128)(2,1)S(1)} %copy-done.6), custom_call_target="tpu_custom_call" | custom-call | flops 68719476736 | bytes 1048576 | tf_op jit(solution)/shard_map/pallas_call | solution.py:104
  221.0 2.6 copy-done.2
  224.0 23.3 %all-to-all-done.3 = bf16[32,224,256]{2,1,0:T(8,128)(2,1)} async-done(((bf16[32,224,256]{2,1,0:T(8,128)(2,1)}), bf16[32,224,256]{2,1,0:T(8,128)(2,1)}, u32[]{:S(2)}, u32[]{:S(2)}) %all-to-all-start.3) | async-done | bytes 3670048 | tf_op jit(solution)/shard_map/all_to_all | solution.py:53
  247.3 1.3 fusion.14
  248.6 1.6 collective-permute-start.11
  250.3 1.0 collective-permute-start.12
  251.3 12.7 %all-to-all-start.4 = ((bf16[32,224,256]{2,1,0:T(8,128)(2,1)}), bf16[32,224,256]{2,1,0:T(8,128)(2,1)}, u32[]{:S(2)}, u32[]{:S(2)}) async-start(bf16[32,224,256]{2,1,0:T(8,128)(2,1)} %gather_fusion.2), calls=%async_computation.4 | async-start | bytes 7340032 | tf_op jit(solution)/shard_map/all_to_all | solution.py:53
  264.0 39.4 %collective-permute-done.13.refs_3_ = bf16[48,7168]{1,0:T(8,128)(2,1)S(1)} collective-permute-done((bf16[48,7168]{1,0:T(8,128)(2,1)}, bf16[48,7168]{1,0:T(8,128)(2,1)S(1)}, u32[]{:S(2)}, u32[]{:S(2)}) %collective-permute-start.13) | collective-permute-done | bytes 688160 | tf_op jit(solution)/shard_map/ppermute | solution.py:49
  303.5 1.8 shard_map.117
  305.3 0.8 copy-done.19
  306.0 0.8 copy-done.20
  306.8 0.9 copy-done.21
  307.8 3.6 all-to-all-done.4
  311.3 0.9 collective-permute-start.14
  312.3 3.1 collective-permute-start.15
  315.4 3.1 shard_map.118
  318.4 3.1 shard_map.119
  321.5 11.9 %all-to-all-start.5 = ((bf16[32,224,256]{2,1,0:T(8,128)(2,1)}), bf16[32,224,256]{2,1,0:T(8,128)(2,1)}, u32[]{:S(2)}, u32[]{:S(2)}) async-start(bf16[32,224,256]{2,1,0:T(8,128)(2,1)} %gather_fusion.3), calls=%async_computation.5 | async-start | bytes 7340032 | tf_op jit(solution)/shard_map/all_to_all | solution.py:53
  333.6 52.4 %all-to-all-done.5 = bf16[32,224,256]{2,1,0:T(8,128)(2,1)} async-done(((bf16[32,224,256]{2,1,0:T(8,128)(2,1)}), bf16[32,224,256]{2,1,0:T(8,128)(2,1)}, u32[]{:S(2)}, u32[]{:S(2)}) %all-to-all-start.5) | async-done | bytes 3670048 | tf_op jit(solution)/shard_map/all_to_all | solution.py:53
  386.0 3.9 collective-permute-start.18
  389.9 0.6 collective-permute-start.19
  390.4 3.1 shard_map.122
  393.5 1.9 collective-permute-done.18.refs_1_
  395.4 1.4 collective-permute-done.19.refs_2_
  396.8 0.7 shard_map.121
  (66 shorter events, 2.6 us)
Async XLA Ops:
  0.6 69.5 %copy-start = (s32[32]{0:T(128)S(1)}, s32[32]{0:T(128)}, u32[]{:S(2)}) copy-start(s32[32]{0:T(128)} %param.11) | copy-start | bytes 388
  3.0 14.9 %collective-permute-start = (bf16[8,7296]{1,0:T(8,128)(2,1)S(1)}, bf16[8,7296]{1,0:T(8,128)(2,1)S(1)}, u32[]{:S(2)}, u32[]{:S(2)}) collective-permute-start(bf16[8,7296]{1,0:T(8,128)(2,1)S(1)} %pad_maximum_fusion.refs_0_), channel_id=1, source_target_pairs={{0,64},{1,65},{2,66},{3,67},{4,68},{5,69},{6,70},{7,71},{8,72},{9,... | collective-permute-start | bytes 350216 | tf_op jit(solution)/shard_map/ppermute | solution.py:49
  3.6 14.3 %collective-permute-start.1 = (bf16[8,7296]{1,0:T(8,128)(2,1)S(1)}, bf16[8,7296]{1,0:T(8,128)(2,1)S(1)}, u32[]{:S(2)}, u32[]{:S(2)}) collective-permute-start(bf16[8,7296]{1,0:T(8,128)(2,1)S(1)} %pad_maximum_fusion.refs_0_), channel_id=1, source_target_pairs={{0,1},{1,0},{2,3},{3,2},{4,5},{5,4},{6,7},{7,6},{8,9},{9,8},{10,11... | collective-permute-start | bytes 350216 | tf_op jit(solution)/shard_map/ppermute | solution.py:49
  6.1 11.9 %collective-permute-start.2 = (bf16[8,7296]{1,0:T(8,128)(2,1)S(1)}, bf16[8,7296]{1,0:T(8,128)(2,1)S(1)}, u32[]{:S(2)}, u32[]{:S(2)}) collective-permute-start(bf16[8,7296]{1,0:T(8,128)(2,1)S(1)} %pad_maximum_fusion.refs_0_), channel_id=1, source_target_pairs={{0,65},{1,64},{2,67},{3,66},{4,69},{5,68},{6,71},{7,70},{8,73},{9,... | collective-permute-start | bytes 350216 | tf_op jit(solution)/shard_map/ppermute | solution.py:49
  6.6 58.4 %all-to-all-start = ((bf16[32,224,256]{2,1,0:T(8,128)(2,1)}), bf16[32,224,256]{2,1,0:T(8,128)(2,1)}, u32[]{:S(2)}, u32[]{:S(2)}) async-start(bf16[32,224,256]{2,1,0:T(8,128)(2,1)} %bitcast.8), calls=%async_computation | async-start | bytes 7340032 | tf_op jit(solution)/shard_map/all_to_all | solution.py:53
  17.9 52.9 %copy-start.25 = (s32[32]{0:T(128)S(1)}, s32[32]{0:T(128)}, u32[]{:S(2)}) copy-start(s32[32]{0:T(128)} %param.12) | copy-start | bytes 388
  65.0 42.6 %collective-permute-start.3 = (bf16[32,7296]{1,0:T(8,128)(2,1)S(1)}, bf16[32,7296]{1,0:T(8,128)(2,1)S(1)}, u32[]{:S(2)}, u32[]{:S(2)}) collective-permute-start(bf16[32,7296]{1,0:T(8,128)(2,1)S(1)} %shard_map.111.refs_0_), channel_id=1, source_target_pairs={{0,2},{1,3},{2,4},{3,5},{4,6},{5,7},{6,0},{7,1},{8,10},{9,11},{10,... | collective-permute-start | bytes 1400840 | tf_op jit(solution)/shard_map/ppermute | solution.py:49
  67.4 41.0 %collective-permute-start.4 = (bf16[32,7296]{1,0:T(8,128)(2,1)S(1)}, bf16[32,7296]{1,0:T(8,128)(2,1)S(1)}, u32[]{:S(2)}, u32[]{:S(2)}) collective-permute-start(bf16[32,7296]{1,0:T(8,128)(2,1)S(1)} %shard_map.111.refs_0_), channel_id=1, source_target_pairs={{0,4},{1,5},{2,6},{3,7},{4,0},{5,1},{6,2},{7,3},{8,12},{9,13},{10,... | collective-permute-start | bytes 1400840 | tf_op jit(solution)/shard_map/ppermute | solution.py:49
  67.4 41.7 %collective-permute-start.5 = (bf16[32,7296]{1,0:T(8,128)(2,1)S(1)}, bf16[32,7296]{1,0:T(8,128)(2,1)S(1)}, u32[]{:S(2)}, u32[]{:S(2)}) collective-permute-start(bf16[32,7296]{1,0:T(8,128)(2,1)S(1)} %shard_map.111.refs_0_), channel_id=1, source_target_pairs={{0,6},{1,7},{2,0},{3,1},{4,2},{5,3},{6,4},{7,5},{8,14},{9,15},{10,... | collective-permute-start | bytes 1400840 | tf_op jit(solution)/shard_map/ppermute | solution.py:49
  70.8 54.2 %all-to-all-start.1 = ((bf16[32,224,256]{2,1,0:T(8,128)(2,1)}), bf16[32,224,256]{2,1,0:T(8,128)(2,1)}, u32[]{:S(2)}, u32[]{:S(2)}) async-start(bf16[32,224,256]{2,1,0:T(8,128)(2,1)} %bitcast.9), calls=%async_computation.1 | async-start | bytes 7340032 | tf_op jit(solution)/shard_map/all_to_all | solution.py:53
  107.6 0.8 copy-start.13
  108.4 0.8 copy-start.15
  109.1 0.8 copy-start.17
  114.6 1.0 copy-start.14
  115.6 1.0 copy-start.16
  116.6 1.0 copy-start.18
  119.6 0.7 copy-start.23
  126.3 14.8 %collective-permute-start.6 = (bf16[48,7168]{1,0:T(8,128)(2,1)}, bf16[48,7168]{1,0:T(8,128)(2,1)S(1)}, u32[]{:S(2)}, u32[]{:S(2)}) collective-permute-start(bf16[48,7168]{1,0:T(8,128)(2,1)} %get-tuple-element.118), channel_id=1, source_target_pairs={{0,8},{1,9},{2,10},{3,11},{4,12},{5,13},{6,14},{7,15},{8,16},{9,17... | collective-permute-start | bytes 2064392 | tf_op jit(solution)/shard_map/ppermute | solution.py:49
  126.3 58.4 %collective-permute-start.7 = (bf16[48,7168]{1,0:T(8,128)(2,1)}, bf16[48,7168]{1,0:T(8,128)(2,1)S(1)}, u32[]{:S(2)}, u32[]{:S(2)}) collective-permute-start(bf16[48,7168]{1,0:T(8,128)(2,1)} %get-tuple-element.117), channel_id=1, source_target_pairs={{0,16},{1,17},{2,18},{3,19},{4,20},{5,21},{6,22},{7,23},{8,24},{9,... | collective-permute-start | bytes 2064392 | tf_op jit(solution)/shard_map/ppermute | solution.py:49
  129.3 56.3 %collective-permute-start.8 = (bf16[48,7168]{1,0:T(8,128)(2,1)}, bf16[48,7168]{1,0:T(8,128)(2,1)S(1)}, u32[]{:S(2)}, u32[]{:S(2)}) collective-permute-start(bf16[48,7168]{1,0:T(8,128)(2,1)} %get-tuple-element.116), channel_id=1, source_target_pairs={{0,24},{1,25},{2,26},{3,27},{4,28},{5,29},{6,30},{7,31},{8,0},{9,1... | collective-permute-start | bytes 2064392 | tf_op jit(solution)/shard_map/ppermute | solution.py:49
  129.7 60.3 %all-to-all-start.2 = ((bf16[32,224,256]{2,1,0:T(8,128)(2,1)}), bf16[32,224,256]{2,1,0:T(8,128)(2,1)}, u32[]{:S(2)}, u32[]{:S(2)}) async-start(bf16[32,224,256]{2,1,0:T(8,128)(2,1)} %bitcast.10), calls=%async_computation.2 | async-start | bytes 7340032 | tf_op jit(solution)/shard_map/all_to_all | solution.py:53
  141.1 0.9 copy-start.7
  184.8 0.8 copy-start.9
  185.6 0.8 copy-start.11
  186.5 1.1 copy-start.8
  187.6 1.1 copy-start.10
  188.7 1.1 copy-start.12
  190.0 6.1 %collective-permute-start.9 = (bf16[192,7168]{1,0:T(8,128)(2,1)S(1)}, bf16[192,7168]{1,0:T(8,128)(2,1)}, u32[]{:S(2)}, u32[]{:S(2)}) collective-permute-start(bf16[192,7168]{1,0:T(8,128)(2,1)S(1)} %shard_map.113.rows_ref), channel_id=1, source_target_pairs={{0,32},{1,33},{2,34},{3,35},{4,36},{5,37},{6,38},{7,39},{8,40},{9,... | collective-permute-start | bytes 8257544 | tf_op jit(solution)/shard_map/ppermute | solution.py:49
  190.1 57.2 %all-to-all-start.3 = ((bf16[32,224,256]{2,1,0:T(8,128)(2,1)}), bf16[32,224,256]{2,1,0:T(8,128)(2,1)}, u32[]{:S(2)}, u32[]{:S(2)}) async-start(bf16[32,224,256]{2,1,0:T(8,128)(2,1)} %gather_fusion.1), calls=%async_computation.3 | async-start | bytes 7340032 | tf_op jit(solution)/shard_map/all_to_all | solution.py:53
  205.4 2.0 copy-start.3
  207.4 2.0 copy-start.5
  209.5 6.3 %copy-start.4 = (bf16[1,7168,256]{2,1,0:T(8,128)(2,1)S(1)}, bf16[1,7168,256]{2,1,0:T(8,128)(2,1)}, u32[]{:S(2)}) copy-start(bf16[1,7168,256]{2,1,0:T(8,128)(2,1)} %gate_ref.3) | copy-start | bytes 11010052
  209.5 6.3 %copy-start.6 = (bf16[1,7168,256]{2,1,0:T(8,128)(2,1)S(1)}, bf16[1,7168,256]{2,1,0:T(8,128)(2,1)}, u32[]{:S(2)}) copy-start(bf16[1,7168,256]{2,1,0:T(8,128)(2,1)} %down_ref.3) | copy-start | bytes 11010052
  215.3 5.6 %collective-permute-start.10 = (bf16[192,7168]{1,0:T(8,128)(2,1)S(1)}, bf16[192,7168]{1,0:T(8,128)(2,1)S(1)}, u32[]{:S(2)}, u32[]{:S(2)}) collective-permute-start(bf16[192,7168]{1,0:T(8,128)(2,1)S(1)} %shard_map.115), channel_id=1, source_target_pairs={{0,32},{1,33},{2,34},{3,35},{4,36},{5,37},{6,38},{7,39},{8,40},{9,... | collective-permute-start | bytes 8257544 | tf_op jit(solution)/shard_map/ppermute | solution.py:49
  221.0 2.6 copy-start.2
  248.6 15.4 %collective-permute-start.11 = (bf16[48,7168]{1,0:T(8,128)(2,1)}, bf16[48,7168]{1,0:T(8,128)(2,1)S(1)}, u32[]{:S(2)}, u32[]{:S(2)}) collective-permute-start(bf16[48,7168]{1,0:T(8,128)(2,1)} %get-tuple-element.114), channel_id=1, source_target_pairs={{0,24},{1,25},{2,26},{3,27},{4,28},{5,29},{6,30},{7,31},{8,0},{9,1... | collective-permute-start | bytes 2064392 | tf_op jit(solution)/shard_map/ppermute | solution.py:49
  250.3 13.8 %collective-permute-start.12 = (bf16[48,7168]{1,0:T(8,128)(2,1)}, bf16[48,7168]{1,0:T(8,128)(2,1)S(1)}, u32[]{:S(2)}, u32[]{:S(2)}) collective-permute-start(bf16[48,7168]{1,0:T(8,128)(2,1)} %get-tuple-element.113), channel_id=1, source_target_pairs={{0,16},{1,17},{2,18},{3,19},{4,20},{5,21},{6,22},{7,23},{8,24},{9,... | collective-permute-start | bytes 2064392 | tf_op jit(solution)/shard_map/ppermute | solution.py:49
  251.3 52.2 %copy-start.24 = (f32[128,192]{1,0:T(8,128)S(1)}, f32[128,192]{1,0:T(8,128)}, u32[]{:S(2)}) copy-start(f32[128,192]{1,0:T(8,128)} %copy-done.23) | copy-start | bytes 294916
  251.3 52.2 %collective-permute-start.13 = (bf16[48,7168]{1,0:T(8,128)(2,1)}, bf16[48,7168]{1,0:T(8,128)(2,1)S(1)}, u32[]{:S(2)}, u32[]{:S(2)}) collective-permute-start(bf16[48,7168]{1,0:T(8,128)(2,1)} %get-tuple-element.112), channel_id=1, source_target_pairs={{0,8},{1,9},{2,10},{3,11},{4,12},{5,13},{6,14},{7,15},{8,16},{9,17... | collective-permute-start | bytes 2064392 | tf_op jit(solution)/shard_map/ppermute | solution.py:49
  251.3 60.1 %all-to-all-start.4 = ((bf16[32,224,256]{2,1,0:T(8,128)(2,1)}), bf16[32,224,256]{2,1,0:T(8,128)(2,1)}, u32[]{:S(2)}, u32[]{:S(2)}) async-start(bf16[32,224,256]{2,1,0:T(8,128)(2,1)} %gather_fusion.2), calls=%async_computation.4 | async-start | bytes 7340032 | tf_op jit(solution)/shard_map/all_to_all | solution.py:53
  305.3 0.8 copy-start.19
  306.0 0.8 copy-start.20
  306.8 0.9 copy-start.21
  311.3 22.0 %collective-permute-start.14 = (bf16[32,7168]{1,0:T(8,128)(2,1)}, bf16[32,7168]{1,0:T(8,128)(2,1)S(1)}, u32[]{:S(2)}, u32[]{:S(2)}) collective-permute-start(bf16[32,7168]{1,0:T(8,128)(2,1)} %copy-done.20), channel_id=1, source_target_pairs={{0,6},{1,7},{2,0},{3,1},{4,2},{5,3},{6,4},{7,5},{8,14},{9,15},{10,... | collective-permute-start | bytes 1376264 | tf_op jit(solution)/shard_map/ppermute | solution.py:49
  312.3 21.1 %collective-permute-start.15 = (bf16[32,7168]{1,0:T(8,128)(2,1)}, bf16[32,7168]{1,0:T(8,128)(2,1)S(1)}, u32[]{:S(2)}, u32[]{:S(2)}) collective-permute-start(bf16[32,7168]{1,0:T(8,128)(2,1)} %copy-done.19), channel_id=1, source_target_pairs={{0,4},{1,5},{2,6},{3,7},{4,0},{5,1},{6,2},{7,3},{8,12},{9,13},{10,... | collective-permute-start | bytes 1376264 | tf_op jit(solution)/shard_map/ppermute | solution.py:49
  315.4 18.1 %collective-permute-start.16 = (bf16[32,7168]{1,0:T(8,128)(2,1)S(1)}, bf16[32,7168]{1,0:T(8,128)(2,1)S(1)}, u32[]{:S(2)}, u32[]{:S(2)}) collective-permute-start(bf16[32,7168]{1,0:T(8,128)(2,1)S(1)} %get-tuple-element.95), channel_id=1, source_target_pairs={{0,2},{1,3},{2,4},{3,5},{4,6},{5,7},{6,0},{7,1},{8,10},{9,11},{10,... | collective-permute-start | bytes 1376264 | tf_op jit(solution)/shard_map/ppermute | solution.py:49
  321.5 11.9 %copy-start.22 = (f32[32,7168]{1,0:T(8,128)S(1)}, f32[32,7168]{1,0:T(8,128)}, u32[]{:S(2)}) copy-start(f32[32,7168]{1,0:T(8,128)} %copy-done.21) | copy-start | bytes 2752516
  321.5 64.5 %all-to-all-start.5 = ((bf16[32,224,256]{2,1,0:T(8,128)(2,1)}), bf16[32,224,256]{2,1,0:T(8,128)(2,1)}, u32[]{:S(2)}, u32[]{:S(2)}) async-start(bf16[32,224,256]{2,1,0:T(8,128)(2,1)} %gather_fusion.3), calls=%async_computation.5 | async-start | bytes 7340032 | tf_op jit(solution)/shard_map/all_to_all | solution.py:53
  386.0 7.5 %collective-permute-start.17 = (bf16[8,7168]{1,0:T(8,128)(2,1)S(1)}, bf16[8,7168]{1,0:T(8,128)(2,1)S(1)}, u32[]{:S(2)}, u32[]{:S(2)}) collective-permute-start(bf16[8,7168]{1,0:T(8,128)(2,1)S(1)} %get-tuple-element.106), channel_id=1, source_target_pairs={{0,64},{1,65},{2,66},{3,67},{4,68},{5,69},{6,70},{7,71},{8,72},{9,... | collective-permute-start | bytes 344072 | tf_op jit(solution)/shard_map/ppermute | solution.py:49
  386.0 9.4 %collective-permute-start.18 = (bf16[8,7168]{1,0:T(8,128)(2,1)S(1)}, bf16[8,7168]{1,0:T(8,128)(2,1)S(1)}, u32[]{:S(2)}, u32[]{:S(2)}) collective-permute-start(bf16[8,7168]{1,0:T(8,128)(2,1)S(1)} %get-tuple-element.107), channel_id=1, source_target_pairs={{0,1},{1,0},{2,3},{3,2},{4,5},{5,4},{6,7},{7,6},{8,9},{9,8},{10,11... | collective-permute-start | bytes 344072 | tf_op jit(solution)/shard_map/ppermute | solution.py:49
  389.9 6.9 %collective-permute-start.19 = (bf16[8,7168]{1,0:T(8,128)(2,1)S(1)}, bf16[8,7168]{1,0:T(8,128)(2,1)S(1)}, u32[]{:S(2)}, u32[]{:S(2)}) collective-permute-start(bf16[8,7168]{1,0:T(8,128)(2,1)S(1)} %get-tuple-element.108), channel_id=1, source_target_pairs={{0,65},{1,64},{2,67},{3,66},{4,69},{5,68},{6,71},{7,70},{8,73},{9,... | collective-permute-start | bytes 344072 | tf_op jit(solution)/shard_map/ppermute | solution.py:49
  390.4 7.1 %copy-start.1 = (s32[32]{0:T(128)S(1)}, s32[32]{0:T(128)}, u32[]{:S(2)}) copy-start(s32[32]{0:T(128)} %param.11) | copy-start | bytes 388

commit v3 on v2

--- a/solution.py
+++ b/solution.py
@@ -167,6 +167,32 @@
     out_ref[...] = (one_ref[...] + two_ref[...].astype(jnp.float32)).astype(out_ref.dtype)
 
 
+def pick_kernel(source_ref, *refs):
+    refs[-1][...] = refs[0][...]
+
+
+def picked(copy_source, spread):
+    count, height, units = spread.shape
+    return pl.pallas_call(
+        pick_kernel,
+        out_shape=jax.ShapeDtypeStruct(spread.shape, spread.dtype),
+        grid_spec=pltpu.PrefetchScalarGridSpec(
+            num_scalar_prefetch=1,
+            grid=(count,),
+            in_specs=[pl.BlockSpec((1, height, units), lambda i, s: (s[i], 0, 0))],
+            out_specs=pl.BlockSpec((1, height, units), lambda i, s: (i, 0, 0)),
+        ),
+        cost_estimate=pl.CostEstimate(flops=0, bytes_accessed=1 << 20, transcendentals=0),
+    )(copy_source, spread)
+
+
+def swap_cores(value, parts=4):
+    rows = value.shape[0] // parts
+    return jnp.concatenate(
+        [send(value[n * rows : (n + 1) * rows], CORE_SWAP) for n in range(parts)], axis=0
+    )
+
+
 def copy_kernel(from_ref, to_ref, held, came, went):
     share = held.shape[1]
     spans = [pl.ds(n * share, share) for n in range(held.shape[0])]
@@ -231,11 +257,11 @@
         stack_kernel, jax.ShapeDtypeStruct((line, width + NOTE), bf16), WORK, held, *near
     )
 
-    held, up_blocks, gate_spread = tie((held, home_up.reshape(blocked), gate_spread))
     blocks = [held] + [send(held, wide_step(n)) for n in range(1, RING)]
-    up_spread = swap_blocks(up_blocks)
-    blocks, gate_spread = tie((blocks, gate_spread))
-    blocks, gate_picks = tie((blocks, gate_spread[copy_source]))
+    both = jnp.concatenate([home_up.reshape(blocked), home_down.reshape(blocked)], axis=1)
+    both, gate_spread = tie((both, gate_spread))
+    both_spread = swap_blocks(both)
+    gate_picks = gate_spread[copy_source]
     places = RING * capacity
     chosen, mixing = whole(
         functools.partial(select_kernel, fanout, capacity, width // 8),
@@ -243,35 +269,31 @@
             jax.ShapeDtypeStruct((places, width), bf16),
             jax.ShapeDtypeStruct((RING * line, places), f32),
         ),
-        WORK,
+        WORK >> 3,
         *blocks,
         scalars=(column_expert,),
     )
 
-    chosen, down_blocks, up_spread = tie((chosen, home_down.reshape(blocked), up_spread))
     chosen = chosen.reshape(RING, capacity, width)
     mine = [chosen[0]] + [send(chosen[n], deep_step(n)) for n in range(1, RING)]
-    down_spread = swap_blocks(down_blocks)
+    gate_picks, both_spread = tie((gate_picks, both_spread))
+    replica_gate = swap_blocks(gate_picks)
+    both_picks = picked(copy_source, both_spread)
     mine = whole(stack_kernel, jax.ShapeDtypeStruct((places, width), bf16), WORK, *mine)
-
-    mine, gate_picks, down_spread = tie((mine, gate_picks, down_spread))
-    other = send(mine, CORE_SWAP)
-    replica_gate = swap_blocks(gate_picks)
-    other, up_spread, down_spread = tie((other, up_spread, down_spread))
-    other, up_picks, down_picks = tie((other, up_spread[copy_source], down_spread[copy_source]))
+    other = swap_cores(mine)
 
     def expert_part(slot_rows, dtype):
         return whole(
             functools.partial(expert_kernel, width // 8),
             jax.ShapeDtypeStruct((places, width), dtype),
-            WORK,
+            1 << 20,
             slot_rows,
             home_gate,
             home_up,
             home_down,
         )
 
-    given = send(expert_part(other, bf16), CORE_SWAP)
+    given = swap_cores(expert_part(other, bf16))
     summed = whole(
         add_kernel,
         jax.ShapeDtypeStruct((places, width), bf16),
@@ -280,10 +302,12 @@
         given,
     )
 
-    summed, up_picks, replica_gate = tie((summed, up_picks, replica_gate))
     summed = summed.reshape(RING, capacity, width)
     back = [summed[0]] + [send(summed[n], deep_step(-n)) for n in range(1, RING)]
-    replica_up = swap_blocks(up_picks)
+    both_picks, replica_gate = tie((both_picks, replica_gate))
+    replica_both = swap_blocks(both_picks)
+    replica_gate = copied(replica_gate.reshape(1, depth, units))
+    mixing, replica_gate = tie((mixing, replica_gate))
     own, *parts = whole(
         functools.partial(gated_kernel, width // 8),
         (jax.ShapeDtypeStruct((line, width), f32),)
@@ -292,25 +316,21 @@
         mixing,
         *back,
     )
-
-    parts, down_picks, replica_up = tie((parts, down_picks, replica_up))
     parts = [send(parts[n - 1], wide_step(-n)) for n in range(1, RING)]
-    replica_down = swap_blocks(down_picks)
-    replica_gate = copied(replica_gate.reshape(1, depth, units))
-    replica_up = copied(replica_up.reshape(1, depth, units))
-    parts, replica_gate, replica_up = tie((parts, replica_gate, replica_up))
     own, *parts = whole(
         sum_kernel,
         (jax.ShapeDtypeStruct((rows, width), f32),)
         + (jax.ShapeDtypeStruct((rows, width), bf16),) * 3,
-        WORK,
+        1 << 20,
         own,
         *parts,
     )
 
-    parts, replica_down = tie((parts, replica_down))
+    parts, replica_both = tie((parts, replica_both))
     parts = [send(parts[n - 1], row_step(n)) for n in range(1, 4)]
-    replica_down = copied(replica_down.reshape(1, depth, units))
+    share = depth // experts
+    replica_up = replica_both[:, :share].reshape(1, depth, units)
+    replica_down = replica_both[:, share:].reshape(1, depth, units)
     mixed = whole(sum_kernel, (jax.ShapeDtypeStruct((rows, width), bf16),), 1 << 20, own, *parts)[0]
     return (mixed, replica_gate, replica_up, replica_down)
 

time: 401 us -> 372 us (0.928)
  the two profiles are of different devices: /device:TPU:2 before, /device:TPU:62 now
where the time goes in v3:
time: 372 us; the launch traced here: 371 us
  waiting for transfers between devices  211 us (57%)
  starting transfers between devices  84.9 us (23%)
  Pallas kernels  39.6 us (11%)
  local copies, waits for them, and re-layouts  23.7 us (6%)
  other arithmetic  10.4 us (3%)
    ppermute x26, waiting for transfers between devices, send(): return lax.ppermute(value, BOTH, pairs)  138 us
    all_to_all x4, waiting for transfers between devices, swap_blocks(): lax.all_to_all(blocks, 'expert', split_axis=0, concat_axis=0, tiled=True)  73.8 us
    all_to_all x4, starting transfers between devices, swap_blocks(): lax.all_to_all(blocks, 'expert', split_axis=0, concat_axis=0, tiled=True)  45.5 us
    ppermute x26, starting transfers between devices, send(): return lax.ppermute(value, BOTH, pairs)  39.4 us
    pallas_call x1, Pallas kernels, picked(): pl.pallas_call(pick_kernel, out_shape=jax.ShapeDtypeStruct(spread.shape,...  19.7 us
    pallas_call x9, Pallas kernels, whole(): pl.pallas_call(kernel, out_shape=out_shape, in_specs=[pl.BlockSpec(memory...  16.8 us
    unnamed x24, local copies, waits for them, and re-layouts  7.48 us
  transfers between devices with their start and end apart: 30, of which 14 were waited for; matrix products, arithmetic and copies ran while one was open for 7% of the time, Pallas kernels for 10%

profile of v3, /device:TPU:62, one launch (start us, length us, event | category | flops | bytes accessed | tf_op | source)
XLA Modules:
  0.0 371.1 jit_solution(16957532274327860037)
XLA Ops:
  0.6 0.7 convert_element_type.14
  1.3 0.7 reduce-precision_convert_fusion.1
  2.1 0.9 pad_maximum_fusion.3.refs_0_
  3.0 0.6 collective-permute-start.2
  3.6 2.4 collective-permute-start.1
  6.0 1.2 collective-permute-start
  7.2 4.5 %collective-permute-done.2.refs_3_ = bf16[8,7296]{1,0:T(8,128)(2,1)S(1)} collective-permute-done((bf16[8,7296]{1,0:T(8,128)(2,1)S(1)}, bf16[8,7296]{1,0:T(8,128)(2,1)S(1)}, u32[]{:S(2)}, u32[]{:S(2)}) %collective-permute-start.2) | collective-permute-done | bytes 116768 | tf_op jit(solution)/shard_map/ppermute | solution.py:49
  11.7 0.6 collective-permute-done.refs_1_
  12.4 0.8 collective-permute-start.5
  13.2 0.9 collective-permute-start.4
  14.1 2.2 collective-permute-start.3
  16.3 10.1 %all-to-all-start = ((bf16[32,224,256]{2,1,0:T(8,128)(2,1)}), bf16[32,224,256]{2,1,0:T(8,128)(2,1)}, u32[]{:S(2)}, u32[]{:S(2)}) async-start(bf16[32,224,256]{2,1,0:T(8,128)(2,1)} %bitcast.8), calls=%async_computation | async-start | bytes 7340032 | tf_op jit(solution)/shard_map/all_to_all | solution.py:53
  26.5 0.6 gather_fusion
  27.2 2.9 collective-permute-done.5.refs_3_
  30.1 17.7 %collective-permute-done.3.refs_1_ = bf16[32,7296]{1,0:T(8,128)(2,1)S(1)} collective-permute-done((bf16[32,7296]{1,0:T(8,128)(2,1)S(1)}, bf16[32,7296]{1,0:T(8,128)(2,1)S(1)}, u32[]{:S(2)}, u32[]{:S(2)}) %collective-permute-start.3) | collective-permute-done | bytes 466976 | tf_op jit(solution)/shard_map/ppermute | solution.py:49
  47.8 1.9 shard_map.112
  49.7 1.3 fusion.18
  51.0 4.2 %collective-permute-start.7 = (bf16[48,7168]{1,0:T(8,128)(2,1)}, bf16[48,7168]{1,0:T(8,128)(2,1)}, u32[]{:S(2)}, u32[]{:S(2)}) collective-permute-start(bf16[48,7168]{1,0:T(8,128)(2,1)} %get-tuple-element.67), channel_id=1, source_target_pairs={{0,16},{1,17},{2,18},{3,19},{4,20},{5,21},{6,22},{7,23},{8,24},{9,... | collective-permute-start | bytes 2064392 | tf_op jit(solution)/shard_map/ppermute | solution.py:49
  55.2 2.6 collective-permute-start.6
  57.8 5.7 %pad_maximum_fusion = bf16[32,448,256]{2,1,0:T(8,128)(2,1)} fusion(bf16[32,224,256]{2,1,0:T(8,128)(2,1)} %bitcast.10, bf16[32,224,256]{2,1,0:T(8,128)(2,1)S(1)} %bitcast.9), kind=kLoop, calls=%fused_computation.2 | loop fusion | flops 14680064 | bytes 14680064 | tf_op jit(solution)/shard_map/concatenate | solution.py:261
  63.6 20.4 %all-to-all-done = bf16[32,224,256]{2,1,0:T(8,128)(2,1)} async-done(((bf16[32,224,256]{2,1,0:T(8,128)(2,1)}), bf16[32,224,256]{2,1,0:T(8,128)(2,1)}, u32[]{:S(2)}, u32[]{:S(2)}) %all-to-all-start) | async-done | bytes 3670048 | tf_op jit(solution)/shard_map/all_to_all | solution.py:53
  84.0 12.4 %all-to-all-start.1 = ((bf16[32,448,256]{2,1,0:T(8,128)(2,1)}), bf16[32,448,256]{2,1,0:T(8,128)(2,1)}, u32[]{:S(2)}, u32[]{:S(2)}) async-start(bf16[32,448,256]{2,1,0:T(8,128)(2,1)} %pad_maximum_fusion), calls=%async_computation.1 | async-start | bytes 14680064 | tf_op jit(solution)/shard_map/all_to_all | solution.py:53
  96.5 13.2 %collective-permute-done.7.refs_2_ = bf16[48,7168]{1,0:T(8,128)(2,1)} collective-permute-done((bf16[48,7168]{1,0:T(8,128)(2,1)}, bf16[48,7168]{1,0:T(8,128)(2,1)}, u32[]{:S(2)}, u32[]{:S(2)}) %collective-permute-start.7) | collective-permute-done | bytes 688160 | tf_op jit(solution)/shard_map/ppermute | solution.py:49
  109.7 1.7 shard_map.115.rows_ref
  111.4 0.2 fusion.17
  111.7 0.5 collective-permute-start.12
  112.3 0.4 collective-permute-start.10
  112.8 1.1 collective-permute-done.9
  113.9 1.0 collective-permute-done.12
  114.9 1.0 collective-permute-done.11
  115.8 1.0 collective-permute-done.10
  116.8 0.2 pad_maximum_fusion.1.rows_ref
  117.1 4.8 %shard_map.117 = bf16[192,7168]{1,0:T(8,128)(2,1)S(1)} custom-call(bf16[192,7168]{1,0:T(8,128)(2,1)S(1)} %pad_maximum_fusion.1.rows_ref, bf16[1,7168,256]{2,1,0:T(8,128)(2,1)S(1)} %copy-done.2, bf16[1,7168,256]{2,1,0:T(8,128)(2,1)S(1)} %copy-done.5, bf16[1,7168,256]{2,1,0:T(8,128)(2,1)} %down_ref.3), custom_call_target="tpu_custom_call" | custom-call | flops 1048576 | bytes 1048576 | tf_op jit(solution)/shard_map/pallas_call | solution.py:104
  122.0 1.4 fusion.16
  123.5 0.4 collective-permute-start.16
  124.0 0.4 collective-permute-start.14
  124.4 4.7 %gather_fusion.1 = bf16[32,224,256]{2,1,0:T(8,128)(2,1)} fusion(bf16[32,224,256]{2,1,0:T(8,128)(2,1)} %all-to-all-done, s32[1024]{0:T(1024)S(1)} %pad_clamp_fusion), kind=kCustom, calls=%fused_computation.1 | custom fusion | bytes 7340160 | tf_op jit(solution)/shard_map/gather | solution.py:264
  129.0 44.2 %all-to-all-done.1.refs_0_ = bf16[32,448,256]{2,1,0:T(8,128)(2,1)} async-done(((bf16[32,448,256]{2,1,0:T(8,128)(2,1)}), bf16[32,448,256]{2,1,0:T(8,128)(2,1)}, u32[]{:S(2)}, u32[]{:S(2)}) %all-to-all-start.1) | async-done | bytes 7340064 | tf_op jit(solution)/shard_map/all_to_all | solution.py:53
  173.2 13.7 %all-to-all-start.2 = ((bf16[32,224,256]{2,1,0:T(8,128)(2,1)}), bf16[32,224,256]{2,1,0:T(8,128)(2,1)}, u32[]{:S(2)}, u32[]{:S(2)}) async-start(bf16[32,224,256]{2,1,0:T(8,128)(2,1)} %gather_fusion.1), calls=%async_computation.2 | async-start | bytes 7340032 | tf_op jit(solution)/shard_map/all_to_all | solution.py:53
  186.9 2.0 copy-done.3
  188.9 2.0 copy-done.6
  191.0 2.0 copy-done.7
  193.0 5.2 %shard_map.116.one_ref = f32[192,7168]{1,0:T(8,128)} custom-call(bf16[192,7168]{1,0:T(8,128)(2,1)S(1)} %shard_map.115.rows_ref, bf16[1,7168,256]{2,1,0:T(8,128)(2,1)S(1)} %copy-done.3, bf16[1,7168,256]{2,1,0:T(8,128)(2,1)S(1)} %copy-done.6, bf16[1,7168,256]{2,1,0:T(8,128)(2,1)S(1)} %copy-done.7), custom_call_target="tpu_custom_call" | custom-call | flops 1048576 | bytes 1048576 | tf_op jit(solution)/shard_map/pallas_call | solution.py:104
  198.3 2.0 pad_maximum_fusion.2.two_ref
  200.3 1.3 copy-done.8
  201.6 0.4 shard_map.118
  202.1 1.3 fusion.15
  203.4 1.5 collective-permute-start.19
  204.9 1.1 collective-permute-start.18
  206.0 2.2 collective-permute-start.17
  208.2 19.7 %shard_map.113 = bf16[32,448,256]{2,1,0:T(8,128)(2,1)} custom-call(s32[32]{0:T(128)} %source_ref.1, bf16[32,448,256]{2,1,0:T(8,128)(2,1)} %all-to-all-done.1.refs_0_), custom_call_target="tpu_custom_call" | custom-call | bytes 1048576 | tf_op jit(solution)/shard_map/pallas_call | solution.py:176
  227.8 9.2 %all-to-all-done.2 = bf16[32,224,256]{2,1,0:T(8,128)(2,1)} async-done(((bf16[32,224,256]{2,1,0:T(8,128)(2,1)}), bf16[32,224,256]{2,1,0:T(8,128)(2,1)}, u32[]{:S(2)}, u32[]{:S(2)}) %all-to-all-start.2) | async-done | bytes 3670048 | tf_op jit(solution)/shard_map/all_to_all | solution.py:53
  237.1 9.3 %all-to-all-start.3 = ((bf16[32,448,256]{2,1,0:T(8,128)(2,1)}), bf16[32,448,256]{2,1,0:T(8,128)(2,1)}, u32[]{:S(2)}, u32[]{:S(2)}) async-start(bf16[32,448,256]{2,1,0:T(8,128)(2,1)} %shard_map.113), calls=%async_computation.3 | async-start | bytes 14680064 | tf_op jit(solution)/shard_map/all_to_all | solution.py:53
  246.4 3.1 shard_map.114
  249.5 1.8 shard_map.119
  251.3 0.9 collective-permute-start.20
  252.2 1.2 collective-permute-start.21
  253.4 2.1 collective-permute-start.22
  255.5 89.7 %collective-permute-done.20.refs_0_ = bf16[32,7168]{1,0:T(8,128)(2,1)S(1)} collective-permute-done((bf16[32,7168]{1,0:T(8,128)(2,1)S(1)}, bf16[32,7168]{1,0:T(8,128)(2,1)S(1)}, u32[]{:S(2)}, u32[]{:S(2)}) %collective-permute-start.20) | collective-permute-done | bytes 458784 | tf_op jit(solution)/shard_map/ppermute | solution.py:49
  345.1 4.9 %collective-permute-done.21.refs_1_ = bf16[32,7168]{1,0:T(8,128)(2,1)S(1)} collective-permute-done((bf16[32,7168]{1,0:T(8,128)(2,1)S(1)}, bf16[32,7168]{1,0:T(8,128)(2,1)S(1)}, u32[]{:S(2)}, u32[]{:S(2)}) %collective-permute-start.21) | collective-permute-done | bytes 458784 | tf_op jit(solution)/shard_map/ppermute | solution.py:49
  350.3 10.6 %collective-permute-start.23 = (bf16[8,7168]{1,0:T(8,128)(2,1)S(1)}, bf16[8,7168]{1,0:T(8,128)(2,1)S(1)}, u32[]{:S(2)}, u32[]{:S(2)}) collective-permute-start(bf16[8,7168]{1,0:T(8,128)(2,1)S(1)} %get-tuple-element.47), channel_id=1, source_target_pairs={{0,64},{1,65},{2,66},{3,67},{4,68},{5,69},{6,70},{7,71},{8,72},{9,... | collective-permute-start | bytes 344072 | tf_op jit(solution)/shard_map/ppermute | solution.py:49
  360.9 2.8 collective-permute-start.25
  363.7 6.7 %fusion.14 = (bf16[32,224,256]{2,1,0:T(8,128)(2,1)}, bf16[32,224,256]{2,1,0:T(8,128)(2,1)}) fusion(bf16[32,448,256]{2,1,0:T(8,128)(2,1)} %all-to-all-done.3), kind=kLoop, calls=%fused_computation.35 | loop fusion | bytes 14680064 | tf_op jit(solution)/shard_map/slice | solution.py:333
  370.4 0.7 shard_map.121
  (49 shorter events, 0.9 us)
Async XLA Ops:
  0.6 25.9 %copy-start = (s32[32]{0:T(128)S(1)}, s32[32]{0:T(128)}, u32[]{:S(2)}) copy-start(s32[32]{0:T(128)} %param.11) | copy-start | bytes 388
  3.0 8.7 %collective-permute-start.2 = (bf16[8,7296]{1,0:T(8,128)(2,1)S(1)}, bf16[8,7296]{1,0:T(8,128)(2,1)S(1)}, u32[]{:S(2)}, u32[]{:S(2)}) collective-permute-start(bf16[8,7296]{1,0:T(8,128)(2,1)S(1)} %pad_maximum_fusion.3.refs_0_), channel_id=1, source_target_pairs={{0,65},{1,64},{2,67},{3,66},{4,69},{5,68},{6,71},{7,70},{8,73},{9,... | collective-permute-start | bytes 350216 | tf_op jit(solution)/shard_map/ppermute | solution.py:49
  3.6 8.2 %collective-permute-start.1 = (bf16[8,7296]{1,0:T(8,128)(2,1)S(1)}, bf16[8,7296]{1,0:T(8,128)(2,1)S(1)}, u32[]{:S(2)}, u32[]{:S(2)}) collective-permute-start(bf16[8,7296]{1,0:T(8,128)(2,1)S(1)} %pad_maximum_fusion.3.refs_0_), channel_id=1, source_target_pairs={{0,1},{1,0},{2,3},{3,2},{4,5},{5,4},{6,7},{7,6},{8,9},{9,8},{10,11... | collective-permute-start | bytes 350216 | tf_op jit(solution)/shard_map/ppermute | solution.py:49
  6.0 6.3 %collective-permute-start = (bf16[8,7296]{1,0:T(8,128)(2,1)S(1)}, bf16[8,7296]{1,0:T(8,128)(2,1)S(1)}, u32[]{:S(2)}, u32[]{:S(2)}) collective-permute-start(bf16[8,7296]{1,0:T(8,128)(2,1)S(1)} %pad_maximum_fusion.3.refs_0_), channel_id=1, source_target_pairs={{0,64},{1,65},{2,66},{3,67},{4,68},{5,69},{6,70},{7,71},{8,72},{9,... | collective-permute-start | bytes 350216 | tf_op jit(solution)/shard_map/ppermute | solution.py:49
  12.4 17.7 %collective-permute-start.5 = (bf16[32,7296]{1,0:T(8,128)(2,1)S(1)}, bf16[32,7296]{1,0:T(8,128)(2,1)S(1)}, u32[]{:S(2)}, u32[]{:S(2)}) collective-permute-start(bf16[32,7296]{1,0:T(8,128)(2,1)S(1)} %shard_map.111.refs_0_), channel_id=1, source_target_pairs={{0,6},{1,7},{2,0},{3,1},{4,2},{5,3},{6,4},{7,5},{8,14},{9,15},{10,... | collective-permute-start | bytes 1400840 | tf_op jit(solution)/shard_map/ppermute | solution.py:49
  13.2 16.9 %collective-permute-start.4 = (bf16[32,7296]{1,0:T(8,128)(2,1)S(1)}, bf16[32,7296]{1,0:T(8,128)(2,1)S(1)}, u32[]{:S(2)}, u32[]{:S(2)}) collective-permute-start(bf16[32,7296]{1,0:T(8,128)(2,1)S(1)} %shard_map.111.refs_0_), channel_id=1, source_target_pairs={{0,4},{1,5},{2,6},{3,7},{4,0},{5,1},{6,2},{7,3},{8,12},{9,13},{10,... | collective-permute-start | bytes 1400840 | tf_op jit(solution)/shard_map/ppermute | solution.py:49
  14.1 33.6 %collective-permute-start.3 = (bf16[32,7296]{1,0:T(8,128)(2,1)S(1)}, bf16[32,7296]{1,0:T(8,128)(2,1)S(1)}, u32[]{:S(2)}, u32[]{:S(2)}) collective-permute-start(bf16[32,7296]{1,0:T(8,128)(2,1)S(1)} %shard_map.111.refs_0_), channel_id=1, source_target_pairs={{0,2},{1,3},{2,4},{3,5},{4,6},{5,7},{6,0},{7,1},{8,10},{9,11},{10,... | collective-permute-start | bytes 1400840 | tf_op jit(solution)/shard_map/ppermute | solution.py:49
  16.3 67.7 %all-to-all-start = ((bf16[32,224,256]{2,1,0:T(8,128)(2,1)}), bf16[32,224,256]{2,1,0:T(8,128)(2,1)}, u32[]{:S(2)}, u32[]{:S(2)}) async-start(bf16[32,224,256]{2,1,0:T(8,128)(2,1)} %bitcast.8), calls=%async_computation | async-start | bytes 7340032 | tf_op jit(solution)/shard_map/all_to_all | solution.py:53
  49.6 1.4 copy-start.9
  49.7 8.2 %copy-start.4 = (bf16[1,7168,256]{2,1,0:T(8,128)(2,1)S(1)}, bf16[1,7168,256]{2,1,0:T(8,128)(2,1)}, u32[]{:S(2)}) copy-start(bf16[1,7168,256]{2,1,0:T(8,128)(2,1)} %up_ref.3) | copy-start | bytes 11010052
  51.0 45.4 %collective-permute-start.8 = (bf16[48,7168]{1,0:T(8,128)(2,1)}, bf16[48,7168]{1,0:T(8,128)(2,1)}, u32[]{:S(2)}, u32[]{:S(2)}) collective-permute-start(bf16[48,7168]{1,0:T(8,128)(2,1)} %get-tuple-element.66), channel_id=1, source_target_pairs={{0,24},{1,25},{2,26},{3,27},{4,28},{5,29},{6,30},{7,31},{8,0},{9,1... | collective-permute-start | bytes 2064392 | tf_op jit(solution)/shard_map/ppermute | solution.py:49
  51.0 58.7 %collective-permute-start.7 = (bf16[48,7168]{1,0:T(8,128)(2,1)}, bf16[48,7168]{1,0:T(8,128)(2,1)}, u32[]{:S(2)}, u32[]{:S(2)}) collective-permute-start(bf16[48,7168]{1,0:T(8,128)(2,1)} %get-tuple-element.67), channel_id=1, source_target_pairs={{0,16},{1,17},{2,18},{3,19},{4,20},{5,21},{6,22},{7,23},{8,24},{9,... | collective-permute-start | bytes 2064392 | tf_op jit(solution)/shard_map/ppermute | solution.py:49
  55.2 54.5 %collective-permute-start.6 = (bf16[48,7168]{1,0:T(8,128)(2,1)}, bf16[48,7168]{1,0:T(8,128)(2,1)}, u32[]{:S(2)}, u32[]{:S(2)}) collective-permute-start(bf16[48,7168]{1,0:T(8,128)(2,1)} %get-tuple-element.68), channel_id=1, source_target_pairs={{0,8},{1,9},{2,10},{3,11},{4,12},{5,13},{6,14},{7,15},{8,16},{9,17... | collective-permute-start | bytes 2064392 | tf_op jit(solution)/shard_map/ppermute | solution.py:49
  84.0 89.2 %all-to-all-start.1 = ((bf16[32,448,256]{2,1,0:T(8,128)(2,1)}), bf16[32,448,256]{2,1,0:T(8,128)(2,1)}, u32[]{:S(2)}, u32[]{:S(2)}) async-start(bf16[32,448,256]{2,1,0:T(8,128)(2,1)} %pad_maximum_fusion), calls=%async_computation.1 | async-start | bytes 14680064 | tf_op jit(solution)/shard_map/all_to_all | solution.py:53
  111.4 5.7 %copy-start.5 = (bf16[1,7168,256]{2,1,0:T(8,128)(2,1)S(1)}, bf16[1,7168,256]{2,1,0:T(8,128)(2,1)}, u32[]{:S(2)}) copy-start(bf16[1,7168,256]{2,1,0:T(8,128)(2,1)} %up_ref.3) | copy-start | bytes 11010052
  111.6 5.5 %copy-start.2 = (bf16[1,7168,256]{2,1,0:T(8,128)(2,1)S(1)}, bf16[1,7168,256]{2,1,0:T(8,128)(2,1)}, u32[]{:S(2)}) copy-start(bf16[1,7168,256]{2,1,0:T(8,128)(2,1)} %gate_ref.3) | copy-start | bytes 11010052
  111.7 2.2 collective-permute-start.9
  111.7 3.1 collective-permute-start.12
  112.2 3.6 collective-permute-start.11
  112.3 4.5 %collective-permute-start.10 = (bf16[48,7168]{1,0:T(8,128)(2,1)S(1)}, bf16[48,7168]{1,0:T(8,128)(2,1)S(1)}, u32[]{:S(2)}, u32[]{:S(2)}) collective-permute-start(bf16[48,7168]{1,0:T(8,128)(2,1)S(1)} %get-tuple-element.65), channel_id=1, source_target_pairs={{0,32},{1,33},{2,34},{3,35},{4,36},{5,37},{6,38},{7,39},{8,40},{9,... | collective-permute-start | bytes 2064392 | tf_op jit(solution)/shard_map/ppermute | solution.py:49
  121.9 2.4 copy-start.11
  123.3 74.9 %collective-permute-start.13 = (bf16[48,7168]{1,0:T(8,128)(2,1)}, bf16[48,7168]{1,0:T(8,128)(2,1)}, u32[]{:S(2)}, u32[]{:S(2)}) collective-permute-start(bf16[48,7168]{1,0:T(8,128)(2,1)} %get-tuple-element.58), channel_id=1, source_target_pairs={{0,32},{1,33},{2,34},{3,35},{4,36},{5,37},{6,38},{7,39},{8,40},{9,... | collective-permute-start | bytes 2064392 | tf_op jit(solution)/shard_map/ppermute | solution.py:49
  123.5 74.8 %collective-permute-start.16 = (bf16[48,7168]{1,0:T(8,128)(2,1)}, bf16[48,7168]{1,0:T(8,128)(2,1)}, u32[]{:S(2)}, u32[]{:S(2)}) collective-permute-start(bf16[48,7168]{1,0:T(8,128)(2,1)} %get-tuple-element.59), channel_id=1, source_target_pairs={{0,32},{1,33},{2,34},{3,35},{4,36},{5,37},{6,38},{7,39},{8,40},{9,... | collective-permute-start | bytes 2064392 | tf_op jit(solution)/shard_map/ppermute | solution.py:49
  123.8 74.4 %collective-permute-start.15 = (bf16[48,7168]{1,0:T(8,128)(2,1)}, bf16[48,7168]{1,0:T(8,128)(2,1)}, u32[]{:S(2)}, u32[]{:S(2)}) collective-permute-start(bf16[48,7168]{1,0:T(8,128)(2,1)} %get-tuple-element.60), channel_id=1, source_target_pairs={{0,32},{1,33},{2,34},{3,35},{4,36},{5,37},{6,38},{7,39},{8,40},{9,... | collective-permute-start | bytes 2064392 | tf_op jit(solution)/shard_map/ppermute | solution.py:49
  124.0 74.3 %collective-permute-start.14 = (bf16[48,7168]{1,0:T(8,128)(2,1)S(1)}, bf16[48,7168]{1,0:T(8,128)(2,1)}, u32[]{:S(2)}, u32[]{:S(2)}) collective-permute-start(bf16[48,7168]{1,0:T(8,128)(2,1)S(1)} %get-tuple-element.61), channel_id=1, source_target_pairs={{0,32},{1,33},{2,34},{3,35},{4,36},{5,37},{6,38},{7,39},{8,40},{9,... | collective-permute-start | bytes 2064392 | tf_op jit(solution)/shard_map/ppermute | solution.py:49
  173.2 63.8 %all-to-all-start.2 = ((bf16[32,224,256]{2,1,0:T(8,128)(2,1)}), bf16[32,224,256]{2,1,0:T(8,128)(2,1)}, u32[]{:S(2)}, u32[]{:S(2)}) async-start(bf16[32,224,256]{2,1,0:T(8,128)(2,1)} %gather_fusion.1), calls=%async_computation.2 | async-start | bytes 7340032 | tf_op jit(solution)/shard_map/all_to_all | solution.py:53
  186.9 2.0 copy-start.3
  188.9 2.0 copy-start.6
  191.0 2.0 copy-start.7
  198.2 3.4 copy-start.8
  203.4 46.1 %collective-permute-start.19 = (bf16[48,7168]{1,0:T(8,128)(2,1)}, bf16[48,7168]{1,0:T(8,128)(2,1)S(1)}, u32[]{:S(2)}, u32[]{:S(2)}) collective-permute-start(bf16[48,7168]{1,0:T(8,128)(2,1)} %get-tuple-element.54), channel_id=1, source_target_pairs={{0,8},{1,9},{2,10},{3,11},{4,12},{5,13},{6,14},{7,15},{8,16},{9,17... | collective-permute-start | bytes 2064392 | tf_op jit(solution)/shard_map/ppermute | solution.py:49
  204.9 44.6 %collective-permute-start.18 = (bf16[48,7168]{1,0:T(8,128)(2,1)}, bf16[48,7168]{1,0:T(8,128)(2,1)S(1)}, u32[]{:S(2)}, u32[]{:S(2)}) collective-permute-start(bf16[48,7168]{1,0:T(8,128)(2,1)} %get-tuple-element.55), channel_id=1, source_target_pairs={{0,16},{1,17},{2,18},{3,19},{4,20},{5,21},{6,22},{7,23},{8,24},{9,... | collective-permute-start | bytes 2064392 | tf_op jit(solution)/shard_map/ppermute | solution.py:49
  206.0 43.5 %collective-permute-start.17 = (bf16[48,7168]{1,0:T(8,128)(2,1)S(1)}, bf16[48,7168]{1,0:T(8,128)(2,1)S(1)}, u32[]{:S(2)}, u32[]{:S(2)}) collective-permute-start(bf16[48,7168]{1,0:T(8,128)(2,1)S(1)} %get-tuple-element.56), channel_id=1, source_target_pairs={{0,24},{1,25},{2,26},{3,27},{4,28},{5,29},{6,30},{7,31},{8,0},{9,1... | collective-permute-start | bytes 2064392 | tf_op jit(solution)/shard_map/ppermute | solution.py:49
  237.1 113.2 %all-to-all-start.3 = ((bf16[32,448,256]{2,1,0:T(8,128)(2,1)}), bf16[32,448,256]{2,1,0:T(8,128)(2,1)}, u32[]{:S(2)}, u32[]{:S(2)}) async-start(bf16[32,448,256]{2,1,0:T(8,128)(2,1)} %shard_map.113), calls=%async_computation.3 | async-start | bytes 14680064 | tf_op jit(solution)/shard_map/all_to_all | solution.py:53
  246.4 3.1 copy-start.10
  251.3 93.8 %collective-permute-start.20 = (bf16[32,7168]{1,0:T(8,128)(2,1)S(1)}, bf16[32,7168]{1,0:T(8,128)(2,1)S(1)}, u32[]{:S(2)}, u32[]{:S(2)}) collective-permute-start(bf16[32,7168]{1,0:T(8,128)(2,1)S(1)} %get-tuple-element.39), channel_id=1, source_target_pairs={{0,6},{1,7},{2,0},{3,1},{4,2},{5,3},{6,4},{7,5},{8,14},{9,15},{10,... | collective-permute-start | bytes 1376264 | tf_op jit(solution)/shard_map/ppermute | solution.py:49
  252.2 97.8 %collective-permute-start.21 = (bf16[32,7168]{1,0:T(8,128)(2,1)S(1)}, bf16[32,7168]{1,0:T(8,128)(2,1)S(1)}, u32[]{:S(2)}, u32[]{:S(2)}) collective-permute-start(bf16[32,7168]{1,0:T(8,128)(2,1)S(1)} %get-tuple-element.40), channel_id=1, source_target_pairs={{0,4},{1,5},{2,6},{3,7},{4,0},{5,1},{6,2},{7,3},{8,12},{9,13},{10,... | collective-permute-start | bytes 1376264 | tf_op jit(solution)/shard_map/ppermute | solution.py:49
  253.4 96.7 %collective-permute-start.22 = (bf16[32,7168]{1,0:T(8,128)(2,1)S(1)}, bf16[32,7168]{1,0:T(8,128)(2,1)S(1)}, u32[]{:S(2)}, u32[]{:S(2)}) collective-permute-start(bf16[32,7168]{1,0:T(8,128)(2,1)S(1)} %get-tuple-element.41), channel_id=1, source_target_pairs={{0,2},{1,3},{2,4},{3,5},{4,6},{5,7},{6,0},{7,1},{8,10},{9,11},{10,... | collective-permute-start | bytes 1376264 | tf_op jit(solution)/shard_map/ppermute | solution.py:49
  350.3 20.1 %collective-permute-start.23 = (bf16[8,7168]{1,0:T(8,128)(2,1)S(1)}, bf16[8,7168]{1,0:T(8,128)(2,1)S(1)}, u32[]{:S(2)}, u32[]{:S(2)}) collective-permute-start(bf16[8,7168]{1,0:T(8,128)(2,1)S(1)} %get-tuple-element.47), channel_id=1, source_target_pairs={{0,64},{1,65},{2,66},{3,67},{4,68},{5,69},{6,70},{7,71},{8,72},{9,... | collective-permute-start | bytes 344072 | tf_op jit(solution)/shard_map/ppermute | solution.py:49
  360.9 9.5 %collective-permute-start.24 = (bf16[8,7168]{1,0:T(8,128)(2,1)S(1)}, bf16[8,7168]{1,0:T(8,128)(2,1)S(1)}, u32[]{:S(2)}, u32[]{:S(2)}) collective-permute-start(bf16[8,7168]{1,0:T(8,128)(2,1)S(1)} %get-tuple-element.48), channel_id=1, source_target_pairs={{0,1},{1,0},{2,3},{3,2},{4,5},{5,4},{6,7},{7,6},{8,9},{9,8},{10,11... | collective-permute-start | bytes 344072 | tf_op jit(solution)/shard_map/ppermute | solution.py:49
  360.9 9.5 %collective-permute-start.25 = (bf16[8,7168]{1,0:T(8,128)(2,1)S(1)}, bf16[8,7168]{1,0:T(8,128)(2,1)S(1)}, u32[]{:S(2)}, u32[]{:S(2)}) collective-permute-start(bf16[8,7168]{1,0:T(8,128)(2,1)S(1)} %get-tuple-element.49), channel_id=1, source_target_pairs={{0,65},{1,64},{2,67},{3,66},{4,69},{5,68},{6,71},{7,70},{8,73},{9,... | collective-permute-start | bytes 344072 | tf_op jit(solution)/shard_map/ppermute | solution.py:49
  363.7 7.4 %copy-start.1 = (s32[32]{0:T(128)S(1)}, s32[32]{0:T(128)}, u32[]{:S(2)}) copy-start(s32[32]{0:T(128)} %param.11) | copy-start | bytes 388

commit v4 on v3

--- a/solution.py
+++ b/solution.py
@@ -63,8 +63,8 @@
 
 
 def select_kernel(fanout, capacity, chunk, column_ref, *refs):
-    blocks, (chosen_ref, mixing_ref) = refs[:RING], refs[RING:]
-    width = chosen_ref.shape[1]
+    blocks, (*chosen_refs, mixing_ref) = refs[:RING], refs[RING:]
+    width = chosen_refs[0].shape[1]
     f32 = jnp.float32
     note = jnp.concatenate([b[:, width:].astype(f32) for b in blocks], axis=0)
     plane = note.shape[0]
@@ -95,9 +95,11 @@
     taken = taken.astype(jnp.bfloat16)
     for low in range(0, width, chunk):
         held = jnp.concatenate([b[:, low : low + chunk] for b in blocks], axis=0)
-        chosen_ref[:, low : low + chunk] = lax.dot_general(
+        chosen = lax.dot_general(
             taken, held, (((0,), (0,)), ((), ())), preferred_element_type=f32
         ).astype(jnp.bfloat16)
+        for n, chosen_ref in enumerate(chosen_refs):
+            chosen_ref[:, low : low + chunk] = chosen[n * capacity : (n + 1) * capacity]
 
 
 def whole(kernel, out_shape, work, *operands, scalars=()):
@@ -107,7 +109,7 @@
         in_specs=[pl.BlockSpec(memory_space=pltpu.SMEM)] * len(scalars)
         + [pl.BlockSpec(memory_space=pltpu.VMEM)] * len(operands),
         out_specs=jax.tree.map(lambda _: pl.BlockSpec(memory_space=pltpu.VMEM), out_shape),
-        compiler_params=pltpu.CompilerParams(vmem_limit_bytes=40 << 20),
+        compiler_params=pltpu.CompilerParams(vmem_limit_bytes=48 << 20),
         cost_estimate=pl.CostEstimate(flops=work, bytes_accessed=1 << 20, transcendentals=0),
     )(*scalars, *operands)
 
@@ -149,48 +151,58 @@
         low += ref.shape[0]
 
 
-def expert_kernel(chunk, rows_ref, gate_ref, up_ref, down_ref, out_ref):
+def expert_kernel(chunk, *refs):
     f32 = jnp.float32
-    gate_act = jnp.dot(rows_ref[...], gate_ref[0], preferred_element_type=f32)
-    up_act = jnp.dot(rows_ref[...], up_ref[0], preferred_element_type=f32)
-    hidden = (gate_act / (1.0 + jnp.exp(-gate_act)) * up_act).astype(jnp.bfloat16)
-    for low in range(0, out_ref.shape[1], chunk):
-        out_ref[:, low : low + chunk] = lax.dot_general(
-            hidden,
-            down_ref[0, low : low + chunk],
-            (((1,), (1,)), ((), ())),
-            preferred_element_type=f32,
-        ).astype(out_ref.dtype)
-
-
-def add_kernel(one_ref, two_ref, out_ref):
-    out_ref[...] = (one_ref[...] + two_ref[...].astype(jnp.float32)).astype(out_ref.dtype)
-
-
-def pick_kernel(source_ref, *refs):
-    refs[-1][...] = refs[0][...]
+    blocks, weights, outs = refs[:RING], refs[RING : RING + 6], refs[RING + 6 :]
+    rows = jnp.concatenate([b[...] for b in blocks], axis=0)
+    hidden = []
+    for gate_ref, up_ref in (weights[:2], weights[3:5]):
+        gate_act = jnp.dot(rows, gate_ref[0], preferred_element_type=f32)
+        up_act = jnp.dot(rows, up_ref[0], preferred_element_type=f32)
+        hidden.append((gate_act / (1.0 + jnp.exp(-gate_act)) * up_act).astype(jnp.bfloat16))
+    height = outs[0].shape[0]
+    for low in range(0, outs[0].shape[1], chunk):
+        span = slice(low, low + chunk)
+        total = 0.0
+        for part, down_ref in zip(hidden, (weights[2], weights[5])):
+            total = total + lax.dot_general(
+                part, down_ref[0, span], (((1,), (1,)), ((), ())), preferred_element_type=f32
+            )
+        for n, out_ref in enumerate(outs):
+            out_ref[:, span] = total[n * height : (n + 1) * height].astype(out_ref.dtype)
+
+
+def pick_kernel(source_ref, from_ref, to_ref, held, came, went):
+    count = held.shape[0]
+    inward = [
+        pltpu.make_async_copy(from_ref.at[source_ref[n]], held.at[n], came.at[n])
+        for n in range(count)
+    ]
+    outward = [pltpu.make_async_copy(held.at[n], to_ref.at[n], went.at[n]) for n in range(count)]
+    for copy in inward:
+        copy.start()
+    for first, second in zip(inward, outward):
+        first.wait()
+        second.start()
+    for copy in outward:
+        copy.wait()
 
 
 def picked(copy_source, spread):
-    count, height, units = spread.shape
+    count = spread.shape[0]
     return pl.pallas_call(
         pick_kernel,
         out_shape=jax.ShapeDtypeStruct(spread.shape, spread.dtype),
-        grid_spec=pltpu.PrefetchScalarGridSpec(
-            num_scalar_prefetch=1,
-            grid=(count,),
-            in_specs=[pl.BlockSpec((1, height, units), lambda i, s: (s[i], 0, 0))],
-            out_specs=pl.BlockSpec((1, height, units), lambda i, s: (i, 0, 0)),
-        ),
+        in_specs=[pl.BlockSpec(memory_space=pltpu.SMEM), pl.BlockSpec(memory_space=pl.ANY)],
+        out_specs=pl.BlockSpec(memory_space=pl.ANY),
+        scratch_shapes=[
+            pltpu.VMEM(spread.shape, spread.dtype),
+            pltpu.SemaphoreType.DMA((count,)),
+            pltpu.SemaphoreType.DMA((count,)),
+        ],
+        compiler_params=pltpu.CompilerParams(vmem_limit_bytes=16 << 20),
         cost_estimate=pl.CostEstimate(flops=0, bytes_accessed=1 << 20, transcendentals=0),
     )(copy_source, spread)
-
-
-def swap_cores(value, parts=4):
-    rows = value.shape[0] // parts
-    return jnp.concatenate(
-        [send(value[n * rows : (n + 1) * rows], CORE_SWAP) for n in range(parts)], axis=0
-    )
 
 
 def copy_kernel(from_ref, to_ref, held, came, went):
@@ -250,64 +262,48 @@
     note = jnp.concatenate([top_ids.astype(bf16)] + bf16_pieces(gates), axis=1)
     note = jnp.pad(note, ((0, 0), (0, NOTE - note.shape[1])))
     held, gate_blocks = tie((jnp.concatenate([tokens, note], axis=1), home_gate.reshape(blocked)))
-    near = [send(held, row_step(n)) for n in range(1, 4)]
+    near = [send(held, row_step(n)) for n in range(1, RING)]
     gate_spread = swap_blocks(gate_blocks)
-    line = 4 * rows
+    both = jnp.concatenate([home_up.reshape(blocked), home_down.reshape(blocked)], axis=1)
+    near, far_gate = tie((near, send(home_gate, CORE_SWAP)))
+    line = RING * rows
     held = whole(
         stack_kernel, jax.ShapeDtypeStruct((line, width + NOTE), bf16), WORK, held, *near
     )
 
     blocks = [held] + [send(held, wide_step(n)) for n in range(1, RING)]
-    both = jnp.concatenate([home_up.reshape(blocked), home_down.reshape(blocked)], axis=1)
-    both, gate_spread = tie((both, gate_spread))
-    both_spread = swap_blocks(both)
-    gate_picks = gate_spread[copy_source]
+    far = (send(home_up, CORE_SWAP), send(home_down, CORE_SWAP))
+    blocks, far = tie((blocks, far))
     places = RING * capacity
-    chosen, mixing = whole(
+    *chosen, mixing = whole(
         functools.partial(select_kernel, fanout, capacity, width // 8),
-        (
-            jax.ShapeDtypeStruct((places, width), bf16),
-            jax.ShapeDtypeStruct((RING * line, places), f32),
-        ),
-        WORK >> 3,
+        (jax.ShapeDtypeStruct((capacity, width), bf16),) * RING
+        + (jax.ShapeDtypeStruct((RING * line, places), f32),),
+        WORK,
         *blocks,
         scalars=(column_expert,),
     )
 
-    chosen = chosen.reshape(RING, capacity, width)
+    both, gate_spread, mixing = tie((both, gate_spread, mixing))
+    both_spread = swap_blocks(both)
+
     mine = [chosen[0]] + [send(chosen[n], deep_step(n)) for n in range(1, RING)]
-    gate_picks, both_spread = tie((gate_picks, both_spread))
+    summed = whole(
+        functools.partial(expert_kernel, width // 8),
+        (jax.ShapeDtypeStruct((capacity, width), bf16),) * RING,
+        WORK,
+        *mine,
+        home_gate,
+        home_up,
+        home_down,
+        far_gate,
+        *far,
+    )
+    gate_picks = gate_spread[copy_source]
+    gate_picks, both_spread, _ = tie((gate_picks, both_spread, summed[0]))
     replica_gate = swap_blocks(gate_picks)
-    both_picks = picked(copy_source, both_spread)
-    mine = whole(stack_kernel, jax.ShapeDtypeStruct((places, width), bf16), WORK, *mine)
-    other = swap_cores(mine)
-
-    def expert_part(slot_rows, dtype):
-        return whole(
-            functools.partial(expert_kernel, width // 8),
-            jax.ShapeDtypeStruct((places, width), dtype),
-            1 << 20,
-            slot_rows,
-            home_gate,
-            home_up,
-            home_down,
-        )
-
-    given = swap_cores(expert_part(other, bf16))
-    summed = whole(
-        add_kernel,
-        jax.ShapeDtypeStruct((places, width), bf16),
-        1 << 20,
-        expert_part(mine, f32),
-        given,
-    )
-
-    summed = summed.reshape(RING, capacity, width)
+
     back = [summed[0]] + [send(summed[n], deep_step(-n)) for n in range(1, RING)]
-    both_picks, replica_gate = tie((both_picks, replica_gate))
-    replica_both = swap_blocks(both_picks)
-    replica_gate = copied(replica_gate.reshape(1, depth, units))
-    mixing, replica_gate = tie((mixing, replica_gate))
     own, *parts = whole(
         functools.partial(gated_kernel, width // 8),
         (jax.ShapeDtypeStruct((line, width), f32),)
@@ -317,6 +313,8 @@
         *back,
     )
     parts = [send(parts[n - 1], wide_step(-n)) for n in range(1, RING)]
+    both_spread, own = tie((both_spread, own))
+    own, both_picks = tie((own, picked(copy_source, both_spread)))
     own, *parts = whole(
         sum_kernel,
         (jax.ShapeDtypeStruct((rows, width), f32),)
@@ -326,8 +324,11 @@
         *parts,
     )
 
-    parts, replica_both = tie((parts, replica_both))
-    parts = [send(parts[n - 1], row_step(n)) for n in range(1, 4)]
+    both_picks, replica_gate, own = tie((both_picks, replica_gate, own))
+    replica_both = swap_blocks(both_picks)
+    replica_gate = copied(replica_gate.reshape(1, depth, units))
+    own, replica_gate = tie((own, replica_gate))
+    parts = [send(parts[n - 1], row_step(n)) for n in range(1, RING)]
     share = depth // experts
     replica_up = replica_both[:, :share].reshape(1, depth, units)
     replica_down = replica_both[:, share:].reshape(1, depth, units)

time: 372 us -> 360 us (0.968)
  the two profiles are of different devices: /device:TPU:62 before, /device:TPU:2 now
where the time goes in v4:
time: 360 us; the launch traced here: 356 us
  waiting for transfers between devices  218 us (61%)
  starting transfers between devices  71.4 us (20%)
  Pallas kernels  33.9 us (9%)
  local copies, waits for them, and re-layouts  22.4 us (6%)
  other arithmetic  9.25 us (3%)
    ppermute x21, waiting for transfers between devices, send(): return lax.ppermute(value, BOTH, pairs)  180 us
    all_to_all x4, starting transfers between devices, swap_blocks(): lax.all_to_all(blocks, 'expert', split_axis=0, concat_axis=0, tiled=True)  44.2 us
    all_to_all x4, waiting for transfers between devices, swap_blocks(): lax.all_to_all(blocks, 'expert', split_axis=0, concat_axis=0, tiled=True)  38.2 us
    ppermute x21, starting transfers between devices, send(): return lax.ppermute(value, BOTH, pairs)  27.2 us
    pallas_call x6, Pallas kernels, whole(): pl.pallas_call(kernel, out_shape=out_shape, in_specs=[pl.BlockSpec(memory...  19.3 us
    pallas_call x1, Pallas kernels, picked(): pl.pallas_call(pick_kernel, out_shape=jax.ShapeDtypeStruct(spread.shape,...  11.5 us
    unnamed x24, local copies, waits for them, and re-layouts  10.4 us
  transfers between devices with their start and end apart: 25, of which 13 were waited for; matrix products, arithmetic and copies ran while one was open for 4% of the time, Pallas kernels for 10%

profile of v4, /device:TPU:2, one launch (start us, length us, event | category | flops | bytes accessed | tf_op | source)
XLA Modules:
  0.0 356.1 jit_solution(10353767672975252233)
XLA Ops:
  0.6 0.0 copy-start
  0.6 0.1 collective-permute-start.3
  0.7 0.7 convert_element_type.14
  1.4 0.7 reduce-precision_convert_fusion.1
  2.1 0.1 fusion.8
  2.2 0.9 pad_maximum_fusion.1.refs_0_
  3.1 1.6 collective-permute-start.2
  4.7 1.0 collective-permute-start.1
  5.7 1.6 collective-permute-start
  7.3 0.0 collective-permute-start.7
  7.3 2.8 collective-permute-done.2.refs_3_
  10.1 0.0 collective-permute-start.8
  10.1 2.1 collective-permute-done.1.refs_2_
  12.2 0.9 collective-permute-done.refs_1_
  13.2 3.1 collective-permute-start.6
  16.2 0.6 collective-permute-start.5
  16.9 1.0 collective-permute-start.4
  17.8 9.0 %all-to-all-start = ((bf16[32,224,256]{2,1,0:T(8,128)(2,1)}), bf16[32,224,256]{2,1,0:T(8,128)(2,1)}, u32[]{:S(2)}, u32[]{:S(2)}) async-start(bf16[32,224,256]{2,1,0:T(8,128)(2,1)} %bitcast.12), calls=%async_computation | async-start | bytes 7340032 | tf_op jit(solution)/shard_map/all_to_all | solution.py:53
  27.0 0.6 gather_fusion
  27.6 0.8 collective-permute-done.6.refs_3_
  28.5 30.3 %collective-permute-done.4.refs_1_ = bf16[32,7296]{1,0:T(8,128)(2,1)S(1)} collective-permute-done((bf16[32,7296]{1,0:T(8,128)(2,1)S(1)}, bf16[32,7296]{1,0:T(8,128)(2,1)S(1)}, u32[]{:S(2)}, u32[]{:S(2)}) %collective-permute-start.4) | collective-permute-done | bytes 466976 | tf_op jit(solution)/shard_map/ppermute | solution.py:49
  58.8 2.7 shard_map.112
  61.5 0.8 copy-done.8
  62.4 0.7 copy-done.10
  63.0 2.5 collective-permute-start.9
  65.6 4.4 %collective-permute-start.10 = (bf16[48,7168]{1,0:T(8,128)(2,1)S(1)}, bf16[48,7168]{1,0:T(8,128)(2,1)S(1)}, u32[]{:S(2)}, u32[]{:S(2)}) collective-permute-start(bf16[48,7168]{1,0:T(8,128)(2,1)S(1)} %get-tuple-element.61), channel_id=1, source_target_pairs={{0,16},{1,17},{2,18},{3,19},{4,20},{5,21},{6,22},{7,23},{8,24},{9,... | collective-permute-start | bytes 2064392 | tf_op jit(solution)/shard_map/ppermute | solution.py:49
  70.0 0.7 collective-permute-start.11
  70.6 6.8 %pad_maximum_fusion = bf16[32,448,256]{2,1,0:T(8,128)(2,1)} fusion(bf16[32,224,256]{2,1,0:T(8,128)(2,1)} %bitcast.9, bf16[32,224,256]{2,1,0:T(8,128)(2,1)} %bitcast.8), kind=kLoop, calls=%fused_computation.2 | loop fusion | flops 14680064 | bytes 14680064 | tf_op jit(solution)/shard_map/concatenate | solution.py:267
  77.5 8.1 %all-to-all-start.1 = ((bf16[32,448,256]{2,1,0:T(8,128)(2,1)}), bf16[32,448,256]{2,1,0:T(8,128)(2,1)}, u32[]{:S(2)}, u32[]{:S(2)}) async-start(bf16[32,448,256]{2,1,0:T(8,128)(2,1)} %pad_maximum_fusion), calls=%async_computation.1 | async-start | bytes 14680064 | tf_op jit(solution)/shard_map/all_to_all | solution.py:53
  85.6 34.0 %collective-permute-done.10.refs_2_ = bf16[48,7168]{1,0:T(8,128)(2,1)S(1)} collective-permute-done((bf16[48,7168]{1,0:T(8,128)(2,1)S(1)}, bf16[48,7168]{1,0:T(8,128)(2,1)S(1)}, u32[]{:S(2)}, u32[]{:S(2)}) %collective-permute-start.10) | collective-permute-done | bytes 688160 | tf_op jit(solution)/shard_map/ppermute | solution.py:49
  119.6 0.8 copy-done.4
  120.5 1.1 copy-done.5
  121.6 1.1 copy-done.9
  122.7 12.8 %shard_map.113 = (bf16[48,7168]{1,0:T(8,128)(2,1)S(1)}, bf16[48,7168]{1,0:T(8,128)(2,1)S(1)}, bf16[48,7168]{1,0:T(8,128)(2,1)S(1)}, bf16[48,7168]{1,0:T(8,128)(2,1)S(1)}) custom-call(bf16[48,7168]{1,0:T(8,128)(2,1)S(1)} %copy-done.9, bf16[48,7168]{1,0:T(8,128)(2,1)S(1)} %collective-permute-done.9.refs_1_, ...), custom_call_target="tpu_custom_call" | custom-call | flops 68719476736 | bytes 1048576 | tf_op jit(solution)/shard_map/pallas_call | solution.py:106
  135.5 0.0 copy-start.6
  135.5 0.8 copy-done.6
  136.3 0.1 collective-permute-start.13
  136.5 1.9 collective-permute-start.14
  138.4 4.7 %gather_fusion.1 = bf16[32,224,256]{2,1,0:T(8,128)(2,1)} fusion(bf16[32,224,256]{2,1,0:T(8,128)(2,1)} %all-to-all-done, s32[1024]{0:T(1024)S(1)} %pad_clamp_fusion), kind=kCustom, calls=%fused_computation.1 | custom fusion | bytes 7340160 | tf_op jit(solution)/shard_map/gather | solution.py:302
  143.0 34.9 %all-to-all-done.1.from_ref = bf16[32,448,256]{2,1,0:T(8,128)(2,1)} async-done(((bf16[32,448,256]{2,1,0:T(8,128)(2,1)}), bf16[32,448,256]{2,1,0:T(8,128)(2,1)}, u32[]{:S(2)}, u32[]{:S(2)}) %all-to-all-start.1) | async-done | bytes 7340064 | tf_op jit(solution)/shard_map/all_to_all | solution.py:53
  177.9 11.2 %all-to-all-start.2 = ((bf16[32,224,256]{2,1,0:T(8,128)(2,1)}), bf16[32,224,256]{2,1,0:T(8,128)(2,1)}, u32[]{:S(2)}, u32[]{:S(2)}) async-start(bf16[32,224,256]{2,1,0:T(8,128)(2,1)} %gather_fusion.1), calls=%async_computation.2 | async-start | bytes 7340032 | tf_op jit(solution)/shard_map/all_to_all | solution.py:53
  189.2 0.0 copy-start.7
  189.2 1.1 copy-done.7
  190.3 0.9 copy-done.11
  191.2 2.9 shard_map.114
  194.1 3.0 collective-permute-start.15
  197.1 0.8 collective-permute-start.16
  197.9 0.8 collective-permute-start.17
  198.8 11.5 %shard_map.115 = bf16[32,448,256]{2,1,0:T(8,128)(2,1)S(1)} custom-call(s32[32]{0:T(128)S(1)} %copy-done.3, bf16[32,448,256]{2,1,0:T(8,128)(2,1)} %all-to-all-done.1.from_ref), custom_call_target="tpu_custom_call" | custom-call | bytes 1048576 | tf_op jit(solution)/shard_map/pallas_call | solution.py:193
  210.3 3.0 copy-done.2
  213.3 22.1 %collective-permute-done.15.refs_0_ = bf16[32,7168]{1,0:T(8,128)(2,1)S(1)} collective-permute-done((bf16[32,7168]{1,0:T(8,128)(2,1)S(1)}, bf16[32,7168]{1,0:T(8,128)(2,1)S(1)}, u32[]{:S(2)}, u32[]{:S(2)}) %collective-permute-start.15) | collective-permute-done | bytes 458784 | tf_op jit(solution)/shard_map/ppermute | solution.py:49
  235.5 3.4 collective-permute-done.16.refs_1_
  238.8 3.5 collective-permute-done.17.refs_2_
  242.3 0.2 shard_map.116
  242.5 15.9 %all-to-all-start.3 = ((bf16[32,448,256]{2,1,0:T(8,128)(2,1)}), bf16[32,448,256]{2,1,0:T(8,128)(2,1)}, u32[]{:S(2)}, u32[]{:S(2)}) async-start(bf16[32,448,256]{2,1,0:T(8,128)(2,1)} %copy-done.2), calls=%async_computation.3 | async-start | bytes 14680064 | tf_op jit(solution)/shard_map/all_to_all | solution.py:53
  258.4 0.1 collective-permute-start.18
  258.5 3.3 collective-permute-start.19
  261.8 0.5 collective-permute-start.20
  262.3 3.1 shard_map.117
  265.4 78.2 %collective-permute-done.18.refs_0_ = bf16[8,7168]{1,0:T(8,128)(2,1)S(1)} collective-permute-done((bf16[8,7168]{1,0:T(8,128)(2,1)S(1)}, bf16[8,7168]{1,0:T(8,128)(2,1)S(1)}, u32[]{:S(2)}, u32[]{:S(2)}) %collective-permute-start.18) | collective-permute-done | bytes 114720 | tf_op jit(solution)/shard_map/ppermute | solution.py:49
  343.6 1.8 collective-permute-done.19.refs_1_
  345.4 0.7 shard_map.118
  346.1 3.2 all-to-all-done.3
  349.4 6.7 %fusion.14 = (bf16[32,224,256]{2,1,0:T(8,128)(2,1)}, bf16[32,224,256]{2,1,0:T(8,128)(2,1)}) fusion(bf16[32,448,256]{2,1,0:T(8,128)(2,1)} %all-to-all-done.3), kind=kLoop, calls=%fused_computation.33 | loop fusion | bytes 14680064 | tf_op jit(solution)/shard_map/slice | solution.py:334
  (30 shorter events, 0.1 us)
Async XLA Ops:
  0.6 26.3 %copy-start = (s32[32]{0:T(128)S(1)}, s32[32]{0:T(128)}, u32[]{:S(2)}) copy-start(s32[32]{0:T(128)} %param.11) | copy-start | bytes 388
  0.6 12.5 %collective-permute-start.3 = (bf16[1,7168,256]{2,1,0:T(8,128)(2,1)}, bf16[1,7168,256]{2,1,0:T(8,128)(2,1)}, u32[]{:S(2)}, u32[]{:S(2)}) collective-permute-start(bf16[1,7168,256]{2,1,0:T(8,128)(2,1)} %refs_4_.1), channel_id=1, source_target_pairs={{0,32},{1,33},{2,34},{3,35},{4,36},{5,37},{6,38},{7,39},{8,40},{9,... | collective-permute-start | bytes 11010056 | tf_op jit(solution)/shard_map/ppermute | solution.py:49
  3.1 7.0 %collective-permute-start.2 = (bf16[8,7296]{1,0:T(8,128)(2,1)S(1)}, bf16[8,7296]{1,0:T(8,128)(2,1)S(1)}, u32[]{:S(2)}, u32[]{:S(2)}) collective-permute-start(bf16[8,7296]{1,0:T(8,128)(2,1)S(1)} %pad_maximum_fusion.1.refs_0_), channel_id=1, source_target_pairs={{0,65},{1,64},{2,67},{3,66},{4,69},{5,68},{6,71},{7,70},{8,73},{9,... | collective-permute-start | bytes 350216 | tf_op jit(solution)/shard_map/ppermute | solution.py:49
  4.7 7.5 %collective-permute-start.1 = (bf16[8,7296]{1,0:T(8,128)(2,1)S(1)}, bf16[8,7296]{1,0:T(8,128)(2,1)S(1)}, u32[]{:S(2)}, u32[]{:S(2)}) collective-permute-start(bf16[8,7296]{1,0:T(8,128)(2,1)S(1)} %pad_maximum_fusion.1.refs_0_), channel_id=1, source_target_pairs={{0,1},{1,0},{2,3},{3,2},{4,5},{5,4},{6,7},{7,6},{8,9},{9,8},{10,11... | collective-permute-start | bytes 350216 | tf_op jit(solution)/shard_map/ppermute | solution.py:49
  5.7 7.4 %collective-permute-start = (bf16[8,7296]{1,0:T(8,128)(2,1)S(1)}, bf16[8,7296]{1,0:T(8,128)(2,1)S(1)}, u32[]{:S(2)}, u32[]{:S(2)}) collective-permute-start(bf16[8,7296]{1,0:T(8,128)(2,1)S(1)} %pad_maximum_fusion.1.refs_0_), channel_id=1, source_target_pairs={{0,64},{1,65},{2,66},{3,67},{4,68},{5,69},{6,70},{7,71},{8,72},{9,... | collective-permute-start | bytes 350216 | tf_op jit(solution)/shard_map/ppermute | solution.py:49
  7.3 20.3 %collective-permute-start.7 = (bf16[1,7168,256]{2,1,0:T(8,128)(2,1)}, bf16[1,7168,256]{2,1,0:T(8,128)(2,1)}, u32[]{:S(2)}, u32[]{:S(2)}) collective-permute-start(bf16[1,7168,256]{2,1,0:T(8,128)(2,1)} %refs_5_.1), channel_id=1, source_target_pairs={{0,32},{1,33},{2,34},{3,35},{4,36},{5,37},{6,38},{7,39},{8,40},{9,... | collective-permute-start | bytes 11010056 | tf_op jit(solution)/shard_map/ppermute | solution.py:49
  10.1 17.5 %collective-permute-start.8 = (bf16[1,7168,256]{2,1,0:T(8,128)(2,1)}, bf16[1,7168,256]{2,1,0:T(8,128)(2,1)}, u32[]{:S(2)}, u32[]{:S(2)}) collective-permute-start(bf16[1,7168,256]{2,1,0:T(8,128)(2,1)} %refs_6_.1), channel_id=1, source_target_pairs={{0,32},{1,33},{2,34},{3,35},{4,36},{5,37},{6,38},{7,39},{8,40},{9,... | collective-permute-start | bytes 11010056 | tf_op jit(solution)/shard_map/ppermute | solution.py:49
  13.2 15.3 %collective-permute-start.6 = (bf16[32,7296]{1,0:T(8,128)(2,1)S(1)}, bf16[32,7296]{1,0:T(8,128)(2,1)S(1)}, u32[]{:S(2)}, u32[]{:S(2)}) collective-permute-start(bf16[32,7296]{1,0:T(8,128)(2,1)S(1)} %shard_map.111.refs_0_), channel_id=1, source_target_pairs={{0,6},{1,7},{2,0},{3,1},{4,2},{5,3},{6,4},{7,5},{8,14},{9,15},{10,... | collective-permute-start | bytes 1400840 | tf_op jit(solution)/shard_map/ppermute | solution.py:49
  16.2 12.2 %collective-permute-start.5 = (bf16[32,7296]{1,0:T(8,128)(2,1)S(1)}, bf16[32,7296]{1,0:T(8,128)(2,1)S(1)}, u32[]{:S(2)}, u32[]{:S(2)}) collective-permute-start(bf16[32,7296]{1,0:T(8,128)(2,1)S(1)} %shard_map.111.refs_0_), channel_id=1, source_target_pairs={{0,4},{1,5},{2,6},{3,7},{4,0},{5,1},{6,2},{7,3},{8,12},{9,13},{10,... | collective-permute-start | bytes 1400840 | tf_op jit(solution)/shard_map/ppermute | solution.py:49
  16.9 41.9 %collective-permute-start.4 = (bf16[32,7296]{1,0:T(8,128)(2,1)S(1)}, bf16[32,7296]{1,0:T(8,128)(2,1)S(1)}, u32[]{:S(2)}, u32[]{:S(2)}) collective-permute-start(bf16[32,7296]{1,0:T(8,128)(2,1)S(1)} %shard_map.111.refs_0_), channel_id=1, source_target_pairs={{0,2},{1,3},{2,4},{3,5},{4,6},{5,7},{6,0},{7,1},{8,10},{9,11},{10,... | collective-permute-start | bytes 1400840 | tf_op jit(solution)/shard_map/ppermute | solution.py:49
  17.8 59.6 %all-to-all-start = ((bf16[32,224,256]{2,1,0:T(8,128)(2,1)}), bf16[32,224,256]{2,1,0:T(8,128)(2,1)}, u32[]{:S(2)}, u32[]{:S(2)}) async-start(bf16[32,224,256]{2,1,0:T(8,128)(2,1)} %bitcast.12), calls=%async_computation | async-start | bytes 7340032 | tf_op jit(solution)/shard_map/all_to_all | solution.py:53
  61.5 0.8 copy-start.8
  62.4 0.7 copy-start.10
  63.0 22.6 %collective-permute-start.9 = (bf16[48,7168]{1,0:T(8,128)(2,1)}, bf16[48,7168]{1,0:T(8,128)(2,1)S(1)}, u32[]{:S(2)}, u32[]{:S(2)}) collective-permute-start(bf16[48,7168]{1,0:T(8,128)(2,1)} %get-tuple-element.60), channel_id=1, source_target_pairs={{0,8},{1,9},{2,10},{3,11},{4,12},{5,13},{6,14},{7,15},{8,16},{9,17... | collective-permute-start | bytes 2064392 | tf_op jit(solution)/shard_map/ppermute | solution.py:49
  65.6 54.0 %collective-permute-start.10 = (bf16[48,7168]{1,0:T(8,128)(2,1)S(1)}, bf16[48,7168]{1,0:T(8,128)(2,1)S(1)}, u32[]{:S(2)}, u32[]{:S(2)}) collective-permute-start(bf16[48,7168]{1,0:T(8,128)(2,1)S(1)} %get-tuple-element.61), channel_id=1, source_target_pairs={{0,16},{1,17},{2,18},{3,19},{4,20},{5,21},{6,22},{7,23},{8,24},{9,... | collective-permute-start | bytes 2064392 | tf_op jit(solution)/shard_map/ppermute | solution.py:49
  70.0 49.6 %collective-permute-start.11 = (bf16[48,7168]{1,0:T(8,128)(2,1)S(1)}, bf16[48,7168]{1,0:T(8,128)(2,1)S(1)}, u32[]{:S(2)}, u32[]{:S(2)}) collective-permute-start(bf16[48,7168]{1,0:T(8,128)(2,1)S(1)} %get-tuple-element.62), channel_id=1, source_target_pairs={{0,24},{1,25},{2,26},{3,27},{4,28},{5,29},{6,30},{7,31},{8,0},{9,1... | collective-permute-start | bytes 2064392 | tf_op jit(solution)/shard_map/ppermute | solution.py:49
  77.5 100.4 %all-to-all-start.1 = ((bf16[32,448,256]{2,1,0:T(8,128)(2,1)}), bf16[32,448,256]{2,1,0:T(8,128)(2,1)}, u32[]{:S(2)}, u32[]{:S(2)}) async-start(bf16[32,448,256]{2,1,0:T(8,128)(2,1)} %pad_maximum_fusion), calls=%async_computation.1 | async-start | bytes 14680064 | tf_op jit(solution)/shard_map/all_to_all | solution.py:53
  119.6 0.8 copy-start.4
  120.5 1.1 copy-start.5
  121.6 1.1 copy-start.9
  122.7 15.7 %copy-start.3 = (s32[32]{0:T(128)S(1)}, s32[32]{0:T(128)}, u32[]{:S(2)}) copy-start(s32[32]{0:T(128)} %source_ref.1) | copy-start | bytes 388
  135.5 0.8 copy-start.6
  136.3 52.8 %collective-permute-start.12 = (bf16[48,7168]{1,0:T(8,128)(2,1)S(1)}, bf16[48,7168]{1,0:T(8,128)(2,1)S(1)}, u32[]{:S(2)}, u32[]{:S(2)}) collective-permute-start(bf16[48,7168]{1,0:T(8,128)(2,1)S(1)} %get-tuple-element.69), channel_id=1, source_target_pairs={{0,24},{1,25},{2,26},{3,27},{4,28},{5,29},{6,30},{7,31},{8,0},{9,1... | collective-permute-start | bytes 2064392 | tf_op jit(solution)/shard_map/ppermute | solution.py:49
  136.3 52.8 %collective-permute-start.13 = (bf16[48,7168]{1,0:T(8,128)(2,1)S(1)}, bf16[48,7168]{1,0:T(8,128)(2,1)S(1)}, u32[]{:S(2)}, u32[]{:S(2)}) collective-permute-start(bf16[48,7168]{1,0:T(8,128)(2,1)S(1)} %get-tuple-element.70), channel_id=1, source_target_pairs={{0,16},{1,17},{2,18},{3,19},{4,20},{5,21},{6,22},{7,23},{8,24},{9,... | collective-permute-start | bytes 2064392 | tf_op jit(solution)/shard_map/ppermute | solution.py:49
  136.5 52.7 %collective-permute-start.14 = (bf16[48,7168]{1,0:T(8,128)(2,1)S(1)}, bf16[48,7168]{1,0:T(8,128)(2,1)}, u32[]{:S(2)}, u32[]{:S(2)}) collective-permute-start(bf16[48,7168]{1,0:T(8,128)(2,1)S(1)} %get-tuple-element.71), channel_id=1, source_target_pairs={{0,8},{1,9},{2,10},{3,11},{4,12},{5,13},{6,14},{7,15},{8,16},{9,17... | collective-permute-start | bytes 2064392 | tf_op jit(solution)/shard_map/ppermute | solution.py:49
  177.9 64.6 %all-to-all-start.2 = ((bf16[32,224,256]{2,1,0:T(8,128)(2,1)}), bf16[32,224,256]{2,1,0:T(8,128)(2,1)}, u32[]{:S(2)}, u32[]{:S(2)}) async-start(bf16[32,224,256]{2,1,0:T(8,128)(2,1)} %gather_fusion.1), calls=%async_computation.2 | async-start | bytes 7340032 | tf_op jit(solution)/shard_map/all_to_all | solution.py:53
  189.2 1.1 copy-start.7
  190.3 0.9 copy-start.11
  194.1 41.4 %collective-permute-start.15 = (bf16[32,7168]{1,0:T(8,128)(2,1)S(1)}, bf16[32,7168]{1,0:T(8,128)(2,1)S(1)}, u32[]{:S(2)}, u32[]{:S(2)}) collective-permute-start(bf16[32,7168]{1,0:T(8,128)(2,1)S(1)} %get-tuple-element.78), channel_id=1, source_target_pairs={{0,6},{1,7},{2,0},{3,1},{4,2},{5,3},{6,4},{7,5},{8,14},{9,15},{10,... | collective-permute-start | bytes 1376264 | tf_op jit(solution)/shard_map/ppermute | solution.py:49
  197.1 41.7 %collective-permute-start.16 = (bf16[32,7168]{1,0:T(8,128)(2,1)S(1)}, bf16[32,7168]{1,0:T(8,128)(2,1)S(1)}, u32[]{:S(2)}, u32[]{:S(2)}) collective-permute-start(bf16[32,7168]{1,0:T(8,128)(2,1)S(1)} %get-tuple-element.79), channel_id=1, source_target_pairs={{0,4},{1,5},{2,6},{3,7},{4,0},{5,1},{6,2},{7,3},{8,12},{9,13},{10,... | collective-permute-start | bytes 1376264 | tf_op jit(solution)/shard_map/ppermute | solution.py:49
  197.9 44.4 %collective-permute-start.17 = (bf16[32,7168]{1,0:T(8,128)(2,1)S(1)}, bf16[32,7168]{1,0:T(8,128)(2,1)S(1)}, u32[]{:S(2)}, u32[]{:S(2)}) collective-permute-start(bf16[32,7168]{1,0:T(8,128)(2,1)S(1)} %get-tuple-element.80), channel_id=1, source_target_pairs={{0,2},{1,3},{2,4},{3,5},{4,6},{5,7},{6,0},{7,1},{8,10},{9,11},{10,... | collective-permute-start | bytes 1376264 | tf_op jit(solution)/shard_map/ppermute | solution.py:49
  210.3 3.0 copy-start.2
  242.5 106.9 %all-to-all-start.3 = ((bf16[32,448,256]{2,1,0:T(8,128)(2,1)}), bf16[32,448,256]{2,1,0:T(8,128)(2,1)}, u32[]{:S(2)}, u32[]{:S(2)}) async-start(bf16[32,448,256]{2,1,0:T(8,128)(2,1)} %copy-done.2), calls=%async_computation.3 | async-start | bytes 14680064 | tf_op jit(solution)/shard_map/all_to_all | solution.py:53
  258.4 85.2 %collective-permute-start.18 = (bf16[8,7168]{1,0:T(8,128)(2,1)S(1)}, bf16[8,7168]{1,0:T(8,128)(2,1)S(1)}, u32[]{:S(2)}, u32[]{:S(2)}) collective-permute-start(bf16[8,7168]{1,0:T(8,128)(2,1)S(1)} %get-tuple-element.85), channel_id=1, source_target_pairs={{0,64},{1,65},{2,66},{3,67},{4,68},{5,69},{6,70},{7,71},{8,72},{9,... | collective-permute-start | bytes 344072 | tf_op jit(solution)/shard_map/ppermute | solution.py:49
  258.5 86.9 %collective-permute-start.19 = (bf16[8,7168]{1,0:T(8,128)(2,1)S(1)}, bf16[8,7168]{1,0:T(8,128)(2,1)S(1)}, u32[]{:S(2)}, u32[]{:S(2)}) collective-permute-start(bf16[8,7168]{1,0:T(8,128)(2,1)S(1)} %get-tuple-element.86), channel_id=1, source_target_pairs={{0,1},{1,0},{2,3},{3,2},{4,5},{5,4},{6,7},{7,6},{8,9},{9,8},{10,11... | collective-permute-start | bytes 344072 | tf_op jit(solution)/shard_map/ppermute | solution.py:49
  261.8 83.6 %collective-permute-start.20 = (bf16[8,7168]{1,0:T(8,128)(2,1)S(1)}, bf16[8,7168]{1,0:T(8,128)(2,1)S(1)}, u32[]{:S(2)}, u32[]{:S(2)}) collective-permute-start(bf16[8,7168]{1,0:T(8,128)(2,1)S(1)} %get-tuple-element.87), channel_id=1, source_target_pairs={{0,65},{1,64},{2,67},{3,66},{4,69},{5,68},{6,71},{7,70},{8,73},{9,... | collective-permute-start | bytes 344072 | tf_op jit(solution)/shard_map/ppermute | solution.py:49
  349.4 6.7 %copy-start.1 = (s32[32]{0:T(128)S(1)}, s32[32]{0:T(128)}, u32[]{:S(2)}) copy-start(s32[32]{0:T(128)} %param.11) | copy-start | bytes 388

commit v5 on v4

--- a/solution.py
+++ b/solution.py
@@ -242,6 +242,49 @@
     )(value)
 
 
+def part_kernel(from_ref, one_ref, two_ref, held, came, went):
+    count, height = held.shape[0], held.shape[1] // 2
+    inward = [pltpu.make_async_copy(from_ref.at[n], held.at[n], came.at[n]) for n in range(count)]
+    outward = [
+        [
+            pltpu.make_async_copy(
+                held.at[n, pl.ds(k * height, height)],
+                to_ref.at[0, pl.ds(n * height, height)],
+                went.at[k, n],
+            )
+            for k, to_ref in enumerate((one_ref, two_ref))
+        ]
+        for n in range(count)
+    ]
+    for copy in inward:
+        copy.start()
+    for first, copies in zip(inward, outward):
+        first.wait()
+        for copy in copies:
+            copy.start()
+    for copies in outward:
+        for copy in copies:
+            copy.wait()
+
+
+def parted(both):
+    count, height, units = both.shape
+    out = jax.ShapeDtypeStruct((1, count * height // 2, units), both.dtype)
+    return pl.pallas_call(
+        part_kernel,
+        out_shape=(out, out),
+        in_specs=[pl.BlockSpec(memory_space=pl.ANY)],
+        out_specs=(pl.BlockSpec(memory_space=pl.ANY),) * 2,
+        scratch_shapes=[
+            pltpu.VMEM(both.shape, both.dtype),
+            pltpu.SemaphoreType.DMA((count,)),
+            pltpu.SemaphoreType.DMA((2, count)),
+        ],
+        compiler_params=pltpu.CompilerParams(vmem_limit_bytes=16 << 20),
+        cost_estimate=pl.CostEstimate(flops=0, bytes_accessed=1 << 10, transcendentals=0),
+    )(both)
+
+
 def on_device(tokens, gates, top_ids, home_expert, copy_source, home_gate, home_up, home_down):
     experts = lax.axis_size("expert")
     rows, width = tokens.shape
@@ -329,9 +372,7 @@
     replica_gate = copied(replica_gate.reshape(1, depth, units))
     own, replica_gate = tie((own, replica_gate))
     parts = [send(parts[n - 1], row_step(n)) for n in range(1, RING)]
-    share = depth // experts
-    replica_up = replica_both[:, :share].reshape(1, depth, units)
-    replica_down = replica_both[:, share:].reshape(1, depth, units)
+    replica_up, replica_down = parted(replica_both)
     mixed = whole(sum_kernel, (jax.ShapeDtypeStruct((rows, width), bf16),), 1 << 20, own, *parts)[0]
     return (mixed, replica_gate, replica_up, replica_down)
 

time: 360 us -> 360 us (level)
  Pallas kernels: 33.9 us -> 40.7 us
  local copies, waits for them, and re-layouts: 22.4 us -> 15.7 us
    pallas_call x0 -> x1, Pallas kernels: none -> 6.76 us  [parted(): pl.pallas_call(part_kernel, out_shape=(out, out), in_specs=[pl.BlockSpec(...]
    slice x1 -> x0, local copies, waits for them, and re-layouts: 6.69 us -> none  [on_device(): replica_down = replica_both[:, share:].reshape(1, depth, units)]
where the time goes in v5:
time: 360 us; the launch traced here: 356 us
  waiting for transfers between devices  218 us (61%)
  starting transfers between devices  71.4 us (20%)
  Pallas kernels  40.7 us (11%)
  local copies, waits for them, and re-layouts  15.7 us (4%)
  other arithmetic  9.25 us (3%)
    ppermute x21, waiting for transfers between devices, send(): return lax.ppermute(value, BOTH, pairs)  180 us
    all_to_all x4, starting transfers between devices, swap_blocks(): lax.all_to_all(blocks, 'expert', split_axis=0, concat_axis=0, tiled=True)  44.2 us
    all_to_all x4, waiting for transfers between devices, swap_blocks(): lax.all_to_all(blocks, 'expert', split_axis=0, concat_axis=0, tiled=True)  38.2 us
    ppermute x21, starting transfers between devices, send(): return lax.ppermute(value, BOTH, pairs)  27.2 us
    pallas_call x6, Pallas kernels, whole(): pl.pallas_call(kernel, out_shape=out_shape, in_specs=[pl.BlockSpec(memory...  19.3 us
    pallas_call x1, Pallas kernels, picked(): pl.pallas_call(pick_kernel, out_shape=jax.ShapeDtypeStruct(spread.shape,...  11.5 us
    unnamed x24, local copies, waits for them, and re-layouts  10.4 us
  transfers between devices with their start and end apart: 25, of which 13 were waited for; matrix products, arithmetic and copies ran while one was open for 4% of the time, Pallas kernels for 10%

profile of v5, /device:TPU:2, one launch (start us, length us, event | category | flops | bytes accessed | tf_op | source)
XLA Modules:
  0.0 356.3 jit_solution(4915902071266722199)
XLA Ops:
  0.6 0.0 copy-start
  0.6 0.1 collective-permute-start.3
  0.7 0.7 convert_element_type.14
  1.4 0.7 reduce-precision_convert_fusion.1
  2.1 0.1 fusion.8
  2.2 0.9 pad_maximum_fusion.1.refs_0_
  3.1 1.6 collective-permute-start.2
  4.7 1.0 collective-permute-start.1
  5.7 1.6 collective-permute-start
  7.3 0.0 collective-permute-start.7
  7.3 2.8 collective-permute-done.2.refs_3_
  10.1 2.1 collective-permute-done.1.refs_2_
  12.2 0.9 collective-permute-done.refs_1_
  13.2 3.1 collective-permute-start.6
  16.2 0.6 collective-permute-start.5
  16.9 1.0 collective-permute-start.4
  17.8 9.0 %all-to-all-start = ((bf16[32,224,256]{2,1,0:T(8,128)(2,1)}), bf16[32,224,256]{2,1,0:T(8,128)(2,1)}, u32[]{:S(2)}, u32[]{:S(2)}) async-start(bf16[32,224,256]{2,1,0:T(8,128)(2,1)} %bitcast.8), calls=%async_computation | async-start | bytes 7340032 | tf_op jit(solution)/shard_map/all_to_all | solution.py:53
  27.0 0.6 gather_fusion
  27.6 0.0 collective-permute-done.7.refs_8_
  27.6 0.8 collective-permute-done.6.refs_3_
  28.5 30.3 %collective-permute-done.4.refs_1_ = bf16[32,7296]{1,0:T(8,128)(2,1)S(1)} collective-permute-done((bf16[32,7296]{1,0:T(8,128)(2,1)S(1)}, bf16[32,7296]{1,0:T(8,128)(2,1)S(1)}, u32[]{:S(2)}, u32[]{:S(2)}) %collective-permute-start.4) | collective-permute-done | bytes 466976 | tf_op jit(solution)/shard_map/ppermute | solution.py:49
  58.8 2.7 shard_map.112
  61.5 0.8 copy-done.8
  62.4 0.7 copy-done.10
  63.0 2.5 collective-permute-start.9
  65.6 4.4 %collective-permute-start.10 = (bf16[48,7168]{1,0:T(8,128)(2,1)S(1)}, bf16[48,7168]{1,0:T(8,128)(2,1)S(1)}, u32[]{:S(2)}, u32[]{:S(2)}) collective-permute-start(bf16[48,7168]{1,0:T(8,128)(2,1)S(1)} %get-tuple-element.63), channel_id=1, source_target_pairs={{0,16},{1,17},{2,18},{3,19},{4,20},{5,21},{6,22},{7,23},{8,24},{9,... | collective-permute-start | bytes 2064392 | tf_op jit(solution)/shard_map/ppermute | solution.py:49
  70.0 0.7 collective-permute-start.11
  70.6 6.8 %pad_maximum_fusion = bf16[32,448,256]{2,1,0:T(8,128)(2,1)} fusion(bf16[32,224,256]{2,1,0:T(8,128)(2,1)} %bitcast.7, bf16[32,224,256]{2,1,0:T(8,128)(2,1)} %bitcast.6), kind=kLoop, calls=%fused_computation.2 | loop fusion | flops 14680064 | bytes 14680064 | tf_op jit(solution)/shard_map/concatenate | solution.py:310
  77.5 8.1 %all-to-all-start.1 = ((bf16[32,448,256]{2,1,0:T(8,128)(2,1)}), bf16[32,448,256]{2,1,0:T(8,128)(2,1)}, u32[]{:S(2)}, u32[]{:S(2)}) async-start(bf16[32,448,256]{2,1,0:T(8,128)(2,1)} %pad_maximum_fusion), calls=%async_computation.1 | async-start | bytes 14680064 | tf_op jit(solution)/shard_map/all_to_all | solution.py:53
  85.6 34.0 %collective-permute-done.10.refs_2_ = bf16[48,7168]{1,0:T(8,128)(2,1)S(1)} collective-permute-done((bf16[48,7168]{1,0:T(8,128)(2,1)S(1)}, bf16[48,7168]{1,0:T(8,128)(2,1)S(1)}, u32[]{:S(2)}, u32[]{:S(2)}) %collective-permute-start.10) | collective-permute-done | bytes 688160 | tf_op jit(solution)/shard_map/ppermute | solution.py:49
  119.6 0.8 copy-done.4
  120.5 1.1 copy-done.5
  121.6 1.1 copy-done.9
  122.7 12.8 %shard_map.113 = (bf16[48,7168]{1,0:T(8,128)(2,1)S(1)}, bf16[48,7168]{1,0:T(8,128)(2,1)S(1)}, bf16[48,7168]{1,0:T(8,128)(2,1)S(1)}, bf16[48,7168]{1,0:T(8,128)(2,1)S(1)}) custom-call(bf16[48,7168]{1,0:T(8,128)(2,1)S(1)} %copy-done.9, bf16[48,7168]{1,0:T(8,128)(2,1)S(1)} %collective-permute-done.9.refs_1_, ...), custom_call_target="tpu_custom_call" | custom-call | flops 68719476736 | bytes 1048576 | tf_op jit(solution)/shard_map/pallas_call | solution.py:106
  135.5 0.0 copy-start.6
  135.5 0.8 copy-done.6
  136.3 0.1 collective-permute-start.13
  136.5 1.9 collective-permute-start.14
  138.4 4.7 %gather_fusion.1 = bf16[32,224,256]{2,1,0:T(8,128)(2,1)} fusion(bf16[32,224,256]{2,1,0:T(8,128)(2,1)} %all-to-all-done, s32[1024]{0:T(1024)S(1)} %pad_clamp_fusion), kind=kCustom, calls=%fused_computation.1 | custom fusion | bytes 7340160 | tf_op jit(solution)/shard_map/gather | solution.py:345
  143.0 34.9 %all-to-all-done.1.from_ref = bf16[32,448,256]{2,1,0:T(8,128)(2,1)} async-done(((bf16[32,448,256]{2,1,0:T(8,128)(2,1)}), bf16[32,448,256]{2,1,0:T(8,128)(2,1)}, u32[]{:S(2)}, u32[]{:S(2)}) %all-to-all-start.1) | async-done | bytes 7340064 | tf_op jit(solution)/shard_map/all_to_all | solution.py:53
  177.9 11.2 %all-to-all-start.2 = ((bf16[32,224,256]{2,1,0:T(8,128)(2,1)}), bf16[32,224,256]{2,1,0:T(8,128)(2,1)}, u32[]{:S(2)}, u32[]{:S(2)}) async-start(bf16[32,224,256]{2,1,0:T(8,128)(2,1)} %gather_fusion.1), calls=%async_computation.2 | async-start | bytes 7340032 | tf_op jit(solution)/shard_map/all_to_all | solution.py:53
  189.2 0.0 copy-start.7
  189.2 1.1 copy-done.7
  190.3 0.9 copy-done.11
  191.2 2.9 shard_map.114
  194.1 3.0 collective-permute-start.15
  197.1 0.8 collective-permute-start.16
  197.9 0.8 collective-permute-start.17
  198.8 11.5 %shard_map.115 = bf16[32,448,256]{2,1,0:T(8,128)(2,1)S(1)} custom-call(s32[32]{0:T(128)S(1)} %copy-done.3, bf16[32,448,256]{2,1,0:T(8,128)(2,1)} %all-to-all-done.1.from_ref), custom_call_target="tpu_custom_call" | custom-call | bytes 1048576 | tf_op jit(solution)/shard_map/pallas_call | solution.py:193
  210.3 3.0 copy-done.2
  213.3 22.1 %collective-permute-done.15.refs_0_ = bf16[32,7168]{1,0:T(8,128)(2,1)S(1)} collective-permute-done((bf16[32,7168]{1,0:T(8,128)(2,1)S(1)}, bf16[32,7168]{1,0:T(8,128)(2,1)S(1)}, u32[]{:S(2)}, u32[]{:S(2)}) %collective-permute-start.15) | collective-permute-done | bytes 458784 | tf_op jit(solution)/shard_map/ppermute | solution.py:49
  235.5 3.4 collective-permute-done.16.refs_1_
  238.8 3.5 collective-permute-done.17.refs_2_
  242.3 0.2 shard_map.116
  242.5 15.9 %all-to-all-start.3 = ((bf16[32,448,256]{2,1,0:T(8,128)(2,1)}), bf16[32,448,256]{2,1,0:T(8,128)(2,1)}, u32[]{:S(2)}, u32[]{:S(2)}) async-start(bf16[32,448,256]{2,1,0:T(8,128)(2,1)} %copy-done.2), calls=%async_computation.3 | async-start | bytes 14680064 | tf_op jit(solution)/shard_map/all_to_all | solution.py:53
  258.4 0.1 collective-permute-start.18
  258.5 3.3 collective-permute-start.19
  261.8 0.5 collective-permute-start.20
  262.3 3.1 shard_map.117
  265.4 78.2 %collective-permute-done.18.refs_0_ = bf16[8,7168]{1,0:T(8,128)(2,1)S(1)} collective-permute-done((bf16[8,7168]{1,0:T(8,128)(2,1)S(1)}, bf16[8,7168]{1,0:T(8,128)(2,1)S(1)}, u32[]{:S(2)}, u32[]{:S(2)}) %collective-permute-start.18) | collective-permute-done | bytes 114720 | tf_op jit(solution)/shard_map/ppermute | solution.py:49
  343.6 1.8 collective-permute-done.19.refs_1_
  345.4 0.7 shard_map.118
  346.1 3.2 all-to-all-done.3.from_ref
  349.4 6.8 %shard_map.119 = (bf16[1,7168,256]{2,1,0:T(8,128)(2,1)}, bf16[1,7168,256]{2,1,0:T(8,128)(2,1)}) custom-call(bf16[32,448,256]{2,1,0:T(8,128)(2,1)} %all-to-all-done.3.from_ref), custom_call_target="tpu_custom_call" | custom-call | bytes 1024 | tf_op jit(solution)/shard_map/pallas_call | solution.py:273
  (30 shorter events, 0.1 us)
Async XLA Ops:
  0.6 26.3 %copy-start = (s32[32]{0:T(128)S(1)}, s32[32]{0:T(128)}, u32[]{:S(2)}) copy-start(s32[32]{0:T(128)} %param.11) | copy-start | bytes 388
  0.6 12.5 %collective-permute-start.3 = (bf16[1,7168,256]{2,1,0:T(8,128)(2,1)}, bf16[1,7168,256]{2,1,0:T(8,128)(2,1)}, u32[]{:S(2)}, u32[]{:S(2)}) collective-permute-start(bf16[1,7168,256]{2,1,0:T(8,128)(2,1)} %refs_4_.1), channel_id=1, source_target_pairs={{0,32},{1,33},{2,34},{3,35},{4,36},{5,37},{6,38},{7,39},{8,40},{9,... | collective-permute-start | bytes 11010056 | tf_op jit(solution)/shard_map/ppermute | solution.py:49
  3.1 7.0 %collective-permute-start.2 = (bf16[8,7296]{1,0:T(8,128)(2,1)S(1)}, bf16[8,7296]{1,0:T(8,128)(2,1)S(1)}, u32[]{:S(2)}, u32[]{:S(2)}) collective-permute-start(bf16[8,7296]{1,0:T(8,128)(2,1)S(1)} %pad_maximum_fusion.1.refs_0_), channel_id=1, source_target_pairs={{0,65},{1,64},{2,67},{3,66},{4,69},{5,68},{6,71},{7,70},{8,73},{9,... | collective-permute-start | bytes 350216 | tf_op jit(solution)/shard_map/ppermute | solution.py:49
  4.7 7.5 %collective-permute-start.1 = (bf16[8,7296]{1,0:T(8,128)(2,1)S(1)}, bf16[8,7296]{1,0:T(8,128)(2,1)S(1)}, u32[]{:S(2)}, u32[]{:S(2)}) collective-permute-start(bf16[8,7296]{1,0:T(8,128)(2,1)S(1)} %pad_maximum_fusion.1.refs_0_), channel_id=1, source_target_pairs={{0,1},{1,0},{2,3},{3,2},{4,5},{5,4},{6,7},{7,6},{8,9},{9,8},{10,11... | collective-permute-start | bytes 350216 | tf_op jit(solution)/shard_map/ppermute | solution.py:49
  5.7 7.4 %collective-permute-start = (bf16[8,7296]{1,0:T(8,128)(2,1)S(1)}, bf16[8,7296]{1,0:T(8,128)(2,1)S(1)}, u32[]{:S(2)}, u32[]{:S(2)}) collective-permute-start(bf16[8,7296]{1,0:T(8,128)(2,1)S(1)} %pad_maximum_fusion.1.refs_0_), channel_id=1, source_target_pairs={{0,64},{1,65},{2,66},{3,67},{4,68},{5,69},{6,70},{7,71},{8,72},{9,... | collective-permute-start | bytes 350216 | tf_op jit(solution)/shard_map/ppermute | solution.py:49
  7.3 20.3 %collective-permute-start.7 = (bf16[1,7168,256]{2,1,0:T(8,128)(2,1)}, bf16[1,7168,256]{2,1,0:T(8,128)(2,1)}, u32[]{:S(2)}, u32[]{:S(2)}) collective-permute-start(bf16[1,7168,256]{2,1,0:T(8,128)(2,1)} %refs_5_.1), channel_id=1, source_target_pairs={{0,32},{1,33},{2,34},{3,35},{4,36},{5,37},{6,38},{7,39},{8,40},{9,... | collective-permute-start | bytes 11010056 | tf_op jit(solution)/shard_map/ppermute | solution.py:49
  10.1 17.5 %collective-permute-start.8 = (bf16[1,7168,256]{2,1,0:T(8,128)(2,1)}, bf16[1,7168,256]{2,1,0:T(8,128)(2,1)}, u32[]{:S(2)}, u32[]{:S(2)}) collective-permute-start(bf16[1,7168,256]{2,1,0:T(8,128)(2,1)} %refs_6_.1), channel_id=1, source_target_pairs={{0,32},{1,33},{2,34},{3,35},{4,36},{5,37},{6,38},{7,39},{8,40},{9,... | collective-permute-start | bytes 11010056 | tf_op jit(solution)/shard_map/ppermute | solution.py:49
  13.2 15.3 %collective-permute-start.6 = (bf16[32,7296]{1,0:T(8,128)(2,1)S(1)}, bf16[32,7296]{1,0:T(8,128)(2,1)S(1)}, u32[]{:S(2)}, u32[]{:S(2)}) collective-permute-start(bf16[32,7296]{1,0:T(8,128)(2,1)S(1)} %shard_map.111.refs_0_), channel_id=1, source_target_pairs={{0,6},{1,7},{2,0},{3,1},{4,2},{5,3},{6,4},{7,5},{8,14},{9,15},{10,... | collective-permute-start | bytes 1400840 | tf_op jit(solution)/shard_map/ppermute | solution.py:49
  16.2 12.2 %collective-permute-start.5 = (bf16[32,7296]{1,0:T(8,128)(2,1)S(1)}, bf16[32,7296]{1,0:T(8,128)(2,1)S(1)}, u32[]{:S(2)}, u32[]{:S(2)}) collective-permute-start(bf16[32,7296]{1,0:T(8,128)(2,1)S(1)} %shard_map.111.refs_0_), channel_id=1, source_target_pairs={{0,4},{1,5},{2,6},{3,7},{4,0},{5,1},{6,2},{7,3},{8,12},{9,13},{10,... | collective-permute-start | bytes 1400840 | tf_op jit(solution)/shard_map/ppermute | solution.py:49
  16.9 41.9 %collective-permute-start.4 = (bf16[32,7296]{1,0:T(8,128)(2,1)S(1)}, bf16[32,7296]{1,0:T(8,128)(2,1)S(1)}, u32[]{:S(2)}, u32[]{:S(2)}) collective-permute-start(bf16[32,7296]{1,0:T(8,128)(2,1)S(1)} %shard_map.111.refs_0_), channel_id=1, source_target_pairs={{0,2},{1,3},{2,4},{3,5},{4,6},{5,7},{6,0},{7,1},{8,10},{9,11},{10,... | collective-permute-start | bytes 1400840 | tf_op jit(solution)/shard_map/ppermute | solution.py:49
  17.8 59.6 %all-to-all-start = ((bf16[32,224,256]{2,1,0:T(8,128)(2,1)}), bf16[32,224,256]{2,1,0:T(8,128)(2,1)}, u32[]{:S(2)}, u32[]{:S(2)}) async-start(bf16[32,224,256]{2,1,0:T(8,128)(2,1)} %bitcast.8), calls=%async_computation | async-start | bytes 7340032 | tf_op jit(solution)/shard_map/all_to_all | solution.py:53
  61.5 0.8 copy-start.8
  62.4 0.7 copy-start.10
  63.0 22.6 %collective-permute-start.9 = (bf16[48,7168]{1,0:T(8,128)(2,1)}, bf16[48,7168]{1,0:T(8,128)(2,1)S(1)}, u32[]{:S(2)}, u32[]{:S(2)}) collective-permute-start(bf16[48,7168]{1,0:T(8,128)(2,1)} %get-tuple-element.62), channel_id=1, source_target_pairs={{0,8},{1,9},{2,10},{3,11},{4,12},{5,13},{6,14},{7,15},{8,16},{9,17... | collective-permute-start | bytes 2064392 | tf_op jit(solution)/shard_map/ppermute | solution.py:49
  65.6 54.0 %collective-permute-start.10 = (bf16[48,7168]{1,0:T(8,128)(2,1)S(1)}, bf16[48,7168]{1,0:T(8,128)(2,1)S(1)}, u32[]{:S(2)}, u32[]{:S(2)}) collective-permute-start(bf16[48,7168]{1,0:T(8,128)(2,1)S(1)} %get-tuple-element.63), channel_id=1, source_target_pairs={{0,16},{1,17},{2,18},{3,19},{4,20},{5,21},{6,22},{7,23},{8,24},{9,... | collective-permute-start | bytes 2064392 | tf_op jit(solution)/shard_map/ppermute | solution.py:49
  70.0 49.6 %collective-permute-start.11 = (bf16[48,7168]{1,0:T(8,128)(2,1)S(1)}, bf16[48,7168]{1,0:T(8,128)(2,1)S(1)}, u32[]{:S(2)}, u32[]{:S(2)}) collective-permute-start(bf16[48,7168]{1,0:T(8,128)(2,1)S(1)} %get-tuple-element.64), channel_id=1, source_target_pairs={{0,24},{1,25},{2,26},{3,27},{4,28},{5,29},{6,30},{7,31},{8,0},{9,1... | collective-permute-start | bytes 2064392 | tf_op jit(solution)/shard_map/ppermute | solution.py:49
  77.5 100.4 %all-to-all-start.1 = ((bf16[32,448,256]{2,1,0:T(8,128)(2,1)}), bf16[32,448,256]{2,1,0:T(8,128)(2,1)}, u32[]{:S(2)}, u32[]{:S(2)}) async-start(bf16[32,448,256]{2,1,0:T(8,128)(2,1)} %pad_maximum_fusion), calls=%async_computation.1 | async-start | bytes 14680064 | tf_op jit(solution)/shard_map/all_to_all | solution.py:53
  119.6 0.8 copy-start.4
  120.5 1.1 copy-start.5
  121.6 1.1 copy-start.9
  122.7 15.7 %copy-start.3 = (s32[32]{0:T(128)S(1)}, s32[32]{0:T(128)}, u32[]{:S(2)}) copy-start(s32[32]{0:T(128)} %source_ref.1) | copy-start | bytes 388
  135.5 0.8 copy-start.6
  136.3 52.8 %collective-permute-start.12 = (bf16[48,7168]{1,0:T(8,128)(2,1)S(1)}, bf16[48,7168]{1,0:T(8,128)(2,1)S(1)}, u32[]{:S(2)}, u32[]{:S(2)}) collective-permute-start(bf16[48,7168]{1,0:T(8,128)(2,1)S(1)} %get-tuple-element.71), channel_id=1, source_target_pairs={{0,24},{1,25},{2,26},{3,27},{4,28},{5,29},{6,30},{7,31},{8,0},{9,1... | collective-permute-start | bytes 2064392 | tf_op jit(solution)/shard_map/ppermute | solution.py:49
  136.3 52.8 %collective-permute-start.13 = (bf16[48,7168]{1,0:T(8,128)(2,1)S(1)}, bf16[48,7168]{1,0:T(8,128)(2,1)S(1)}, u32[]{:S(2)}, u32[]{:S(2)}) collective-permute-start(bf16[48,7168]{1,0:T(8,128)(2,1)S(1)} %get-tuple-element.72), channel_id=1, source_target_pairs={{0,16},{1,17},{2,18},{3,19},{4,20},{5,21},{6,22},{7,23},{8,24},{9,... | collective-permute-start | bytes 2064392 | tf_op jit(solution)/shard_map/ppermute | solution.py:49
  136.5 52.7 %collective-permute-start.14 = (bf16[48,7168]{1,0:T(8,128)(2,1)S(1)}, bf16[48,7168]{1,0:T(8,128)(2,1)}, u32[]{:S(2)}, u32[]{:S(2)}) collective-permute-start(bf16[48,7168]{1,0:T(8,128)(2,1)S(1)} %get-tuple-element.73), channel_id=1, source_target_pairs={{0,8},{1,9},{2,10},{3,11},{4,12},{5,13},{6,14},{7,15},{8,16},{9,17... | collective-permute-start | bytes 2064392 | tf_op jit(solution)/shard_map/ppermute | solution.py:49
  177.9 64.6 %all-to-all-start.2 = ((bf16[32,224,256]{2,1,0:T(8,128)(2,1)}), bf16[32,224,256]{2,1,0:T(8,128)(2,1)}, u32[]{:S(2)}, u32[]{:S(2)}) async-start(bf16[32,224,256]{2,1,0:T(8,128)(2,1)} %gather_fusion.1), calls=%async_computation.2 | async-start | bytes 7340032 | tf_op jit(solution)/shard_map/all_to_all | solution.py:53
  189.2 1.1 copy-start.7
  190.3 0.9 copy-start.11
  194.1 41.4 %collective-permute-start.15 = (bf16[32,7168]{1,0:T(8,128)(2,1)S(1)}, bf16[32,7168]{1,0:T(8,128)(2,1)S(1)}, u32[]{:S(2)}, u32[]{:S(2)}) collective-permute-start(bf16[32,7168]{1,0:T(8,128)(2,1)S(1)} %get-tuple-element.80), channel_id=1, source_target_pairs={{0,6},{1,7},{2,0},{3,1},{4,2},{5,3},{6,4},{7,5},{8,14},{9,15},{10,... | collective-permute-start | bytes 1376264 | tf_op jit(solution)/shard_map/ppermute | solution.py:49
  197.1 41.7 %collective-permute-start.16 = (bf16[32,7168]{1,0:T(8,128)(2,1)S(1)}, bf16[32,7168]{1,0:T(8,128)(2,1)S(1)}, u32[]{:S(2)}, u32[]{:S(2)}) collective-permute-start(bf16[32,7168]{1,0:T(8,128)(2,1)S(1)} %get-tuple-element.81), channel_id=1, source_target_pairs={{0,4},{1,5},{2,6},{3,7},{4,0},{5,1},{6,2},{7,3},{8,12},{9,13},{10,... | collective-permute-start | bytes 1376264 | tf_op jit(solution)/shard_map/ppermute | solution.py:49
  197.9 44.4 %collective-permute-start.17 = (bf16[32,7168]{1,0:T(8,128)(2,1)S(1)}, bf16[32,7168]{1,0:T(8,128)(2,1)S(1)}, u32[]{:S(2)}, u32[]{:S(2)}) collective-permute-start(bf16[32,7168]{1,0:T(8,128)(2,1)S(1)} %get-tuple-element.82), channel_id=1, source_target_pairs={{0,2},{1,3},{2,4},{3,5},{4,6},{5,7},{6,0},{7,1},{8,10},{9,11},{10,... | collective-permute-start | bytes 1376264 | tf_op jit(solution)/shard_map/ppermute | solution.py:49
  210.3 3.0 copy-start.2
  242.5 106.9 %all-to-all-start.3 = ((bf16[32,448,256]{2,1,0:T(8,128)(2,1)}), bf16[32,448,256]{2,1,0:T(8,128)(2,1)}, u32[]{:S(2)}, u32[]{:S(2)}) async-start(bf16[32,448,256]{2,1,0:T(8,128)(2,1)} %copy-done.2), calls=%async_computation.3 | async-start | bytes 14680064 | tf_op jit(solution)/shard_map/all_to_all | solution.py:53
  258.4 85.2 %collective-permute-start.18 = (bf16[8,7168]{1,0:T(8,128)(2,1)S(1)}, bf16[8,7168]{1,0:T(8,128)(2,1)S(1)}, u32[]{:S(2)}, u32[]{:S(2)}) collective-permute-start(bf16[8,7168]{1,0:T(8,128)(2,1)S(1)} %get-tuple-element.87), channel_id=1, source_target_pairs={{0,64},{1,65},{2,66},{3,67},{4,68},{5,69},{6,70},{7,71},{8,72},{9,... | collective-permute-start | bytes 344072 | tf_op jit(solution)/shard_map/ppermute | solution.py:49
  258.5 86.9 %collective-permute-start.19 = (bf16[8,7168]{1,0:T(8,128)(2,1)S(1)}, bf16[8,7168]{1,0:T(8,128)(2,1)S(1)}, u32[]{:S(2)}, u32[]{:S(2)}) collective-permute-start(bf16[8,7168]{1,0:T(8,128)(2,1)S(1)} %get-tuple-element.88), channel_id=1, source_target_pairs={{0,1},{1,0},{2,3},{3,2},{4,5},{5,4},{6,7},{7,6},{8,9},{9,8},{10,11... | collective-permute-start | bytes 344072 | tf_op jit(solution)/shard_map/ppermute | solution.py:49
  261.8 83.6 %collective-permute-start.20 = (bf16[8,7168]{1,0:T(8,128)(2,1)S(1)}, bf16[8,7168]{1,0:T(8,128)(2,1)S(1)}, u32[]{:S(2)}, u32[]{:S(2)}) collective-permute-start(bf16[8,7168]{1,0:T(8,128)(2,1)S(1)} %get-tuple-element.89), channel_id=1, source_target_pairs={{0,65},{1,64},{2,67},{3,66},{4,69},{5,68},{6,71},{7,70},{8,73},{9,... | collective-permute-start | bytes 344072 | tf_op jit(solution)/shard_map/ppermute | solution.py:49
  345.4 10.7 %copy-start.1 = (s32[32]{0:T(128)S(1)}, s32[32]{0:T(128)}, u32[]{:S(2)}) copy-start(s32[32]{0:T(128)} %param.11) | copy-start | bytes 388
